TPU v7x, 1024 devices: a whole 4x4x32 slice. The times are simulated.
1024 devices in a mesh: lon: 128 (over x, z), lat: 8 (over y, core).
Axes of the slice: x: 4, y: 4, z: 32, core: 2. Of those that a mesh axis runs over, the one named last changes fastest.
Arguments:
- velocity_u: float32 [48, 1024, 1024], P(None, 'lon', 'lat'), may hold values from -4 to 4
- velocity_v: float32 [48, 1024, 1024], P(None, 'lon', 'lat'), may hold values from -4 to 4
- buoyancy: float32 [48, 1024, 1024], P(None, 'lon', 'lat'), may hold values from -6 to 6
- wind_x: float32 [1024, 1024], P('lon', 'lat'), may hold values from -0.02 to 0.02
- wind_y: float32 [1024, 1024], P('lon', 'lat'), may hold values from -0.02 to 0.02
- free_surface: float32 [1024, 1024], P('lon', 'lat'), may hold values from -0.8 to 0.8
- land_sea: int32 [1024, 1024], P('lon', 'lat'), may hold values 0 or 1
- bottom_level: int32 [1024, 1024], P('lon', 'lat'), may hold values from 4 to 48
Outputs:
- new_u: float32 [48, 1024, 1024], P(None, 'lon', 'lat')
- new_v: float32 [48, 1024, 1024], P(None, 'lon', 'lat')
- new_surface: float32 [1024, 1024], P('lon', 'lat')
All inputs are finite; a program needn't handle non-finite values. No bound on the sum of `land_sea` on one device may be relied on, other than what follows from the above.
Results may differ from a plain program's by a relative error of at most 0.00002.
Values sent between devices are 32-bit elements; how exact they have to be, the bound alone decides.
No kernel may reach another device: no remote copies, remote signals or barrier semaphores. Data moves between devices by JAX's collectives and lax.ppermute only.
A program may use at most 32 MiB of HBM per device.

v0:
```python
import jax
import jax.numpy as jnp
from jax import lax
from jax.sharding import PartitionSpec as P

SUBSTEPS = 30


def with_halo(cells, sides, width, closed):
    for axis, dim in sides:
        count = lax.axis_size(axis)
        ends = count if closed else count - 1
        head = lax.slice_in_dim(cells, 0, width, axis=dim)
        tail = lax.slice_in_dim(cells, cells.shape[dim] - width, cells.shape[dim], axis=dim)
        cells = jnp.concatenate(
            [
                lax.ppermute(tail, axis, [(i, (i + 1) % count) for i in range(ends)]),
                cells,
                lax.ppermute(head, axis, [((i + 1) % count, i) for i in range(ends)]),
            ],
            axis=dim,
        )
    return cells


def ahead(a, axis):
    size = a.shape[axis]
    lead = lax.slice_in_dim(a, 1, size, axis=axis)
    blank = jnp.zeros_like(lax.slice_in_dim(a, 0, 1, axis=axis))
    return jnp.concatenate([lead, blank], axis)


def behind(a, axis):
    size = a.shape[axis]
    lead = lax.slice_in_dim(a, 0, size - 1, axis=axis)
    blank = jnp.zeros_like(lax.slice_in_dim(a, 0, 1, axis=axis))
    return jnp.concatenate([blank, lead], axis)


def surface_rims(fields, width):
    wider = with_halo(fields, (("lon", 1),), width, True)
    return with_halo(wider, (("lat", 2),), width, False)


def local(velocity_u, velocity_v, buoyancy, wind_x, wind_y, free_surface, land_sea, bottom_level):
    levels_count, cols, rows_here = velocity_u.shape
    levels = jnp.arange(levels_count, dtype=jnp.float32)
    thick = ((1.0 + 2.0 * levels / levels_count) / levels_count)[:, None, None]
    water = (land_sea * bottom_level).astype(jnp.float32)
    pressure = jnp.cumsum(thick * buoyancy, axis=0)
    packed = jnp.concatenate([velocity_u, velocity_v, pressure, water[None]], 0)
    wider = with_halo(packed, (("lon", 1),), 1, True)
    framed = with_halo(wider, (("lat", 2),), 1, False)

    def east(a):
        return a[..., 2:, 1:-1]

    def west(a):
        return a[..., :-2, 1:-1]

    def north(a):
        return a[..., 1:-1, 2:]

    def south(a):
        return a[..., 1:-1, :-2]

    ext_u = framed[:levels_count]
    ext_v = framed[levels_count : 2 * levels_count]
    ext_p = framed[2 * levels_count : 3 * levels_count]
    ext_wet = (levels[:, None, None] < framed[3 * levels_count][None]).astype(jnp.float32)
    wet = ext_wet[..., 1:-1, 1:-1]
    face_u = wet * east(ext_wet)
    face_v = wet * north(ext_wet)
    top = (levels == 0.0).astype(jnp.float32)[:, None, None]
    lap_u = east(ext_u) + west(ext_u) + north(ext_u) + south(ext_u) - 4.0 * velocity_u
    lap_v = east(ext_v) + west(ext_v) + north(ext_v) + south(ext_v) - 4.0 * velocity_v
    force_u = 0.05 * lap_u - (east(ext_p) - pressure) + top * (wind_x[None] / thick[0])
    force_v = 0.05 * lap_v - (north(ext_p) - pressure) + top * (wind_y[None] / thick[0])
    star_u = (velocity_u + 6.0 * force_u) * face_u
    star_v = (velocity_v + 6.0 * force_v) * face_v
    depth_u = jnp.sum(thick * face_u, axis=0)
    depth_v = jnp.sum(thick * face_v, axis=0)
    forcing_u = jnp.sum(thick * face_u * force_u, axis=0)
    forcing_v = jnp.sum(thick * face_v * force_v, axis=0)
    flow_u = jnp.sum(thick * face_u * velocity_u, axis=0)
    flow_v = jnp.sum(thick * face_v * velocity_v, axis=0)
    wet_two = land_sea.astype(jnp.float32)
    substeps = SUBSTEPS
    width = 1
    rounds = substeps // width
    fixed_fields = jnp.stack(
        [forcing_u, forcing_v, depth_u, depth_v, wet_two, face_u[0], face_v[0]], 0
    )
    fixed_ext = surface_rims(fixed_fields, width)
    ext_forcing_u, ext_forcing_v, ext_depth_u, ext_depth_v, ext_wet_two, ext_open_u, ext_open_v = (
        fixed_ext[0],
        fixed_ext[1],
        fixed_ext[2],
        fixed_ext[3],
        fixed_ext[4],
        fixed_ext[5],
        fixed_ext[6],
    )
    total_rows = rows_here * lax.axis_size("lat")
    global_rows = (lax.axis_index("lat") * rows_here).astype(jnp.float32) + jnp.arange(
        -width, rows_here + width, dtype=jnp.float32
    )
    coriolis_u = (0.4 * (2.0 * (global_rows + 0.5) / total_rows - 1.0))[None, :]
    coriolis_v = (0.4 * (2.0 * (global_rows + 1.0) / total_rows - 1.0))[None, :]
    tau = 6.0 / substeps

    def one_round(turn, carry):
        surface, trans_u, trans_v, total_u, total_v = carry
        moving = surface_rims(jnp.stack([surface, trans_u, trans_v], 0), width)
        surf_e, east_flow, north_flow = (moving[0], moving[1], moving[2])
        spread = east_flow - behind(east_flow, 0) + north_flow - behind(north_flow, 1)
        surf_new = surf_e - tau * ext_wet_two * spread
        vbar = 0.25 * (
            north_flow
            + ahead(north_flow, 0)
            + behind(north_flow, 1)
            + ahead(behind(north_flow, 1), 0)
        )
        ubar = 0.25 * (
            east_flow + behind(east_flow, 0) + ahead(east_flow, 1) + behind(ahead(east_flow, 1), 0)
        )
        next_u = ext_open_u * (
            east_flow
            + tau
            * (ext_forcing_u - ext_depth_u * (ahead(surf_new, 0) - surf_new) + coriolis_u * vbar)
        )
        next_v = ext_open_v * (
            north_flow
            + tau
            * (ext_forcing_v - ext_depth_v * (ahead(surf_new, 1) - surf_new) - coriolis_v * ubar)
        )
        total_u = total_u + next_u[width : width + cols, width : width + rows_here]
        total_v = total_v + next_v[width : width + cols, width : width + rows_here]
        inner_slice = (slice(width, width + cols), slice(width, width + rows_here))
        return (surf_new[inner_slice], next_u[inner_slice], next_v[inner_slice], total_u, total_v)

    start = (free_surface, flow_u, flow_v, jnp.zeros_like(flow_u), jnp.zeros_like(flow_v))
    surface, trans_u, trans_v, total_u, total_v = lax.fori_loop(0, rounds, one_round, start)
    mean_u = total_u / substeps
    mean_v = total_v / substeps
    new_u = (
        star_u
        + face_u * ((mean_u - jnp.sum(thick * star_u, axis=0)) / jnp.maximum(depth_u, 0.25))[None]
    )
    new_v = (
        star_v
        + face_v * ((mean_v - jnp.sum(thick * star_v, axis=0)) / jnp.maximum(depth_v, 0.25))[None]
    )
    return (new_u, new_v, surface)


def solution(mesh):
    return jax.shard_map(
        local,
        mesh=mesh,
        in_specs=(
            P(None, "lon", "lat"),
            P(None, "lon", "lat"),
            P(None, "lon", "lat"),
            P("lon", "lat"),
            P("lon", "lat"),
            P("lon", "lat"),
            P("lon", "lat"),
            P("lon", "lat"),
        ),
        out_specs=(P(None, "lon", "lat"), P(None, "lon", "lat"), P("lon", "lat")),
        check_vma=False,
    )
```

profile of v0, /device:TPU:1, one launch (start us, length us, event | category | flops | bytes accessed | tf_op | source)
XLA Modules:
  0.0 628.0 jit_solution(5197262102394108993)
XLA Ops:
  3.8 21.4 %collective-permute-start.4 = (f32[145,1,128]{2,1,0:T(1,128)S(1)}, f32[145,1,128]{2,1,0:T(1,128)S(1)}, u32[]{:S(2)}, u32[]{:S(2)}) collective-permute-start(f32[145,1,128]{2,1,0:T(1,128)S(1)} %get-tuple-element.272), channel_id=1, source_target_pairs={{8,0},{16,8},{24,16},{32,24},{40,32},{48,40},{56,48},{64,56},{72,6... | collective-permute-start | bytes 222728 | tf_op jit(solution)/shard_map/ppermute | solution.py:19
  27.9 5.7 collective-permute-done.5
  48.9 6.7 %collective-permute-start.9 = (f32[7,1,128]{2,1,0:T(1,128)S(1)}, f32[7,1,128]{2,1,0:T(1,128)S(1)}, u32[]{:S(2)}, u32[]{:S(2)}) collective-permute-start(f32[7,1,128]{2,1,0:T(1,128)S(1)} %get-tuple-element.283), channel_id=1, source_target_pairs={{8,0},{16,8},{24,16},{32,24},{40,32},{48,40},{56,48},{64,56},{72,6... | collective-permute-start | bytes 10760 | tf_op jit(solution)/shard_map/ppermute | solution.py:19
  56.4 4.8 collective-permute-start.10
  66.9 559.6 %while.21 = (s32[]{:T(128)}, f32[8,128]{1,0:T(8,128)S(1)}, f32[8,128]{1,0:T(8,128)S(1)}, f32[8,128]{1,0:T(8,128)S(1)}, f32[8,128]{1,0:T(8,128)S(1)}, /*index=5*/...) while((s32[]{:T(128)}, f32[8,128]{1,0:T(8,128)S(1)}, ...), condition=%wide.region_8.9_spmd.clone.clone.clone, body=%wide.region_7.8_spmd.clone.clone.clone.sunk | while | flops 77940 | bytes 357483 | solution.py:143
  66.9 7.4 %collective-permute-start = (f32[3,1,128]{2,1,0:T(1,128)S(1)}, f32[3,1,128]{2,1,0:T(1,128)S(1)}, u32[]{:S(2)}, u32[]{:S(2)}) collective-permute-start(f32[3,1,128]{2,1,0:T(1,128)S(1)} %get-tuple-element.388), channel_id=1, source_target_pairs={{8,0},{16,8},{24,16},{32,24},{40,32},{48,40},{56,48},{64,56},{72,6... | collective-permute-start | bytes 4616 | tf_op jit(solution)/shard_map/while/body/eval_jaxpr/ppermute | solution.py:19
  76.4 5.5 collective-permute-done.1
  94.7 4.1 collective-permute-done.1
  100.8 5.4 collective-permute-start.3
  113.2 4.1 collective-permute-done.1
  119.3 5.4 collective-permute-start.3
  131.8 4.1 collective-permute-done.1
  137.9 5.4 collective-permute-start.3
  150.3 4.1 collective-permute-done.1
  156.4 5.4 collective-permute-start.3
  168.8 4.1 collective-permute-done.1
  174.9 5.4 collective-permute-start.3
  187.3 4.1 collective-permute-done.1
  193.4 5.4 collective-permute-start.3
  205.9 4.1 collective-permute-done.1
  212.0 5.4 collective-permute-start.3
  224.4 4.1 collective-permute-done.1
  230.5 5.4 collective-permute-start.3
  242.9 4.1 collective-permute-done.1
  249.0 5.4 collective-permute-start.3
  261.5 4.1 collective-permute-done.1
  267.6 5.4 collective-permute-start.3
  280.0 4.1 collective-permute-done.1
  286.1 5.4 collective-permute-start.3
  298.5 4.1 collective-permute-done.1
  304.6 5.4 collective-permute-start.3
  317.0 4.1 collective-permute-done.1
  323.1 5.4 collective-permute-start.3
  335.6 4.1 collective-permute-done.1
  341.7 5.4 collective-permute-start.3
  354.1 4.1 collective-permute-done.1
  360.2 5.4 collective-permute-start.3
  372.6 4.1 collective-permute-done.1
  378.7 5.4 collective-permute-start.3
  391.2 4.1 collective-permute-done.1
  397.3 5.4 collective-permute-start.3
  409.7 4.1 collective-permute-done.1
  415.8 5.4 collective-permute-start.3
  428.2 4.1 collective-permute-done.1
  434.3 5.4 collective-permute-start.3
  446.7 4.1 collective-permute-done.1
  452.8 5.4 collective-permute-start.3
  465.3 4.1 collective-permute-done.1
  471.4 5.4 collective-permute-start.3
  483.8 4.1 collective-permute-done.1
  489.9 5.4 collective-permute-start.3
  502.3 4.1 collective-permute-done.1
  508.4 5.4 collective-permute-start.3
  520.9 4.1 collective-permute-done.1
  527.0 5.4 collective-permute-start.3
  539.4 4.1 collective-permute-done.1
  545.5 5.4 collective-permute-start.3
  557.9 4.1 collective-permute-done.1
  564.0 5.4 collective-permute-start.3
  582.5 5.4 collective-permute-start.3
  595.0 4.1 collective-permute-done.1
  601.1 5.4 collective-permute-start.3
  613.5 4.1 collective-permute-done.1
  619.6 5.4 collective-permute-start.3
  (816 shorter events, 302.1 us)
Async XLA Ops:
  3.8 24.1 %collective-permute-start.4 = (f32[145,1,128]{2,1,0:T(1,128)S(1)}, f32[145,1,128]{2,1,0:T(1,128)S(1)}, u32[]{:S(2)}, u32[]{:S(2)}) collective-permute-start(f32[145,1,128]{2,1,0:T(1,128)S(1)} %get-tuple-element.272), channel_id=1, source_target_pairs={{8,0},{16,8},{24,16},{32,24},{40,32},{48,40},{56,48},{64,56},{72,6... | collective-permute-start | bytes 222728 | tf_op jit(solution)/shard_map/ppermute | solution.py:19
  25.3 8.4 %collective-permute-start.5 = (f32[145,1,128]{2,1,0:T(1,128)S(1)}, f32[145,1,128]{2,1,0:T(1,128)S(1)}, u32[]{:S(2)}, u32[]{:S(2)}) collective-permute-start(f32[145,1,128]{2,1,0:T(1,128)S(1)} %get-tuple-element.271), channel_id=1, source_target_pairs={{0,8},{8,16},{16,24},{24,32},{32,40},{40,48},{48,56},{56,64},{64,7... | collective-permute-start | bytes 222728 | tf_op jit(solution)/shard_map/ppermute | solution.py:17
  34.8 8.1 %collective-permute-start.6 = (f32[145,10,1]{0,2,1:T(1,128)S(1)}, f32[145,10,1]{0,2,1:T(1,128)S(1)}, u32[]{:S(2)}, u32[]{:S(2)}) collective-permute-start(f32[145,10,1]{0,2,1:T(1,128)S(1)} %copy.11), channel_id=1, source_target_pairs={{1,0},{2,1},{3,2},{4,3},{5,4},{6,5},{7,6},{9,8},{10,9},{11,10},{12... | collective-permute-start | bytes 17408 | tf_op jit(solution)/shard_map/ppermute | solution.py:19
  47.0 8.6 %collective-permute-start.8 = (f32[7,1,128]{2,1,0:T(1,128)S(1)}, f32[7,1,128]{2,1,0:T(1,128)S(1)}, u32[]{:S(2)}, u32[]{:S(2)}) collective-permute-start(f32[7,1,128]{2,1,0:T(1,128)S(1)} %get-tuple-element.282), channel_id=1, source_target_pairs={{0,8},{8,16},{16,24},{24,32},{32,40},{40,48},{48,56},{56,64},{64,7... | collective-permute-start | bytes 10760 | tf_op jit(solution)/shard_map/ppermute | solution.py:17
  48.9 7.4 %collective-permute-start.9 = (f32[7,1,128]{2,1,0:T(1,128)S(1)}, f32[7,1,128]{2,1,0:T(1,128)S(1)}, u32[]{:S(2)}, u32[]{:S(2)}) collective-permute-start(f32[7,1,128]{2,1,0:T(1,128)S(1)} %get-tuple-element.283), channel_id=1, source_target_pairs={{8,0},{16,8},{24,16},{32,24},{40,32},{48,40},{56,48},{64,56},{72,6... | collective-permute-start | bytes 10760 | tf_op jit(solution)/shard_map/ppermute | solution.py:19
  66.9 9.5 %collective-permute-start = (f32[3,1,128]{2,1,0:T(1,128)S(1)}, f32[3,1,128]{2,1,0:T(1,128)S(1)}, u32[]{:S(2)}, u32[]{:S(2)}) collective-permute-start(f32[3,1,128]{2,1,0:T(1,128)S(1)} %get-tuple-element.388), channel_id=1, source_target_pairs={{8,0},{16,8},{24,16},{32,24},{40,32},{48,40},{56,48},{64,56},{72,6... | collective-permute-start | bytes 4616 | tf_op jit(solution)/shard_map/while/body/eval_jaxpr/ppermute | solution.py:19
  74.3 7.6 %collective-permute-start.1 = (f32[3,1,128]{2,1,0:T(1,128)S(1)}, f32[3,1,128]{2,1,0:T(1,128)S(1)}, u32[]{:S(2)}, u32[]{:S(2)}) collective-permute-start(f32[3,1,128]{2,1,0:T(1,128)S(1)} %get-tuple-element.389), channel_id=1, source_target_pairs={{0,8},{8,16},{16,24},{24,32},{32,40},{40,48},{48,56},{56,64},{64,7... | collective-permute-start | bytes 4616 | tf_op jit(solution)/shard_map/while/body/eval_jaxpr/ppermute | solution.py:17
  91.1 7.6 %collective-permute-start.1 = (f32[3,1,128]{2,1,0:T(1,128)S(1)}, f32[3,1,128]{2,1,0:T(1,128)S(1)}, u32[]{:S(2)}, u32[]{:S(2)}) collective-permute-start(f32[3,1,128]{2,1,0:T(1,128)S(1)} %get-tuple-element.389), channel_id=1, source_target_pairs={{0,8},{8,16},{16,24},{24,32},{32,40},{40,48},{48,56},{56,64},{64,7... | collective-permute-start | bytes 4616 | tf_op jit(solution)/shard_map/while/body/eval_jaxpr/ppermute | solution.py:17
  98.8 7.3 %collective-permute-start.2 = (f32[3,10,1]{2,1,0:T(8,128)S(1)}, f32[3,10,1]{2,1,0:T(8,128)S(1)}, u32[]{:S(2)}, u32[]{:S(2)}) collective-permute-start(f32[3,10,1]{2,1,0:T(8,128)S(1)} %get-tuple-element.390), channel_id=1, source_target_pairs={{1,0},{2,1},{3,2},{4,3},{5,4},{6,5},{7,6},{9,8},{10,9},{11,10},{12... | collective-permute-start | bytes 368 | tf_op jit(solution)/shard_map/while/body/eval_jaxpr/ppermute | solution.py:19
  109.7 7.6 %collective-permute-start.1 = (f32[3,1,128]{2,1,0:T(1,128)S(1)}, f32[3,1,128]{2,1,0:T(1,128)S(1)}, u32[]{:S(2)}, u32[]{:S(2)}) collective-permute-start(f32[3,1,128]{2,1,0:T(1,128)S(1)} %get-tuple-element.389), channel_id=1, source_target_pairs={{0,8},{8,16},{16,24},{24,32},{32,40},{40,48},{48,56},{56,64},{64,7... | collective-permute-start | bytes 4616 | tf_op jit(solution)/shard_map/while/body/eval_jaxpr/ppermute | solution.py:17
  117.4 7.3 %collective-permute-start.2 = (f32[3,10,1]{2,1,0:T(8,128)S(1)}, f32[3,10,1]{2,1,0:T(8,128)S(1)}, u32[]{:S(2)}, u32[]{:S(2)}) collective-permute-start(f32[3,10,1]{2,1,0:T(8,128)S(1)} %get-tuple-element.390), channel_id=1, source_target_pairs={{1,0},{2,1},{3,2},{4,3},{5,4},{6,5},{7,6},{9,8},{10,9},{11,10},{12... | collective-permute-start | bytes 368 | tf_op jit(solution)/shard_map/while/body/eval_jaxpr/ppermute | solution.py:19
  128.2 7.6 %collective-permute-start.1 = (f32[3,1,128]{2,1,0:T(1,128)S(1)}, f32[3,1,128]{2,1,0:T(1,128)S(1)}, u32[]{:S(2)}, u32[]{:S(2)}) collective-permute-start(f32[3,1,128]{2,1,0:T(1,128)S(1)} %get-tuple-element.389), channel_id=1, source_target_pairs={{0,8},{8,16},{16,24},{24,32},{32,40},{40,48},{48,56},{56,64},{64,7... | collective-permute-start | bytes 4616 | tf_op jit(solution)/shard_map/while/body/eval_jaxpr/ppermute | solution.py:17
  135.9 7.3 %collective-permute-start.2 = (f32[3,10,1]{2,1,0:T(8,128)S(1)}, f32[3,10,1]{2,1,0:T(8,128)S(1)}, u32[]{:S(2)}, u32[]{:S(2)}) collective-permute-start(f32[3,10,1]{2,1,0:T(8,128)S(1)} %get-tuple-element.390), channel_id=1, source_target_pairs={{1,0},{2,1},{3,2},{4,3},{5,4},{6,5},{7,6},{9,8},{10,9},{11,10},{12... | collective-permute-start | bytes 368 | tf_op jit(solution)/shard_map/while/body/eval_jaxpr/ppermute | solution.py:19
  146.7 7.6 %collective-permute-start.1 = (f32[3,1,128]{2,1,0:T(1,128)S(1)}, f32[3,1,128]{2,1,0:T(1,128)S(1)}, u32[]{:S(2)}, u32[]{:S(2)}) collective-permute-start(f32[3,1,128]{2,1,0:T(1,128)S(1)} %get-tuple-element.389), channel_id=1, source_target_pairs={{0,8},{8,16},{16,24},{24,32},{32,40},{40,48},{48,56},{56,64},{64,7... | collective-permute-start | bytes 4616 | tf_op jit(solution)/shard_map/while/body/eval_jaxpr/ppermute | solution.py:17
  154.5 7.3 %collective-permute-start.2 = (f32[3,10,1]{2,1,0:T(8,128)S(1)}, f32[3,10,1]{2,1,0:T(8,128)S(1)}, u32[]{:S(2)}, u32[]{:S(2)}) collective-permute-start(f32[3,10,1]{2,1,0:T(8,128)S(1)} %get-tuple-element.390), channel_id=1, source_target_pairs={{1,0},{2,1},{3,2},{4,3},{5,4},{6,5},{7,6},{9,8},{10,9},{11,10},{12... | collective-permute-start | bytes 368 | tf_op jit(solution)/shard_map/while/body/eval_jaxpr/ppermute | solution.py:19
  165.3 7.6 %collective-permute-start.1 = (f32[3,1,128]{2,1,0:T(1,128)S(1)}, f32[3,1,128]{2,1,0:T(1,128)S(1)}, u32[]{:S(2)}, u32[]{:S(2)}) collective-permute-start(f32[3,1,128]{2,1,0:T(1,128)S(1)} %get-tuple-element.389), channel_id=1, source_target_pairs={{0,8},{8,16},{16,24},{24,32},{32,40},{40,48},{48,56},{56,64},{64,7... | collective-permute-start | bytes 4616 | tf_op jit(solution)/shard_map/while/body/eval_jaxpr/ppermute | solution.py:17
  173.0 7.3 %collective-permute-start.2 = (f32[3,10,1]{2,1,0:T(8,128)S(1)}, f32[3,10,1]{2,1,0:T(8,128)S(1)}, u32[]{:S(2)}, u32[]{:S(2)}) collective-permute-start(f32[3,10,1]{2,1,0:T(8,128)S(1)} %get-tuple-element.390), channel_id=1, source_target_pairs={{1,0},{2,1},{3,2},{4,3},{5,4},{6,5},{7,6},{9,8},{10,9},{11,10},{12... | collective-permute-start | bytes 368 | tf_op jit(solution)/shard_map/while/body/eval_jaxpr/ppermute | solution.py:19
  183.8 7.6 %collective-permute-start.1 = (f32[3,1,128]{2,1,0:T(1,128)S(1)}, f32[3,1,128]{2,1,0:T(1,128)S(1)}, u32[]{:S(2)}, u32[]{:S(2)}) collective-permute-start(f32[3,1,128]{2,1,0:T(1,128)S(1)} %get-tuple-element.389), channel_id=1, source_target_pairs={{0,8},{8,16},{16,24},{24,32},{32,40},{40,48},{48,56},{56,64},{64,7... | collective-permute-start | bytes 4616 | tf_op jit(solution)/shard_map/while/body/eval_jaxpr/ppermute | solution.py:17
  191.5 7.3 %collective-permute-start.2 = (f32[3,10,1]{2,1,0:T(8,128)S(1)}, f32[3,10,1]{2,1,0:T(8,128)S(1)}, u32[]{:S(2)}, u32[]{:S(2)}) collective-permute-start(f32[3,10,1]{2,1,0:T(8,128)S(1)} %get-tuple-element.390), channel_id=1, source_target_pairs={{1,0},{2,1},{3,2},{4,3},{5,4},{6,5},{7,6},{9,8},{10,9},{11,10},{12... | collective-permute-start | bytes 368 | tf_op jit(solution)/shard_map/while/body/eval_jaxpr/ppermute | solution.py:19
  202.3 7.6 %collective-permute-start.1 = (f32[3,1,128]{2,1,0:T(1,128)S(1)}, f32[3,1,128]{2,1,0:T(1,128)S(1)}, u32[]{:S(2)}, u32[]{:S(2)}) collective-permute-start(f32[3,1,128]{2,1,0:T(1,128)S(1)} %get-tuple-element.389), channel_id=1, source_target_pairs={{0,8},{8,16},{16,24},{24,32},{32,40},{40,48},{48,56},{56,64},{64,7... | collective-permute-start | bytes 4616 | tf_op jit(solution)/shard_map/while/body/eval_jaxpr/ppermute | solution.py:17
  210.0 7.3 %collective-permute-start.2 = (f32[3,10,1]{2,1,0:T(8,128)S(1)}, f32[3,10,1]{2,1,0:T(8,128)S(1)}, u32[]{:S(2)}, u32[]{:S(2)}) collective-permute-start(f32[3,10,1]{2,1,0:T(8,128)S(1)} %get-tuple-element.390), channel_id=1, source_target_pairs={{1,0},{2,1},{3,2},{4,3},{5,4},{6,5},{7,6},{9,8},{10,9},{11,10},{12... | collective-permute-start | bytes 368 | tf_op jit(solution)/shard_map/while/body/eval_jaxpr/ppermute | solution.py:19
  220.8 7.6 %collective-permute-start.1 = (f32[3,1,128]{2,1,0:T(1,128)S(1)}, f32[3,1,128]{2,1,0:T(1,128)S(1)}, u32[]{:S(2)}, u32[]{:S(2)}) collective-permute-start(f32[3,1,128]{2,1,0:T(1,128)S(1)} %get-tuple-element.389), channel_id=1, source_target_pairs={{0,8},{8,16},{16,24},{24,32},{32,40},{40,48},{48,56},{56,64},{64,7... | collective-permute-start | bytes 4616 | tf_op jit(solution)/shard_map/while/body/eval_jaxpr/ppermute | solution.py:17
  228.6 7.3 %collective-permute-start.2 = (f32[3,10,1]{2,1,0:T(8,128)S(1)}, f32[3,10,1]{2,1,0:T(8,128)S(1)}, u32[]{:S(2)}, u32[]{:S(2)}) collective-permute-start(f32[3,10,1]{2,1,0:T(8,128)S(1)} %get-tuple-element.390), channel_id=1, source_target_pairs={{1,0},{2,1},{3,2},{4,3},{5,4},{6,5},{7,6},{9,8},{10,9},{11,10},{12... | collective-permute-start | bytes 368 | tf_op jit(solution)/shard_map/while/body/eval_jaxpr/ppermute | solution.py:19
  239.4 7.6 %collective-permute-start.1 = (f32[3,1,128]{2,1,0:T(1,128)S(1)}, f32[3,1,128]{2,1,0:T(1,128)S(1)}, u32[]{:S(2)}, u32[]{:S(2)}) collective-permute-start(f32[3,1,128]{2,1,0:T(1,128)S(1)} %get-tuple-element.389), channel_id=1, source_target_pairs={{0,8},{8,16},{16,24},{24,32},{32,40},{40,48},{48,56},{56,64},{64,7... | collective-permute-start | bytes 4616 | tf_op jit(solution)/shard_map/while/body/eval_jaxpr/ppermute | solution.py:17
  247.1 7.3 %collective-permute-start.2 = (f32[3,10,1]{2,1,0:T(8,128)S(1)}, f32[3,10,1]{2,1,0:T(8,128)S(1)}, u32[]{:S(2)}, u32[]{:S(2)}) collective-permute-start(f32[3,10,1]{2,1,0:T(8,128)S(1)} %get-tuple-element.390), channel_id=1, source_target_pairs={{1,0},{2,1},{3,2},{4,3},{5,4},{6,5},{7,6},{9,8},{10,9},{11,10},{12... | collective-permute-start | bytes 368 | tf_op jit(solution)/shard_map/while/body/eval_jaxpr/ppermute | solution.py:19
  257.9 7.6 %collective-permute-start.1 = (f32[3,1,128]{2,1,0:T(1,128)S(1)}, f32[3,1,128]{2,1,0:T(1,128)S(1)}, u32[]{:S(2)}, u32[]{:S(2)}) collective-permute-start(f32[3,1,128]{2,1,0:T(1,128)S(1)} %get-tuple-element.389), channel_id=1, source_target_pairs={{0,8},{8,16},{16,24},{24,32},{32,40},{40,48},{48,56},{56,64},{64,7... | collective-permute-start | bytes 4616 | tf_op jit(solution)/shard_map/while/body/eval_jaxpr/ppermute | solution.py:17
  265.6 7.3 %collective-permute-start.2 = (f32[3,10,1]{2,1,0:T(8,128)S(1)}, f32[3,10,1]{2,1,0:T(8,128)S(1)}, u32[]{:S(2)}, u32[]{:S(2)}) collective-permute-start(f32[3,10,1]{2,1,0:T(8,128)S(1)} %get-tuple-element.390), channel_id=1, source_target_pairs={{1,0},{2,1},{3,2},{4,3},{5,4},{6,5},{7,6},{9,8},{10,9},{11,10},{12... | collective-permute-start | bytes 368 | tf_op jit(solution)/shard_map/while/body/eval_jaxpr/ppermute | solution.py:19
  276.4 7.6 %collective-permute-start.1 = (f32[3,1,128]{2,1,0:T(1,128)S(1)}, f32[3,1,128]{2,1,0:T(1,128)S(1)}, u32[]{:S(2)}, u32[]{:S(2)}) collective-permute-start(f32[3,1,128]{2,1,0:T(1,128)S(1)} %get-tuple-element.389), channel_id=1, source_target_pairs={{0,8},{8,16},{16,24},{24,32},{32,40},{40,48},{48,56},{56,64},{64,7... | collective-permute-start | bytes 4616 | tf_op jit(solution)/shard_map/while/body/eval_jaxpr/ppermute | solution.py:17
  284.2 7.3 %collective-permute-start.2 = (f32[3,10,1]{2,1,0:T(8,128)S(1)}, f32[3,10,1]{2,1,0:T(8,128)S(1)}, u32[]{:S(2)}, u32[]{:S(2)}) collective-permute-start(f32[3,10,1]{2,1,0:T(8,128)S(1)} %get-tuple-element.390), channel_id=1, source_target_pairs={{1,0},{2,1},{3,2},{4,3},{5,4},{6,5},{7,6},{9,8},{10,9},{11,10},{12... | collective-permute-start | bytes 368 | tf_op jit(solution)/shard_map/while/body/eval_jaxpr/ppermute | solution.py:19
  295.0 7.6 %collective-permute-start.1 = (f32[3,1,128]{2,1,0:T(1,128)S(1)}, f32[3,1,128]{2,1,0:T(1,128)S(1)}, u32[]{:S(2)}, u32[]{:S(2)}) collective-permute-start(f32[3,1,128]{2,1,0:T(1,128)S(1)} %get-tuple-element.389), channel_id=1, source_target_pairs={{0,8},{8,16},{16,24},{24,32},{32,40},{40,48},{48,56},{56,64},{64,7... | collective-permute-start | bytes 4616 | tf_op jit(solution)/shard_map/while/body/eval_jaxpr/ppermute | solution.py:17
  302.7 7.3 %collective-permute-start.2 = (f32[3,10,1]{2,1,0:T(8,128)S(1)}, f32[3,10,1]{2,1,0:T(8,128)S(1)}, u32[]{:S(2)}, u32[]{:S(2)}) collective-permute-start(f32[3,10,1]{2,1,0:T(8,128)S(1)} %get-tuple-element.390), channel_id=1, source_target_pairs={{1,0},{2,1},{3,2},{4,3},{5,4},{6,5},{7,6},{9,8},{10,9},{11,10},{12... | collective-permute-start | bytes 368 | tf_op jit(solution)/shard_map/while/body/eval_jaxpr/ppermute | solution.py:19
  313.5 7.6 %collective-permute-start.1 = (f32[3,1,128]{2,1,0:T(1,128)S(1)}, f32[3,1,128]{2,1,0:T(1,128)S(1)}, u32[]{:S(2)}, u32[]{:S(2)}) collective-permute-start(f32[3,1,128]{2,1,0:T(1,128)S(1)} %get-tuple-element.389), channel_id=1, source_target_pairs={{0,8},{8,16},{16,24},{24,32},{32,40},{40,48},{48,56},{56,64},{64,7... | collective-permute-start | bytes 4616 | tf_op jit(solution)/shard_map/while/body/eval_jaxpr/ppermute | solution.py:17
  321.2 7.3 %collective-permute-start.2 = (f32[3,10,1]{2,1,0:T(8,128)S(1)}, f32[3,10,1]{2,1,0:T(8,128)S(1)}, u32[]{:S(2)}, u32[]{:S(2)}) collective-permute-start(f32[3,10,1]{2,1,0:T(8,128)S(1)} %get-tuple-element.390), channel_id=1, source_target_pairs={{1,0},{2,1},{3,2},{4,3},{5,4},{6,5},{7,6},{9,8},{10,9},{11,10},{12... | collective-permute-start | bytes 368 | tf_op jit(solution)/shard_map/while/body/eval_jaxpr/ppermute | solution.py:19
  332.0 7.6 %collective-permute-start.1 = (f32[3,1,128]{2,1,0:T(1,128)S(1)}, f32[3,1,128]{2,1,0:T(1,128)S(1)}, u32[]{:S(2)}, u32[]{:S(2)}) collective-permute-start(f32[3,1,128]{2,1,0:T(1,128)S(1)} %get-tuple-element.389), channel_id=1, source_target_pairs={{0,8},{8,16},{16,24},{24,32},{32,40},{40,48},{48,56},{56,64},{64,7... | collective-permute-start | bytes 4616 | tf_op jit(solution)/shard_map/while/body/eval_jaxpr/ppermute | solution.py:17
  339.7 7.3 %collective-permute-start.2 = (f32[3,10,1]{2,1,0:T(8,128)S(1)}, f32[3,10,1]{2,1,0:T(8,128)S(1)}, u32[]{:S(2)}, u32[]{:S(2)}) collective-permute-start(f32[3,10,1]{2,1,0:T(8,128)S(1)} %get-tuple-element.390), channel_id=1, source_target_pairs={{1,0},{2,1},{3,2},{4,3},{5,4},{6,5},{7,6},{9,8},{10,9},{11,10},{12... | collective-permute-start | bytes 368 | tf_op jit(solution)/shard_map/while/body/eval_jaxpr/ppermute | solution.py:19
  350.5 7.6 %collective-permute-start.1 = (f32[3,1,128]{2,1,0:T(1,128)S(1)}, f32[3,1,128]{2,1,0:T(1,128)S(1)}, u32[]{:S(2)}, u32[]{:S(2)}) collective-permute-start(f32[3,1,128]{2,1,0:T(1,128)S(1)} %get-tuple-element.389), channel_id=1, source_target_pairs={{0,8},{8,16},{16,24},{24,32},{32,40},{40,48},{48,56},{56,64},{64,7... | collective-permute-start | bytes 4616 | tf_op jit(solution)/shard_map/while/body/eval_jaxpr/ppermute | solution.py:17
  358.3 7.3 %collective-permute-start.2 = (f32[3,10,1]{2,1,0:T(8,128)S(1)}, f32[3,10,1]{2,1,0:T(8,128)S(1)}, u32[]{:S(2)}, u32[]{:S(2)}) collective-permute-start(f32[3,10,1]{2,1,0:T(8,128)S(1)} %get-tuple-element.390), channel_id=1, source_target_pairs={{1,0},{2,1},{3,2},{4,3},{5,4},{6,5},{7,6},{9,8},{10,9},{11,10},{12... | collective-permute-start | bytes 368 | tf_op jit(solution)/shard_map/while/body/eval_jaxpr/ppermute | solution.py:19
  369.1 7.6 %collective-permute-start.1 = (f32[3,1,128]{2,1,0:T(1,128)S(1)}, f32[3,1,128]{2,1,0:T(1,128)S(1)}, u32[]{:S(2)}, u32[]{:S(2)}) collective-permute-start(f32[3,1,128]{2,1,0:T(1,128)S(1)} %get-tuple-element.389), channel_id=1, source_target_pairs={{0,8},{8,16},{16,24},{24,32},{32,40},{40,48},{48,56},{56,64},{64,7... | collective-permute-start | bytes 4616 | tf_op jit(solution)/shard_map/while/body/eval_jaxpr/ppermute | solution.py:17
  376.8 7.3 %collective-permute-start.2 = (f32[3,10,1]{2,1,0:T(8,128)S(1)}, f32[3,10,1]{2,1,0:T(8,128)S(1)}, u32[]{:S(2)}, u32[]{:S(2)}) collective-permute-start(f32[3,10,1]{2,1,0:T(8,128)S(1)} %get-tuple-element.390), channel_id=1, source_target_pairs={{1,0},{2,1},{3,2},{4,3},{5,4},{6,5},{7,6},{9,8},{10,9},{11,10},{12... | collective-permute-start | bytes 368 | tf_op jit(solution)/shard_map/while/body/eval_jaxpr/ppermute | solution.py:19
  387.6 7.6 %collective-permute-start.1 = (f32[3,1,128]{2,1,0:T(1,128)S(1)}, f32[3,1,128]{2,1,0:T(1,128)S(1)}, u32[]{:S(2)}, u32[]{:S(2)}) collective-permute-start(f32[3,1,128]{2,1,0:T(1,128)S(1)} %get-tuple-element.389), channel_id=1, source_target_pairs={{0,8},{8,16},{16,24},{24,32},{32,40},{40,48},{48,56},{56,64},{64,7... | collective-permute-start | bytes 4616 | tf_op jit(solution)/shard_map/while/body/eval_jaxpr/ppermute | solution.py:17
  395.3 7.3 %collective-permute-start.2 = (f32[3,10,1]{2,1,0:T(8,128)S(1)}, f32[3,10,1]{2,1,0:T(8,128)S(1)}, u32[]{:S(2)}, u32[]{:S(2)}) collective-permute-start(f32[3,10,1]{2,1,0:T(8,128)S(1)} %get-tuple-element.390), channel_id=1, source_target_pairs={{1,0},{2,1},{3,2},{4,3},{5,4},{6,5},{7,6},{9,8},{10,9},{11,10},{12... | collective-permute-start | bytes 368 | tf_op jit(solution)/shard_map/while/body/eval_jaxpr/ppermute | solution.py:19
  406.1 7.6 %collective-permute-start.1 = (f32[3,1,128]{2,1,0:T(1,128)S(1)}, f32[3,1,128]{2,1,0:T(1,128)S(1)}, u32[]{:S(2)}, u32[]{:S(2)}) collective-permute-start(f32[3,1,128]{2,1,0:T(1,128)S(1)} %get-tuple-element.389), channel_id=1, source_target_pairs={{0,8},{8,16},{16,24},{24,32},{32,40},{40,48},{48,56},{56,64},{64,7... | collective-permute-start | bytes 4616 | tf_op jit(solution)/shard_map/while/body/eval_jaxpr/ppermute | solution.py:17
  413.9 7.3 %collective-permute-start.2 = (f32[3,10,1]{2,1,0:T(8,128)S(1)}, f32[3,10,1]{2,1,0:T(8,128)S(1)}, u32[]{:S(2)}, u32[]{:S(2)}) collective-permute-start(f32[3,10,1]{2,1,0:T(8,128)S(1)} %get-tuple-element.390), channel_id=1, source_target_pairs={{1,0},{2,1},{3,2},{4,3},{5,4},{6,5},{7,6},{9,8},{10,9},{11,10},{12... | collective-permute-start | bytes 368 | tf_op jit(solution)/shard_map/while/body/eval_jaxpr/ppermute | solution.py:19
  424.7 7.6 %collective-permute-start.1 = (f32[3,1,128]{2,1,0:T(1,128)S(1)}, f32[3,1,128]{2,1,0:T(1,128)S(1)}, u32[]{:S(2)}, u32[]{:S(2)}) collective-permute-start(f32[3,1,128]{2,1,0:T(1,128)S(1)} %get-tuple-element.389), channel_id=1, source_target_pairs={{0,8},{8,16},{16,24},{24,32},{32,40},{40,48},{48,56},{56,64},{64,7... | collective-permute-start | bytes 4616 | tf_op jit(solution)/shard_map/while/body/eval_jaxpr/ppermute | solution.py:17
  432.4 7.3 %collective-permute-start.2 = (f32[3,10,1]{2,1,0:T(8,128)S(1)}, f32[3,10,1]{2,1,0:T(8,128)S(1)}, u32[]{:S(2)}, u32[]{:S(2)}) collective-permute-start(f32[3,10,1]{2,1,0:T(8,128)S(1)} %get-tuple-element.390), channel_id=1, source_target_pairs={{1,0},{2,1},{3,2},{4,3},{5,4},{6,5},{7,6},{9,8},{10,9},{11,10},{12... | collective-permute-start | bytes 368 | tf_op jit(solution)/shard_map/while/body/eval_jaxpr/ppermute | solution.py:19
  443.2 7.6 %collective-permute-start.1 = (f32[3,1,128]{2,1,0:T(1,128)S(1)}, f32[3,1,128]{2,1,0:T(1,128)S(1)}, u32[]{:S(2)}, u32[]{:S(2)}) collective-permute-start(f32[3,1,128]{2,1,0:T(1,128)S(1)} %get-tuple-element.389), channel_id=1, source_target_pairs={{0,8},{8,16},{16,24},{24,32},{32,40},{40,48},{48,56},{56,64},{64,7... | collective-permute-start | bytes 4616 | tf_op jit(solution)/shard_map/while/body/eval_jaxpr/ppermute | solution.py:17
  450.9 7.3 %collective-permute-start.2 = (f32[3,10,1]{2,1,0:T(8,128)S(1)}, f32[3,10,1]{2,1,0:T(8,128)S(1)}, u32[]{:S(2)}, u32[]{:S(2)}) collective-permute-start(f32[3,10,1]{2,1,0:T(8,128)S(1)} %get-tuple-element.390), channel_id=1, source_target_pairs={{1,0},{2,1},{3,2},{4,3},{5,4},{6,5},{7,6},{9,8},{10,9},{11,10},{12... | collective-permute-start | bytes 368 | tf_op jit(solution)/shard_map/while/body/eval_jaxpr/ppermute | solution.py:19
  461.7 7.6 %collective-permute-start.1 = (f32[3,1,128]{2,1,0:T(1,128)S(1)}, f32[3,1,128]{2,1,0:T(1,128)S(1)}, u32[]{:S(2)}, u32[]{:S(2)}) collective-permute-start(f32[3,1,128]{2,1,0:T(1,128)S(1)} %get-tuple-element.389), channel_id=1, source_target_pairs={{0,8},{8,16},{16,24},{24,32},{32,40},{40,48},{48,56},{56,64},{64,7... | collective-permute-start | bytes 4616 | tf_op jit(solution)/shard_map/while/body/eval_jaxpr/ppermute | solution.py:17
  469.5 7.3 %collective-permute-start.2 = (f32[3,10,1]{2,1,0:T(8,128)S(1)}, f32[3,10,1]{2,1,0:T(8,128)S(1)}, u32[]{:S(2)}, u32[]{:S(2)}) collective-permute-start(f32[3,10,1]{2,1,0:T(8,128)S(1)} %get-tuple-element.390), channel_id=1, source_target_pairs={{1,0},{2,1},{3,2},{4,3},{5,4},{6,5},{7,6},{9,8},{10,9},{11,10},{12... | collective-permute-start | bytes 368 | tf_op jit(solution)/shard_map/while/body/eval_jaxpr/ppermute | solution.py:19
  480.2 7.6 %collective-permute-start.1 = (f32[3,1,128]{2,1,0:T(1,128)S(1)}, f32[3,1,128]{2,1,0:T(1,128)S(1)}, u32[]{:S(2)}, u32[]{:S(2)}) collective-permute-start(f32[3,1,128]{2,1,0:T(1,128)S(1)} %get-tuple-element.389), channel_id=1, source_target_pairs={{0,8},{8,16},{16,24},{24,32},{32,40},{40,48},{48,56},{56,64},{64,7... | collective-permute-start | bytes 4616 | tf_op jit(solution)/shard_map/while/body/eval_jaxpr/ppermute | solution.py:17
  488.0 7.3 %collective-permute-start.2 = (f32[3,10,1]{2,1,0:T(8,128)S(1)}, f32[3,10,1]{2,1,0:T(8,128)S(1)}, u32[]{:S(2)}, u32[]{:S(2)}) collective-permute-start(f32[3,10,1]{2,1,0:T(8,128)S(1)} %get-tuple-element.390), channel_id=1, source_target_pairs={{1,0},{2,1},{3,2},{4,3},{5,4},{6,5},{7,6},{9,8},{10,9},{11,10},{12... | collective-permute-start | bytes 368 | tf_op jit(solution)/shard_map/while/body/eval_jaxpr/ppermute | solution.py:19
  498.8 7.6 %collective-permute-start.1 = (f32[3,1,128]{2,1,0:T(1,128)S(1)}, f32[3,1,128]{2,1,0:T(1,128)S(1)}, u32[]{:S(2)}, u32[]{:S(2)}) collective-permute-start(f32[3,1,128]{2,1,0:T(1,128)S(1)} %get-tuple-element.389), channel_id=1, source_target_pairs={{0,8},{8,16},{16,24},{24,32},{32,40},{40,48},{48,56},{56,64},{64,7... | collective-permute-start | bytes 4616 | tf_op jit(solution)/shard_map/while/body/eval_jaxpr/ppermute | solution.py:17
  506.5 7.3 %collective-permute-start.2 = (f32[3,10,1]{2,1,0:T(8,128)S(1)}, f32[3,10,1]{2,1,0:T(8,128)S(1)}, u32[]{:S(2)}, u32[]{:S(2)}) collective-permute-start(f32[3,10,1]{2,1,0:T(8,128)S(1)} %get-tuple-element.390), channel_id=1, source_target_pairs={{1,0},{2,1},{3,2},{4,3},{5,4},{6,5},{7,6},{9,8},{10,9},{11,10},{12... | collective-permute-start | bytes 368 | tf_op jit(solution)/shard_map/while/body/eval_jaxpr/ppermute | solution.py:19
  517.3 7.6 %collective-permute-start.1 = (f32[3,1,128]{2,1,0:T(1,128)S(1)}, f32[3,1,128]{2,1,0:T(1,128)S(1)}, u32[]{:S(2)}, u32[]{:S(2)}) collective-permute-start(f32[3,1,128]{2,1,0:T(1,128)S(1)} %get-tuple-element.389), channel_id=1, source_target_pairs={{0,8},{8,16},{16,24},{24,32},{32,40},{40,48},{48,56},{56,64},{64,7... | collective-permute-start | bytes 4616 | tf_op jit(solution)/shard_map/while/body/eval_jaxpr/ppermute | solution.py:17
  525.0 7.3 %collective-permute-start.2 = (f32[3,10,1]{2,1,0:T(8,128)S(1)}, f32[3,10,1]{2,1,0:T(8,128)S(1)}, u32[]{:S(2)}, u32[]{:S(2)}) collective-permute-start(f32[3,10,1]{2,1,0:T(8,128)S(1)} %get-tuple-element.390), channel_id=1, source_target_pairs={{1,0},{2,1},{3,2},{4,3},{5,4},{6,5},{7,6},{9,8},{10,9},{11,10},{12... | collective-permute-start | bytes 368 | tf_op jit(solution)/shard_map/while/body/eval_jaxpr/ppermute | solution.py:19
  535.8 7.6 %collective-permute-start.1 = (f32[3,1,128]{2,1,0:T(1,128)S(1)}, f32[3,1,128]{2,1,0:T(1,128)S(1)}, u32[]{:S(2)}, u32[]{:S(2)}) collective-permute-start(f32[3,1,128]{2,1,0:T(1,128)S(1)} %get-tuple-element.389), channel_id=1, source_target_pairs={{0,8},{8,16},{16,24},{24,32},{32,40},{40,48},{48,56},{56,64},{64,7... | collective-permute-start | bytes 4616 | tf_op jit(solution)/shard_map/while/body/eval_jaxpr/ppermute | solution.py:17
  543.6 7.3 %collective-permute-start.2 = (f32[3,10,1]{2,1,0:T(8,128)S(1)}, f32[3,10,1]{2,1,0:T(8,128)S(1)}, u32[]{:S(2)}, u32[]{:S(2)}) collective-permute-start(f32[3,10,1]{2,1,0:T(8,128)S(1)} %get-tuple-element.390), channel_id=1, source_target_pairs={{1,0},{2,1},{3,2},{4,3},{5,4},{6,5},{7,6},{9,8},{10,9},{11,10},{12... | collective-permute-start | bytes 368 | tf_op jit(solution)/shard_map/while/body/eval_jaxpr/ppermute | solution.py:19
  554.4 7.6 %collective-permute-start.1 = (f32[3,1,128]{2,1,0:T(1,128)S(1)}, f32[3,1,128]{2,1,0:T(1,128)S(1)}, u32[]{:S(2)}, u32[]{:S(2)}) collective-permute-start(f32[3,1,128]{2,1,0:T(1,128)S(1)} %get-tuple-element.389), channel_id=1, source_target_pairs={{0,8},{8,16},{16,24},{24,32},{32,40},{40,48},{48,56},{56,64},{64,7... | collective-permute-start | bytes 4616 | tf_op jit(solution)/shard_map/while/body/eval_jaxpr/ppermute | solution.py:17
  562.1 7.3 %collective-permute-start.2 = (f32[3,10,1]{2,1,0:T(8,128)S(1)}, f32[3,10,1]{2,1,0:T(8,128)S(1)}, u32[]{:S(2)}, u32[]{:S(2)}) collective-permute-start(f32[3,10,1]{2,1,0:T(8,128)S(1)} %get-tuple-element.390), channel_id=1, source_target_pairs={{1,0},{2,1},{3,2},{4,3},{5,4},{6,5},{7,6},{9,8},{10,9},{11,10},{12... | collective-permute-start | bytes 368 | tf_op jit(solution)/shard_map/while/body/eval_jaxpr/ppermute | solution.py:19
  572.9 7.6 %collective-permute-start.1 = (f32[3,1,128]{2,1,0:T(1,128)S(1)}, f32[3,1,128]{2,1,0:T(1,128)S(1)}, u32[]{:S(2)}, u32[]{:S(2)}) collective-permute-start(f32[3,1,128]{2,1,0:T(1,128)S(1)} %get-tuple-element.389), channel_id=1, source_target_pairs={{0,8},{8,16},{16,24},{24,32},{32,40},{40,48},{48,56},{56,64},{64,7... | collective-permute-start | bytes 4616 | tf_op jit(solution)/shard_map/while/body/eval_jaxpr/ppermute | solution.py:17
  580.6 7.3 %collective-permute-start.2 = (f32[3,10,1]{2,1,0:T(8,128)S(1)}, f32[3,10,1]{2,1,0:T(8,128)S(1)}, u32[]{:S(2)}, u32[]{:S(2)}) collective-permute-start(f32[3,10,1]{2,1,0:T(8,128)S(1)} %get-tuple-element.390), channel_id=1, source_target_pairs={{1,0},{2,1},{3,2},{4,3},{5,4},{6,5},{7,6},{9,8},{10,9},{11,10},{12... | collective-permute-start | bytes 368 | tf_op jit(solution)/shard_map/while/body/eval_jaxpr/ppermute | solution.py:19
  591.4 7.6 %collective-permute-start.1 = (f32[3,1,128]{2,1,0:T(1,128)S(1)}, f32[3,1,128]{2,1,0:T(1,128)S(1)}, u32[]{:S(2)}, u32[]{:S(2)}) collective-permute-start(f32[3,1,128]{2,1,0:T(1,128)S(1)} %get-tuple-element.389), channel_id=1, source_target_pairs={{0,8},{8,16},{16,24},{24,32},{32,40},{40,48},{48,56},{56,64},{64,7... | collective-permute-start | bytes 4616 | tf_op jit(solution)/shard_map/while/body/eval_jaxpr/ppermute | solution.py:17
  599.2 7.3 %collective-permute-start.2 = (f32[3,10,1]{2,1,0:T(8,128)S(1)}, f32[3,10,1]{2,1,0:T(8,128)S(1)}, u32[]{:S(2)}, u32[]{:S(2)}) collective-permute-start(f32[3,10,1]{2,1,0:T(8,128)S(1)} %get-tuple-element.390), channel_id=1, source_target_pairs={{1,0},{2,1},{3,2},{4,3},{5,4},{6,5},{7,6},{9,8},{10,9},{11,10},{12... | collective-permute-start | bytes 368 | tf_op jit(solution)/shard_map/while/body/eval_jaxpr/ppermute | solution.py:19
  610.0 7.6 %collective-permute-start.1 = (f32[3,1,128]{2,1,0:T(1,128)S(1)}, f32[3,1,128]{2,1,0:T(1,128)S(1)}, u32[]{:S(2)}, u32[]{:S(2)}) collective-permute-start(f32[3,1,128]{2,1,0:T(1,128)S(1)} %get-tuple-element.389), channel_id=1, source_target_pairs={{0,8},{8,16},{16,24},{24,32},{32,40},{40,48},{48,56},{56,64},{64,7... | collective-permute-start | bytes 4616 | tf_op jit(solution)/shard_map/while/body/eval_jaxpr/ppermute | solution.py:17
  (74 other events, 1621.4 us)
where the time goes:
time: 634 us; the launch traced here: 628 us
  starting transfers between devices  425 us (67%)
  waiting for transfers between devices  162 us (26%)
  local copies, waits for them, and re-layouts  19.5 us (3%)
  other arithmetic  17.7 us (3%)
    ppermute x64, starting transfers between devices, with_halo(): lax.ppermute(tail, axis, [(i, (i + 1) % count) for i in range(ends)])  270 us
    ppermute x64, waiting for transfers between devices, with_halo(): lax.ppermute(tail, axis, [(i, (i + 1) % count) for i in range(ends)])  157 us
    ppermute x64, starting transfers between devices, with_halo(): lax.ppermute(head, axis, [((i + 1) % count, i) for i in range(ends)])  154 us
  transfers between devices with their start and end apart: 128, of which 63 were waited for; matrix products, arithmetic and copies ran while one was open for 1% of the time, Pallas kernels for 0%

commit v1 on v0

v1 whole, which is shorter than its diff:
```python
import jax
import jax.numpy as jnp
import numpy as np
from jax import lax
from jax.experimental import pallas as pl
from jax.experimental.pallas import tpu as pltpu
from jax.sharding import PartitionSpec as P

SUBSTEPS = 30
LANES = 128
COLS = 8
RIM = 32
REACH = 4
FIELDS = 9 * COLS
STEP = 6.0
VMEM_BYTES = 32 * 1024 * 1024


def thickness(levels):
    index = np.arange(levels, dtype=np.float32)
    return (np.float32(1.0) + np.float32(2.0) * index / np.float32(levels)) / np.float32(levels)


def lane_index():
    return lax.broadcasted_iota(jnp.int32, (COLS, LANES), 1)


def col_index():
    return lax.broadcasted_iota(jnp.int32, (COLS, LANES), 0)


def is_even(axis):
    return lax.rem(lax.axis_index(axis), 2) == 0


def level(k):
    return pl.ds(COLS * k, COLS)


def north(own, rim):
    last = lane_index() == LANES - 1
    a, b = pltpu.roll(own, LANES - 1, 1), pltpu.roll(rim, LANES - 1, 1)
    return jnp.where(last, b, a), jnp.where(last, a, b)


def south(own, rim):
    first = lane_index() == 0
    a, b = pltpu.roll(own, 1, 1), pltpu.roll(rim, 1, 1)
    return jnp.where(first, b, a), jnp.where(first, a, b)


def pair_rims(first, second):
    lane = lax.broadcasted_iota(jnp.int32, first.shape, 1)
    return jnp.where((lane >= RIM) & (lane < LANES - RIM), pltpu.roll(second, LANES // 2, 1), first)


def pack_rows(u_ref, v_ref, b_ref, plane_refs, a_ref, z_ref):
    even = is_even("lat")
    lane = lane_index()
    slot = lane // RIM

    def strips(parts, shifts):
        moved = [pltpu.roll(p, s, 1) if s else p for p, s in zip(parts, shifts)]
        return jnp.where(
            slot < 2, jnp.where(slot == 0, moved[0], moved[1]), jnp.where(slot == 2, moved[2], moved[3])
        )

    for k in range(u_ref.shape[0] // COLS):
        u, v, b = u_ref[level(k), :], v_ref[level(k), :], b_ref[level(k), :]
        parts = (u, v, b, plane_refs[k][...] if k < len(plane_refs) else b)
        upper = strips(parts, (32, 64, 96, 0))
        lower = strips(parts, (0, 32, 64, 96))
        a_ref[level(k), :] = jnp.where(even, upper, lower)
        z_ref[level(k), :] = jnp.where(even, lower, upper)


def pack_rows_kernel(u_ref, v_ref, b_ref, water_ref, eta_ref, wx_ref, wy_ref, a_ref, z_ref):
    pack_rows(u_ref, v_ref, b_ref, (water_ref, eta_ref, wx_ref, wy_ref), a_ref, z_ref)


def pack_cols_kernel(u_ref, v_ref, b_ref, water_ref, a_in, z_in, a_ref, z_ref, hu_ref, hv_ref, hb_ref, hp_ref):
    even = is_even("lat")
    lane = lane_index()
    upper = lane < LANES // 2
    levels = u_ref.shape[0] // COLS
    for k in range(levels):
        a, z = a_in[level(k), :], z_in[level(k), :]
        n, s = jnp.where(even, a, z), jnp.where(even, z, a)
        hu_ref[level(k), :] = jnp.where(upper, n, pltpu.roll(s, 96, 1))
        hv_ref[level(k), :] = jnp.where(upper, pltpu.roll(n, 96, 1), pltpu.roll(s, 64, 1))
        hb_ref[level(k), :] = jnp.where(upper, pltpu.roll(n, 64, 1), pltpu.roll(s, 32, 1))
        if k < 4:
            hp_ref[level(k), :] = jnp.where(upper, pltpu.roll(n, 32, 1), s)
    even_col = is_even("lon")

    def edge(ref, rows, col):
        return ref[pl.ds(col, rows, stride=COLS), :]

    def store(col, out_ref):
        out_ref[pl.ds(0, levels), :] = edge(u_ref, levels, col)
        out_ref[pl.ds(levels, levels), :] = edge(v_ref, levels, col)
        out_ref[pl.ds(2 * levels, levels), :] = edge(b_ref, levels, col)
        out_ref[pl.ds(3 * levels, levels), :] = pair_rims(edge(hu_ref, levels, col), edge(hv_ref, levels, col))
        out_ref[pl.ds(4 * levels, levels), :] = edge(hb_ref, levels, col)
        out_ref[pl.ds(5 * levels, 1), :] = water_ref[pl.ds(col, 1), :]
        out_ref[pl.ds(5 * levels + 1, 1), :] = hp_ref[pl.ds(col, 1), :]
        out_ref[pl.ds(5 * levels + 2, 6), :] = jnp.zeros((6, LANES), jnp.float32)

    @pl.when(even_col)
    def _():
        store(COLS - 1, a_ref)
        store(0, z_ref)

    @pl.when(jnp.logical_not(even_col))
    def _():
        store(0, a_ref)
        store(COLS - 1, z_ref)


def levels_kernel(
    u_ref, v_ref, b_ref, hu_ref, hv_ref, hb_ref, hp_ref, water_ref, eta_ref, wx_ref, wy_ref, a_in, z_in,
    x_ref, su_ref, sv_ref, east_ref, west_ref,
):
    levels = u_ref.shape[0] // COLS
    thick = thickness(levels)
    even = is_even("lon")
    a, z = a_in[...], z_in[...]
    east_ref[pl.ds(0, a.shape[0]), :] = jnp.where(even, a, z)
    west_ref[pl.ds(0, a.shape[0]), :] = jnp.where(even, z, a)
    for ref in (east_ref, west_ref):
        ref[pl.ds(a.shape[0], levels), :] = pltpu.roll(ref[pl.ds(3 * levels, levels), :], LANES // 2, 1)
    own_at = {"u": 0, "v": levels, "b": 2 * levels, "w": 5 * levels}
    rim_at = {"u": 3 * levels, "v": a.shape[0], "b": 4 * levels, "w": 5 * levels + 1}
    col = col_index()
    top_col, bottom_col = col == COLS - 1, col == 0

    def row(ref, at):
        return jnp.broadcast_to(ref[pl.ds(at, 1), :], (COLS, LANES))

    def east(pair, name, k):
        own, rim = pair
        return (
            jnp.where(top_col, row(east_ref, own_at[name] + k), pltpu.roll(own, COLS - 1, 0)),
            jnp.where(top_col, row(east_ref, rim_at[name] + k), pltpu.roll(rim, COLS - 1, 0)),
        )

    def west(pair, name, k):
        own, rim = pair
        return (
            jnp.where(bottom_col, row(west_ref, own_at[name] + k), pltpu.roll(own, 1, 0)),
            jnp.where(bottom_col, row(west_ref, rim_at[name] + k), pltpu.roll(rim, 1, 0)),
        )

    water = (water_ref[...], hp_ref[pl.ds(0, COLS), :])
    eta = (eta_ref[...], hp_ref[pl.ds(COLS, COLS), :])
    wx = (wx_ref[...], hp_ref[pl.ds(2 * COLS, COLS), :])
    wy = (wy_ref[...], hp_ref[pl.ds(3 * COLS, COLS), :])
    open_u = [jnp.minimum(w, e) for w, e in zip(water, east(water, "w", 0))]
    open_v = [jnp.minimum(w, n) for w, n in zip(water, north(*water))]
    zero = jnp.zeros((COLS, LANES), jnp.float32)
    slope_u, slope_v = [zero, zero], [zero, zero]
    forcing_u, forcing_v = [zero, zero], [zero, zero]
    flow_u, flow_v = [zero, zero], [zero, zero]
    for k in range(levels):
        dz = float(thick[k])
        u = (u_ref[level(k), :], hu_ref[level(k), :])
        v = (v_ref[level(k), :], hv_ref[level(k), :])
        b = (b_ref[level(k), :], hb_ref[level(k), :])
        around_u = list(zip(east(u, "u", k), west(u, "u", k), north(*u), south(*u)))
        around_v = list(zip(east(v, "v", k), west(v, "v", k), north(*v), south(*v)))
        b_east, b_north = east(b, "b", k), north(*b)
        for t in range(2):
            slope_u[t] = slope_u[t] + dz * (b_east[t] - b[t])
            slope_v[t] = slope_v[t] + dz * (b_north[t] - b[t])
            force_u = 0.05 * (sum(around_u[t][1:], around_u[t][0]) - 4.0 * u[t]) - slope_u[t]
            force_v = 0.05 * (sum(around_v[t][1:], around_v[t][0]) - 4.0 * v[t]) - slope_v[t]
            if k == 0:
                force_u = force_u + wx[t] / dz
                force_v = force_v + wy[t] / dz
            wet_u, wet_v = open_u[t] > float(k), open_v[t] > float(k)
            force_u, vel_u = jnp.where(wet_u, force_u, 0.0), jnp.where(wet_u, u[t], 0.0)
            force_v, vel_v = jnp.where(wet_v, force_v, 0.0), jnp.where(wet_v, v[t], 0.0)
            forcing_u[t] = forcing_u[t] + dz * force_u
            forcing_v[t] = forcing_v[t] + dz * force_v
            flow_u[t] = flow_u[t] + dz * vel_u
            flow_v[t] = flow_v[t] + dz * vel_v
            if t == 0:
                su_ref[level(k), :] = vel_u + STEP * force_u
                sv_ref[level(k), :] = vel_v + STEP * force_v
    fields = (forcing_u, forcing_v, flow_u, flow_v, water, eta)
    for i, f in enumerate(fields):
        x_ref[level(i), :] = f[0]
    for i in range(3):
        x_ref[level(6 + i), :] = pair_rims(fields[2 * i][1], fields[2 * i + 1][1])


def depth_of(count, levels):
    return (count + count * (count - 1.0) * (1.0 / levels)) * (1.0 / levels)


def substeps_kernel(
    y_ref, a_in, z_in, su_ref, sv_ref, out_u, out_v, out_eta,
    eta_ref, u_ref, v_ref, w_ref, fu_ref, fv_ref, du_ref, dv_ref, cu_ref, cv_ref, tw_ref, q_ref, t_ref,
):
    levels = su_ref.shape[0] // COLS
    tau = STEP / SUBSTEPS
    blocks = 2 * REACH + 1
    even = is_even("lon")
    lane = lane_index()

    def at(p, shift=0):
        return pl.ds(COLS * (p + 1) + shift, COLS)

    places = (
        ((z_in, 0), (a_in, 2)), ((z_in, 1), (a_in, 1)), ((z_in, 2), (a_in, 0)),
        ((y_ref, 2), (y_ref, 0)), ((y_ref, 1), (y_ref, 1)), ((y_ref, 0), (y_ref, 2)),
        ((a_in, 0), (z_in, 2)), ((a_in, 1), (z_in, 1)), ((a_in, 2), (z_in, 0)),
    )
    for p, (for_even, for_odd) in enumerate(places):
        def tile(i):
            first = for_even[0][pl.ds(for_even[1] * FIELDS + COLS * i, COLS), :]
            if p == REACH:
                return first
            return jnp.where(even, first, for_odd[0][pl.ds(for_odd[1] * FIELDS + COLS * i, COLS), :])

        targets = (fu_ref, fv_ref, u_ref, v_ref, w_ref, eta_ref)
        for i, ref in enumerate(targets):
            value = tile(i)
            ref[0, at(p), :] = tau * value if i < 2 else value
        for i in range(3):
            value = tile(6 + i)
            other = pltpu.roll(value, LANES // 2, 1)
            if i == 0:
                value, other = tau * value, tau * other
            targets[2 * i][1, at(p), :] = value
            targets[2 * i + 1][1, at(p), :] = other

    total_rows = LANES * lax.axis_size("lat")
    base = (lax.axis_index("lat") * LANES).astype(jnp.float32)
    own_row = lane.astype(jnp.float32) + base
    rim_row = jnp.where(lane < LANES // 2, lane + LANES, lane - LANES).astype(jnp.float32) + base
    spin = [
        [0.25 * tau * 0.4 * (2.0 * (r + half) * (1.0 / total_rows) - 1.0) for half in (0.5, 1.0)]
        for r in (own_row, rim_row)
    ]
    for p in range(blocks):
        water = [w_ref[t, at(p), :] for t in range(2)]
        water_north = north(*water)
        for t in range(2):
            open_u = jnp.minimum(water[t], w_ref[t, at(p, 1), :])
            open_v = jnp.minimum(water[t], water_north[t])
            du_ref[t, at(p), :] = tau * depth_of(open_u, levels)
            dv_ref[t, at(p), :] = tau * depth_of(open_v, levels)
            cu_ref[t, at(p), :] = jnp.where(open_u > 0.0, spin[t][0], 0.0)
            cv_ref[t, at(p), :] = jnp.where(open_v > 0.0, spin[t][1], 0.0)
            tw_ref[t, at(p), :] = jnp.where(water[t] > 0.0, tau, 0.0)

    flow_u, flow_v = u_ref[0, at(REACH), :], v_ref[0, at(REACH), :]
    zero = jnp.zeros((COLS, LANES), jnp.float32)

    def substep(first, last):
        def body(_, carry):
            total_u, total_v = carry
            for p in range(first, last):
                u = [u_ref[t, at(p), :] for t in range(2)]
                u_west = [u_ref[t, at(p, -1), :] for t in range(2)]
                v = [v_ref[t, at(p), :] for t in range(2)]
                v_south = south(*v)
                both = [u[t] + u_west[t] for t in range(2)]
                both_north = north(*both)
                for t in range(2):
                    spread = (u[t] - u_west[t]) + (v[t] - v_south[t])
                    eta_ref[t, at(p), :] = eta_ref[t, at(p), :] - tw_ref[t, at(p), :] * spread
                    q_ref[t, at(p), :] = v[t] + v_south[t]
                    t_ref[t, at(p), :] = both[t] + both_north[t]
            for p in range(first, last):
                eta = [eta_ref[t, at(p), :] for t in range(2)]
                eta_north = north(*eta)
                for t in range(2):
                    vbar = q_ref[t, at(p), :] + q_ref[t, at(p, 1), :]
                    rise_u = eta_ref[t, at(p, 1), :] - eta[t]
                    rise_v = eta_north[t] - eta[t]
                    next_u = (u_ref[t, at(p), :] + fu_ref[t, at(p), :]) + (
                        cu_ref[t, at(p), :] * vbar - du_ref[t, at(p), :] * rise_u
                    )
                    next_v = (v_ref[t, at(p), :] + fv_ref[t, at(p), :]) - (
                        cv_ref[t, at(p), :] * t_ref[t, at(p), :] + dv_ref[t, at(p), :] * rise_v
                    )
                    u_ref[t, at(p), :] = next_u
                    v_ref[t, at(p), :] = next_v
                    if p == REACH and t == 0:
                        total_u, total_v = total_u + next_u, total_v + next_v
            return total_u, total_v

        return body

    carry = (zero, zero)
    done = 0
    for ring in range(REACH):
        until = SUBSTEPS - COLS * (REACH - 1 - ring)
        carry = lax.fori_loop(0, until - done, substep(ring, blocks - ring), carry)
        done = until
    out_eta[...] = eta_ref[0, at(REACH), :]
    water = [w_ref[t, at(REACH), :] for t in range(2)]
    open_u = jnp.minimum(water[0], w_ref[0, at(REACH, 1), :])
    open_v = jnp.minimum(water[0], north(*water)[0])
    star_u = flow_u + (STEP / tau) * fu_ref[0, at(REACH), :]
    star_v = flow_v + (STEP / tau) * fv_ref[0, at(REACH), :]
    lift_u = (carry[0] / SUBSTEPS - star_u) / jnp.maximum(depth_of(open_u, levels), 0.25)
    lift_v = (carry[1] / SUBSTEPS - star_v) / jnp.maximum(depth_of(open_v, levels), 0.25)
    for k in range(levels):
        out_u[level(k), :] = su_ref[level(k), :] + jnp.where(open_u > float(k), lift_u, 0.0)
        out_v[level(k), :] = sv_ref[level(k), :] + jnp.where(open_v > float(k), lift_v, 0.0)


def call(kernel, shapes, scratch, *operands):
    return pl.pallas_call(
        kernel,
        out_shape=[jax.ShapeDtypeStruct(s, jnp.float32) for s in shapes],
        scratch_shapes=[pltpu.VMEM(s, jnp.float32) for s in scratch],
        compiler_params=pltpu.CompilerParams(vmem_limit_bytes=VMEM_BYTES),
    )(*operands)


def swap(x, axis, first, hop, wraps):
    count = lax.axis_size(axis)
    pairs = []
    for i in range(first, count, 2):
        j = i + hop
        if wraps or 0 <= j < count:
            pairs += [(i, j % count), (j % count, i)]
    return lax.ppermute(x, axis, pairs)


def local(velocity_u, velocity_v, buoyancy, wind_x, wind_y, free_surface, land_sea, bottom_level):
    levels = velocity_u.shape[0]
    flat = (levels * COLS, LANES)
    u, v, b = (a.reshape(flat) for a in (velocity_u, velocity_v, buoyancy))
    water = (land_sea * bottom_level).astype(jnp.float32)
    rows_a, rows_z = call(
        pack_rows_kernel, [flat, flat], [], u, v, b, water, free_surface, wind_x, wind_y
    )
    rows_a = swap(rows_a, "lat", 0, 1, False)
    rows_z = swap(rows_z, "lat", 1, 1, False)
    edge = (5 * levels + 8, LANES)
    cols_a, cols_z, hu, hv, hb, hp = call(
        pack_cols_kernel, [edge, edge, flat, flat, flat, (4 * COLS, LANES)], [], u, v, b, water, rows_a, rows_z
    )
    cols_a = swap(cols_a, "lon", 0, 1, True)
    cols_z = swap(cols_z, "lon", 1, 1, True)
    both = (edge[0] + levels, LANES)
    x, star_u, star_v = call(
        levels_kernel, [(FIELDS, LANES), flat, flat], [both, both],
        u, v, b, hu, hv, hb, hp, water, free_surface, wind_x, wind_y, cols_a, cols_z,
    )
    near_a = swap(x, "lon", 0, 1, True)
    near_z = swap(x, "lon", 1, 1, True)
    y = jnp.concatenate([near_a, x, near_z], 0)
    far_a = swap(y, "lon", 0, 3, True)
    far_z = swap(y, "lon", 1, 3, True)
    state = (2, (2 * REACH + 3) * COLS, LANES)
    new_u, new_v, surface = call(
        substeps_kernel, [flat, flat, (COLS, LANES)], [state] * 13, y, far_a, far_z, star_u, star_v
    )
    return new_u.reshape(velocity_u.shape), new_v.reshape(velocity_v.shape), surface


def solution(mesh):
    return jax.shard_map(
        local,
        mesh=mesh,
        in_specs=(P(None, "lon", "lat"),) * 3 + (P("lon", "lat"),) * 5,
        out_specs=(P(None, "lon", "lat"), P(None, "lon", "lat"), P("lon", "lat")),
        check_vma=False,
    )
```

time: 634 us -> 76.1 us (0.12)
  the two profiles are of different devices: /device:TPU:1 before, /device:TPU:80 now
where the time goes in v1:
time: 76.1 us; the launch traced here: 75.6 us
  starting transfers between devices  43.6 us (57%)
  waiting for transfers between devices  19.6 us (26%)
  Pallas kernels  7.47 us (10%)
  local copies, waits for them, and re-layouts  3.48 us (5%)
  between operations  0.77 us (1%)
    ppermute x8, starting transfers between devices, swap(): return lax.ppermute(x, axis, pairs)  43.6 us
    ppermute x8, waiting for transfers between devices, swap(): return lax.ppermute(x, axis, pairs)  19.6 us
    pallas_call x4, Pallas kernels, call(): pl.pallas_call(kernel, out_shape=[jax.ShapeDtypeStruct(s, jnp.float32) fo...  7.47 us
    unnamed x14, local copies, waits for them, and re-layouts  3.48 us
  transfers between devices with their start and end apart: 8, of which 6 were waited for; matrix products, arithmetic and copies ran while one was open for 0% of the time, Pallas kernels for 0%

profile of v1, /device:TPU:80, one launch (start us, length us, event | category | flops | bytes accessed | tf_op | source)
XLA Modules:
  0.0 75.6 jit_solution(10976971785800468093)
XLA Ops:
  0.6 0.0 copy-start.4
  0.6 0.0 copy-start.5
  0.7 0.7 multiply_convert_fusion.water_ref
  1.4 0.0 copy-start.3
  1.4 0.0 copy-done.4
  1.4 0.0 copy-done.5
  1.4 0.7 copy-done.3
  2.1 0.0 copy-start
  2.1 0.9 %copy-done = f32[48,8,128]{2,1,0:T(8,128)S(1)} copy-done((f32[48,8,128]{2,1,0:T(8,128)S(1)}, f32[48,8,128]{2,1,0:T(8,128)}, u32[]{:S(2)}) %copy-start) | copy-done | bytes 196632
  3.0 0.0 copy-start.1
  3.0 0.9 %copy-done.1 = f32[48,8,128]{2,1,0:T(8,128)S(1)} copy-done((f32[48,8,128]{2,1,0:T(8,128)S(1)}, f32[48,8,128]{2,1,0:T(8,128)}, u32[]{:S(2)}) %copy-start.1) | copy-done | bytes 196632
  3.9 0.0 copy-start.2
  3.9 0.9 %copy-done.2 = f32[48,8,128]{2,1,0:T(8,128)S(1)} copy-done((f32[48,8,128]{2,1,0:T(8,128)S(1)}, f32[48,8,128]{2,1,0:T(8,128)}, u32[]{:S(2)}) %copy-start.2) | copy-done | bytes 196632
  4.8 0.3 shard_map.103
  5.2 1.9 %collective-permute-start = (f32[384,128]{1,0:T(8,128)S(1)}, f32[384,128]{1,0:T(8,128)S(1)}, u32[]{:S(2)}, u32[]{:S(2)}) collective-permute-start(f32[384,128]{1,0:T(8,128)S(1)} %get-tuple-element.17), channel_id=1, source_target_pairs={{0,1},{1,0},{2,3},{3,2},{4,5},{5,4},{6,7},{7,6},{8,9},{9,8},{10,11... | collective-permute-start | bytes 589832 | tf_op jit(solution)/shard_map/ppermute | solution.py:332
  7.1 2.5 %collective-permute-start.1 = (f32[384,128]{1,0:T(8,128)S(1)}, f32[384,128]{1,0:T(8,128)S(1)}, u32[]{:S(2)}, u32[]{:S(2)}) collective-permute-start(f32[384,128]{1,0:T(8,128)S(1)} %get-tuple-element.18), channel_id=1, source_target_pairs={{1,2},{2,1},{3,4},{4,3},{5,6},{6,5},{9,10},{10,9},{11,12},{12,11},... | collective-permute-start | bytes 589832 | tf_op jit(solution)/shard_map/ppermute | solution.py:332
  9.6 0.0 collective-permute-done.a_in
  9.6 4.5 %collective-permute-done.1.z_in = f32[384,128]{1,0:T(8,128)S(1)} collective-permute-done((f32[384,128]{1,0:T(8,128)S(1)}, f32[384,128]{1,0:T(8,128)S(1)}, u32[]{:S(2)}, u32[]{:S(2)}) %collective-permute-start.1) | collective-permute-done | bytes 196640 | tf_op jit(solution)/shard_map/ppermute | solution.py:332
  14.1 0.4 shard_map.104
  14.5 3.8 %collective-permute-start.2 = (f32[248,128]{1,0:T(8,128)S(1)}, f32[248,128]{1,0:T(8,128)S(1)}, u32[]{:S(2)}, u32[]{:S(2)}) collective-permute-start(f32[248,128]{1,0:T(8,128)S(1)} %get-tuple-element.23), channel_id=1, source_target_pairs={{0,8},{8,0},{16,24},{24,16},{32,40},{40,32},{48,56},{56,48},{64,72... | collective-permute-start | bytes 380936 | tf_op jit(solution)/shard_map/ppermute | solution.py:332
  18.3 1.9 %collective-permute-start.3 = (f32[248,128]{1,0:T(8,128)S(1)}, f32[248,128]{1,0:T(8,128)S(1)}, u32[]{:S(2)}, u32[]{:S(2)}) collective-permute-start(f32[248,128]{1,0:T(8,128)S(1)} %get-tuple-element.24), channel_id=1, source_target_pairs={{8,16},{16,8},{24,32},{32,24},{40,48},{48,40},{56,64},{64,56},{72,... | collective-permute-start | bytes 380936 | tf_op jit(solution)/shard_map/ppermute | solution.py:332
  20.3 2.1 %collective-permute-done.2.a_in = f32[248,128]{1,0:T(8,128)S(1)} collective-permute-done((f32[248,128]{1,0:T(8,128)S(1)}, f32[248,128]{1,0:T(8,128)S(1)}, u32[]{:S(2)}, u32[]{:S(2)}) %collective-permute-start.2) | collective-permute-done | bytes 127008 | tf_op jit(solution)/shard_map/ppermute | solution.py:332
  22.4 3.4 %collective-permute-done.3.z_in = f32[248,128]{1,0:T(8,128)S(1)} collective-permute-done((f32[248,128]{1,0:T(8,128)S(1)}, f32[248,128]{1,0:T(8,128)S(1)}, u32[]{:S(2)}, u32[]{:S(2)}) %collective-permute-start.3) | collective-permute-done | bytes 127008 | tf_op jit(solution)/shard_map/ppermute | solution.py:332
  25.8 0.8 %shard_map.105 = (f32[72,128]{1,0:T(8,128)S(1)}, f32[384,128]{1,0:T(8,128)S(1)}, f32[384,128]{1,0:T(8,128)S(1)}) custom-call(f32[384,128]{1,0:T(8,128)S(1)} %bitcast.7, f32[384,128]{1,0:T(8,128)S(1)} %bitcast.10, f32[384,128]{1,0:T(8,128)S(1)} %bitcast.13, f32[384,128]{1,0:T(8,128)S(1)} %get-tuple-element.19.hu_ref, ...), custom_call_target="tpu_custom_call" | custom-call | tf_op jit(solution)/shard_map/pallas_call | solution.py:317
  26.6 5.2 %collective-permute-start.4 = (f32[72,128]{1,0:T(8,128)S(1)}, f32[72,128]{1,0:T(8,128)S(1)}, u32[]{:S(2)}, u32[]{:S(2)}) collective-permute-start(f32[72,128]{1,0:T(8,128)S(1)} %get-tuple-element.25), channel_id=1, source_target_pairs={{0,8},{8,0},{16,24},{24,16},{32,40},{40,32},{48,56},{56,48},{64,72... | collective-permute-start | bytes 110600 | tf_op jit(solution)/shard_map/ppermute | solution.py:332
  31.8 15.1 %collective-permute-start.5 = (f32[72,128]{1,0:T(8,128)S(1)}, f32[72,128]{1,0:T(8,128)S(1)}, u32[]{:S(2)}, u32[]{:S(2)}) collective-permute-start(f32[72,128]{1,0:T(8,128)S(1)} %get-tuple-element.25), channel_id=1, source_target_pairs={{8,16},{16,8},{24,32},{32,24},{40,48},{48,40},{56,64},{64,56},{72,... | collective-permute-start | bytes 110600 | tf_op jit(solution)/shard_map/ppermute | solution.py:332
  46.9 0.0 collective-permute-done.4
  46.9 1.9 %collective-permute-done.5 = f32[72,128]{1,0:T(8,128)S(1)} collective-permute-done((f32[72,128]{1,0:T(8,128)S(1)}, f32[72,128]{1,0:T(8,128)S(1)}, u32[]{:S(2)}, u32[]{:S(2)}) %collective-permute-start.5) | collective-permute-done | bytes 36896 | tf_op jit(solution)/shard_map/ppermute | solution.py:332
  48.8 11.2 %collective-permute-start.7 = (f32[216,128]{1,0:T(8,128)S(1)}, f32[216,128]{1,0:T(8,128)S(1)}, u32[]{:S(2)}, u32[]{:S(2)}) collective-permute-start(f32[216,128]{1,0:T(8,128)S(1)} %constant_dynamic-update-slice_fusion.y_ref), channel_id=1, source_target_pairs={{8,32},{32,8},{24,48},{48,24},{40,64},{64,40},{56,80},{80,56},{72,... | collective-permute-start | bytes 331784 | tf_op jit(solution)/shard_map/ppermute | solution.py:332
  60.0 1.9 %collective-permute-start.6 = (f32[216,128]{1,0:T(8,128)S(1)}, f32[216,128]{1,0:T(8,128)S(1)}, u32[]{:S(2)}, u32[]{:S(2)}) collective-permute-start(f32[216,128]{1,0:T(8,128)S(1)} %constant_dynamic-update-slice_fusion.y_ref), channel_id=1, source_target_pairs={{0,24},{24,0},{16,40},{40,16},{32,56},{56,32},{48,72},{72,48},{64,... | collective-permute-start | bytes 331784 | tf_op jit(solution)/shard_map/ppermute | solution.py:332
  61.9 2.6 %collective-permute-done.7.z_in = f32[216,128]{1,0:T(8,128)S(1)} collective-permute-done((f32[216,128]{1,0:T(8,128)S(1)}, f32[216,128]{1,0:T(8,128)S(1)}, u32[]{:S(2)}, u32[]{:S(2)}) %collective-permute-start.7) | collective-permute-done | bytes 110624 | tf_op jit(solution)/shard_map/ppermute | solution.py:332
  64.5 5.2 %collective-permute-done.6.a_in = f32[216,128]{1,0:T(8,128)S(1)} collective-permute-done((f32[216,128]{1,0:T(8,128)S(1)}, f32[216,128]{1,0:T(8,128)S(1)}, u32[]{:S(2)}, u32[]{:S(2)}) %collective-permute-start.6) | collective-permute-done | bytes 110624 | tf_op jit(solution)/shard_map/ppermute | solution.py:332
  69.7 6.0 %shard_map.106 = (f32[384,128]{1,0:T(8,128)}, f32[384,128]{1,0:T(8,128)}, f32[8,128]{1,0:T(8,128)}) custom-call(f32[216,128]{1,0:T(8,128)S(1)} %constant_dynamic-update-slice_fusion.y_ref, f32[216,128]{1,0:T(8,128)S(1)} %collective-permute-done.6.a_in, f32[216,128]{1,0:T(8,128)S(1)} %collective-permute-done.7.z_in, f32[384,128]{1,0:T(8,128)S(1)} %get-tuple-element.26.su_ref, ...), custom_call_target="tpu_custom_call" | custom-call | tf_op jit(solution)/shard_map/pallas_call | solution.py:317
  (3 shorter events, 0.0 us)
Async XLA Ops:
  0.6 0.7 copy-start.4
  0.6 0.7 copy-start.5
  1.4 0.7 copy-start.3
  2.1 0.9 %copy-start = (f32[48,8,128]{2,1,0:T(8,128)S(1)}, f32[48,8,128]{2,1,0:T(8,128)}, u32[]{:S(2)}) copy-start(f32[48,8,128]{2,1,0:T(8,128)} %param.8) | copy-start | bytes 589828
  3.0 0.9 %copy-start.1 = (f32[48,8,128]{2,1,0:T(8,128)S(1)}, f32[48,8,128]{2,1,0:T(8,128)}, u32[]{:S(2)}) copy-start(f32[48,8,128]{2,1,0:T(8,128)} %param.9) | copy-start | bytes 589828
  3.9 0.9 %copy-start.2 = (f32[48,8,128]{2,1,0:T(8,128)S(1)}, f32[48,8,128]{2,1,0:T(8,128)}, u32[]{:S(2)}) copy-start(f32[48,8,128]{2,1,0:T(8,128)} %param.10) | copy-start | bytes 589828
  5.2 4.4 %collective-permute-start = (f32[384,128]{1,0:T(8,128)S(1)}, f32[384,128]{1,0:T(8,128)S(1)}, u32[]{:S(2)}, u32[]{:S(2)}) collective-permute-start(f32[384,128]{1,0:T(8,128)S(1)} %get-tuple-element.17), channel_id=1, source_target_pairs={{0,1},{1,0},{2,3},{3,2},{4,5},{5,4},{6,7},{7,6},{8,9},{9,8},{10,11... | collective-permute-start | bytes 589832 | tf_op jit(solution)/shard_map/ppermute | solution.py:332
  7.1 7.0 %collective-permute-start.1 = (f32[384,128]{1,0:T(8,128)S(1)}, f32[384,128]{1,0:T(8,128)S(1)}, u32[]{:S(2)}, u32[]{:S(2)}) collective-permute-start(f32[384,128]{1,0:T(8,128)S(1)} %get-tuple-element.18), channel_id=1, source_target_pairs={{1,2},{2,1},{3,4},{4,3},{5,6},{6,5},{9,10},{10,9},{11,12},{12,11},... | collective-permute-start | bytes 589832 | tf_op jit(solution)/shard_map/ppermute | solution.py:332
  14.5 7.9 %collective-permute-start.2 = (f32[248,128]{1,0:T(8,128)S(1)}, f32[248,128]{1,0:T(8,128)S(1)}, u32[]{:S(2)}, u32[]{:S(2)}) collective-permute-start(f32[248,128]{1,0:T(8,128)S(1)} %get-tuple-element.23), channel_id=1, source_target_pairs={{0,8},{8,0},{16,24},{24,16},{32,40},{40,32},{48,56},{56,48},{64,72... | collective-permute-start | bytes 380936 | tf_op jit(solution)/shard_map/ppermute | solution.py:332
  18.3 7.4 %collective-permute-start.3 = (f32[248,128]{1,0:T(8,128)S(1)}, f32[248,128]{1,0:T(8,128)S(1)}, u32[]{:S(2)}, u32[]{:S(2)}) collective-permute-start(f32[248,128]{1,0:T(8,128)S(1)} %get-tuple-element.24), channel_id=1, source_target_pairs={{8,16},{16,8},{24,32},{32,24},{40,48},{48,40},{56,64},{64,56},{72,... | collective-permute-start | bytes 380936 | tf_op jit(solution)/shard_map/ppermute | solution.py:332
  26.6 20.4 %collective-permute-start.4 = (f32[72,128]{1,0:T(8,128)S(1)}, f32[72,128]{1,0:T(8,128)S(1)}, u32[]{:S(2)}, u32[]{:S(2)}) collective-permute-start(f32[72,128]{1,0:T(8,128)S(1)} %get-tuple-element.25), channel_id=1, source_target_pairs={{0,8},{8,0},{16,24},{24,16},{32,40},{40,32},{48,56},{56,48},{64,72... | collective-permute-start | bytes 110600 | tf_op jit(solution)/shard_map/ppermute | solution.py:332
  31.8 17.0 %collective-permute-start.5 = (f32[72,128]{1,0:T(8,128)S(1)}, f32[72,128]{1,0:T(8,128)S(1)}, u32[]{:S(2)}, u32[]{:S(2)}) collective-permute-start(f32[72,128]{1,0:T(8,128)S(1)} %get-tuple-element.25), channel_id=1, source_target_pairs={{8,16},{16,8},{24,32},{32,24},{40,48},{48,40},{56,64},{64,56},{72,... | collective-permute-start | bytes 110600 | tf_op jit(solution)/shard_map/ppermute | solution.py:332
  48.8 15.7 %collective-permute-start.7 = (f32[216,128]{1,0:T(8,128)S(1)}, f32[216,128]{1,0:T(8,128)S(1)}, u32[]{:S(2)}, u32[]{:S(2)}) collective-permute-start(f32[216,128]{1,0:T(8,128)S(1)} %constant_dynamic-update-slice_fusion.y_ref), channel_id=1, source_target_pairs={{8,32},{32,8},{24,48},{48,24},{40,64},{64,40},{56,80},{80,56},{72,... | collective-permute-start | bytes 331784 | tf_op jit(solution)/shard_map/ppermute | solution.py:332
  60.0 9.7 %collective-permute-start.6 = (f32[216,128]{1,0:T(8,128)S(1)}, f32[216,128]{1,0:T(8,128)S(1)}, u32[]{:S(2)}, u32[]{:S(2)}) collective-permute-start(f32[216,128]{1,0:T(8,128)S(1)} %constant_dynamic-update-slice_fusion.y_ref), channel_id=1, source_target_pairs={{0,24},{24,0},{16,40},{40,16},{32,56},{56,32},{48,72},{72,48},{64,... | collective-permute-start | bytes 331784 | tf_op jit(solution)/shard_map/ppermute | solution.py:332

commit v2 on v1

--- a/solution.py
+++ b/solution.py
@@ -10,6 +10,8 @@
 LANES = 128
 COLS = 8
 RIM = 32
+SLOTS = 4
+CHUNKS = 4
 REACH = 4
 FIELDS = 9 * COLS
 STEP = 6.0
@@ -54,43 +56,78 @@
     return jnp.where((lane >= RIM) & (lane < LANES - RIM), pltpu.roll(second, LANES // 2, 1), first)
 
 
-def pack_rows(u_ref, v_ref, b_ref, plane_refs, a_ref, z_ref):
+def strips(parts, shifts):
+    slot = lane_index() // RIM
+    moved = [pltpu.roll(p, s, 1) if s else p for p, s in zip(parts, shifts)]
+    return jnp.where(
+        slot < 2, jnp.where(slot == 0, moved[0], moved[1]), jnp.where(slot == 2, moved[2], moved[3])
+    )
+
+
+def pack_rows_kernel(
+    u_in, v_in, b_in, land_in, bottom_in, eta_in, wx_in, wy_in,
+    a_ref, z_ref, u_ref, v_ref, b_ref, plane_ref, land_ref, bottom_ref, sems, plane_sem,
+):
+    levels = u_in.shape[0] // COLS
+    groups = levels // SLOTS
+    chunks = sems.shape[0]
+    fields = ((u_in, u_ref), (v_in, v_ref), (b_in, b_ref))
+    part = u_in.shape[0] // chunks
+    copies = [
+        [
+            pltpu.make_async_copy(src.at[pl.ds(c * part, part)], dst.at[pl.ds(c * part, part)], sems.at[c, f])
+            for f, (src, dst) in enumerate(fields)
+        ]
+        for c in range(chunks)
+    ]
+    planes = [
+        pltpu.make_async_copy(src, dst, plane_sem.at[i])
+        for i, (src, dst) in enumerate(
+            (
+                (land_in, land_ref), (bottom_in, bottom_ref), (eta_in, plane_ref.at[level(1)]),
+                (wx_in, plane_ref.at[level(2)]), (wy_in, plane_ref.at[level(3)]),
+            )
+        )
+    ]
+    for copy in sum(copies, []) + planes:
+        copy.start()
     even = is_even("lat")
-    lane = lane_index()
-    slot = lane // RIM
-
-    def strips(parts, shifts):
-        moved = [pltpu.roll(p, s, 1) if s else p for p, s in zip(parts, shifts)]
-        return jnp.where(
-            slot < 2, jnp.where(slot == 0, moved[0], moved[1]), jnp.where(slot == 2, moved[2], moved[3])
-        )
-
-    for k in range(u_ref.shape[0] // COLS):
-        u, v, b = u_ref[level(k), :], v_ref[level(k), :], b_ref[level(k), :]
-        parts = (u, v, b, plane_refs[k][...] if k < len(plane_refs) else b)
-        upper = strips(parts, (32, 64, 96, 0))
-        lower = strips(parts, (0, 32, 64, 96))
-        a_ref[level(k), :] = jnp.where(even, upper, lower)
-        z_ref[level(k), :] = jnp.where(even, lower, upper)
-
-
-def pack_rows_kernel(u_ref, v_ref, b_ref, water_ref, eta_ref, wx_ref, wy_ref, a_ref, z_ref):
-    pack_rows(u_ref, v_ref, b_ref, (water_ref, eta_ref, wx_ref, wy_ref), a_ref, z_ref)
-
-
-def pack_cols_kernel(u_ref, v_ref, b_ref, water_ref, a_in, z_in, a_ref, z_ref, hu_ref, hv_ref, hb_ref, hp_ref):
+
+    def send(at, parts):
+        upper, lower = strips(parts, (32, 64, 96, 0)), strips(parts, (0, 32, 64, 96))
+        a_ref[level(at), :] = jnp.where(even, upper, lower)
+        z_ref[level(at), :] = jnp.where(even, lower, upper)
+
+    for c in range(chunks):
+        for f, (_, ref) in enumerate(fields):
+            copies[c][f].wait()
+            for g in range(c * groups // chunks, (c + 1) * groups // chunks):
+                send(f * groups + g, [ref[level(SLOTS * g + s), :] for s in range(SLOTS)])
+    for copy in planes:
+        copy.wait()
+    plane_ref[level(0), :] = (land_ref[...] * bottom_ref[...]).astype(jnp.float32)
+    send(3 * groups, [plane_ref[level(s), :] for s in range(SLOTS)])
+
+
+def pack_cols_kernel(u_ref, v_ref, b_ref, plane_ref, z_in, a_in, a_ref, z_ref, hu_ref, hv_ref, hb_ref, hp_ref):
     even = is_even("lat")
-    lane = lane_index()
-    upper = lane < LANES // 2
+    upper = lane_index() < LANES // 2
     levels = u_ref.shape[0] // COLS
-    for k in range(levels):
-        a, z = a_in[level(k), :], z_in[level(k), :]
-        n, s = jnp.where(even, a, z), jnp.where(even, z, a)
-        hu_ref[level(k), :] = jnp.where(upper, n, pltpu.roll(s, 96, 1))
-        hv_ref[level(k), :] = jnp.where(upper, pltpu.roll(n, 96, 1), pltpu.roll(s, 64, 1))
-        hb_ref[level(k), :] = jnp.where(upper, pltpu.roll(n, 64, 1), pltpu.roll(s, 32, 1))
-        if k < 4:
-            hp_ref[level(k), :] = jnp.where(upper, pltpu.roll(n, 32, 1), s)
+    groups = levels // SLOTS
+
+    def receive(at, s):
+        a, z = a_in[level(at), :], z_in[level(at), :]
+        n, o = jnp.where(even, a, z), jnp.where(even, z, a)
+        to_first, to_last = (LANES - RIM * s) % LANES, (LANES - RIM - RIM * s) % LANES
+        n = pltpu.roll(n, to_first, 1) if to_first else n
+        o = pltpu.roll(o, to_last, 1) if to_last else o
+        return jnp.where(upper, n, o)
+
+    for f, ref in enumerate((hu_ref, hv_ref, hb_ref)):
+        for k in range(levels):
+            ref[level(k), :] = receive(f * groups + k // SLOTS, k % SLOTS)
+    for s in range(SLOTS):
+        hp_ref[level(s), :] = receive(3 * groups, s)
     even_col = is_even("lon")
 
     def edge(ref, rows, col):
@@ -102,7 +139,7 @@
         out_ref[pl.ds(2 * levels, levels), :] = edge(b_ref, levels, col)
         out_ref[pl.ds(3 * levels, levels), :] = pair_rims(edge(hu_ref, levels, col), edge(hv_ref, levels, col))
         out_ref[pl.ds(4 * levels, levels), :] = edge(hb_ref, levels, col)
-        out_ref[pl.ds(5 * levels, 1), :] = water_ref[pl.ds(col, 1), :]
+        out_ref[pl.ds(5 * levels, 1), :] = plane_ref[pl.ds(col, 1), :]
         out_ref[pl.ds(5 * levels + 1, 1), :] = hp_ref[pl.ds(col, 1), :]
         out_ref[pl.ds(5 * levels + 2, 6), :] = jnp.zeros((6, LANES), jnp.float32)
 
@@ -118,7 +155,7 @@
 
 
 def levels_kernel(
-    u_ref, v_ref, b_ref, hu_ref, hv_ref, hb_ref, hp_ref, water_ref, eta_ref, wx_ref, wy_ref, a_in, z_in,
+    u_ref, v_ref, b_ref, hu_ref, hv_ref, hb_ref, hp_ref, plane_ref, z_in, a_in,
     x_ref, su_ref, sv_ref, east_ref, west_ref,
 ):
     levels = u_ref.shape[0] // COLS
@@ -151,10 +188,7 @@
             jnp.where(bottom_col, row(west_ref, rim_at[name] + k), pltpu.roll(rim, 1, 0)),
         )
 
-    water = (water_ref[...], hp_ref[pl.ds(0, COLS), :])
-    eta = (eta_ref[...], hp_ref[pl.ds(COLS, COLS), :])
-    wx = (wx_ref[...], hp_ref[pl.ds(2 * COLS, COLS), :])
-    wy = (wy_ref[...], hp_ref[pl.ds(3 * COLS, COLS), :])
+    water, eta, wx, wy = [(plane_ref[level(i), :], hp_ref[level(i), :]) for i in range(SLOTS)]
     open_u = [jnp.minimum(w, e) for w, e in zip(water, east(water, "w", 0))]
     open_v = [jnp.minimum(w, n) for w, n in zip(water, north(*water))]
     zero = jnp.zeros((COLS, LANES), jnp.float32)
@@ -201,6 +235,7 @@
 def substeps_kernel(
     y_ref, a_in, z_in, su_ref, sv_ref, out_u, out_v, out_eta,
     eta_ref, u_ref, v_ref, w_ref, fu_ref, fv_ref, du_ref, dv_ref, cu_ref, cv_ref, tw_ref, q_ref, t_ref,
+    eta_north_ref, u_north_ref, tw_north_ref,
 ):
     levels = su_ref.shape[0] // COLS
     tau = STEP / SUBSTEPS
@@ -212,9 +247,9 @@
         return pl.ds(COLS * (p + 1) + shift, COLS)
 
     places = (
-        ((z_in, 0), (a_in, 2)), ((z_in, 1), (a_in, 1)), ((z_in, 2), (a_in, 0)),
-        ((y_ref, 2), (y_ref, 0)), ((y_ref, 1), (y_ref, 1)), ((y_ref, 0), (y_ref, 2)),
-        ((a_in, 0), (z_in, 2)), ((a_in, 1), (z_in, 1)), ((a_in, 2), (z_in, 0)),
+        ((z_in, 2), (a_in, 0)), ((z_in, 1), (a_in, 1)), ((z_in, 0), (a_in, 2)),
+        ((y_ref, 0), (y_ref, 2)), ((y_ref, 1), (y_ref, 1)), ((y_ref, 2), (y_ref, 0)),
+        ((a_in, 2), (z_in, 0)), ((a_in, 1), (z_in, 1)), ((a_in, 0), (z_in, 2)),
     )
     for p, (for_even, for_odd) in enumerate(places):
         def tile(i):
@@ -246,7 +281,10 @@
     for p in range(blocks):
         water = [w_ref[t, at(p), :] for t in range(2)]
         water_north = north(*water)
+        eta_north = north(eta_ref[0, at(p), :], eta_ref[1, at(p), :])
         for t in range(2):
+            eta_north_ref[t, at(p), :] = eta_north[t]
+            tw_north_ref[t, at(p), :] = jnp.where(water_north[t] > 0.0, tau, 0.0)
             open_u = jnp.minimum(water[t], w_ref[t, at(p, 1), :])
             open_v = jnp.minimum(water[t], water_north[t])
             du_ref[t, at(p), :] = tau * depth_of(open_u, levels)
@@ -265,17 +303,22 @@
                 u = [u_ref[t, at(p), :] for t in range(2)]
                 u_west = [u_ref[t, at(p, -1), :] for t in range(2)]
                 v = [v_ref[t, at(p), :] for t in range(2)]
-                v_south = south(*v)
-                both = [u[t] + u_west[t] for t in range(2)]
-                both_north = north(*both)
+                v_south, v_north, u_north = south(*v), north(*v), north(*u)
                 for t in range(2):
+                    u_north_ref[t, at(p), :] = u_north[t]
+                for t in range(2):
+                    u_north_west = u_north_ref[t, at(p, -1), :]
                     spread = (u[t] - u_west[t]) + (v[t] - v_south[t])
+                    spread_north = (u_north[t] - u_north_west) + (v_north[t] - v[t])
                     eta_ref[t, at(p), :] = eta_ref[t, at(p), :] - tw_ref[t, at(p), :] * spread
+                    eta_north_ref[t, at(p), :] = (
+                        eta_north_ref[t, at(p), :] - tw_north_ref[t, at(p), :] * spread_north
+                    )
                     q_ref[t, at(p), :] = v[t] + v_south[t]
-                    t_ref[t, at(p), :] = both[t] + both_north[t]
+                    t_ref[t, at(p), :] = (u[t] + u_west[t]) + (u_north[t] + u_north_west)
             for p in range(first, last):
                 eta = [eta_ref[t, at(p), :] for t in range(2)]
-                eta_north = north(*eta)
+                eta_north = [eta_north_ref[t, at(p), :] for t in range(2)]
                 for t in range(2):
                     vbar = q_ref[t, at(p), :] + q_ref[t, at(p, 1), :]
                     rise_u = eta_ref[t, at(p, 1), :] - eta[t]
@@ -298,7 +341,7 @@
     done = 0
     for ring in range(REACH):
         until = SUBSTEPS - COLS * (REACH - 1 - ring)
-        carry = lax.fori_loop(0, until - done, substep(ring, blocks - ring), carry)
+        carry = lax.fori_loop(0, until - done, substep(ring, blocks - ring), carry, unroll=2)
         done = until
     out_eta[...] = eta_ref[0, at(REACH), :]
     water = [w_ref[t, at(REACH), :] for t in range(2)]
@@ -313,12 +356,13 @@
         out_v[level(k), :] = sv_ref[level(k), :] + jnp.where(open_v > float(k), lift_v, 0.0)
 
 
-def call(kernel, shapes, scratch, *operands):
+def call(kernel, shapes, scratch, *operands, **specs):
     return pl.pallas_call(
         kernel,
         out_shape=[jax.ShapeDtypeStruct(s, jnp.float32) for s in shapes],
-        scratch_shapes=[pltpu.VMEM(s, jnp.float32) for s in scratch],
+        scratch_shapes=[pltpu.VMEM(s, jnp.float32) if isinstance(s, tuple) else s for s in scratch],
         compiler_params=pltpu.CompilerParams(vmem_limit_bytes=VMEM_BYTES),
+        **specs,
     )(*operands)
 
 
@@ -336,31 +380,37 @@
     levels = velocity_u.shape[0]
     flat = (levels * COLS, LANES)
     u, v, b = (a.reshape(flat) for a in (velocity_u, velocity_v, buoyancy))
-    water = (land_sea * bottom_level).astype(jnp.float32)
-    rows_a, rows_z = call(
-        pack_rows_kernel, [flat, flat], [], u, v, b, water, free_surface, wind_x, wind_y
-    )
+    send = (3 * levels // SLOTS * COLS + COLS, LANES)
+    inputs = (u, v, b, land_sea, bottom_level, free_surface, wind_x, wind_y)
+    whole = pltpu.VMEM((COLS, LANES), jnp.int32)
+    rows_a, rows_z, u, v, b, planes = call(
+        pack_rows_kernel,
+        [send, send, flat, flat, flat, (SLOTS * COLS, LANES)],
+        [whole, whole, pltpu.SemaphoreType.DMA((CHUNKS, 3)), pltpu.SemaphoreType.DMA((5,))],
+        *[pltpu.with_memory_space_constraint(a, pltpu.HBM) for a in inputs],
+        in_specs=[pl.BlockSpec(memory_space=pltpu.HBM)] * 8,
+    )
+    rows_z = swap(rows_z, "lat", 1, 1, False)
     rows_a = swap(rows_a, "lat", 0, 1, False)
-    rows_z = swap(rows_z, "lat", 1, 1, False)
     edge = (5 * levels + 8, LANES)
     cols_a, cols_z, hu, hv, hb, hp = call(
-        pack_cols_kernel, [edge, edge, flat, flat, flat, (4 * COLS, LANES)], [], u, v, b, water, rows_a, rows_z
-    )
+        pack_cols_kernel, [edge, edge, flat, flat, flat, (SLOTS * COLS, LANES)], [], u, v, b, planes, rows_z, rows_a
+    )
+    cols_z = swap(cols_z, "lon", 1, 1, True)
     cols_a = swap(cols_a, "lon", 0, 1, True)
-    cols_z = swap(cols_z, "lon", 1, 1, True)
     both = (edge[0] + levels, LANES)
     x, star_u, star_v = call(
         levels_kernel, [(FIELDS, LANES), flat, flat], [both, both],
-        u, v, b, hu, hv, hb, hp, water, free_surface, wind_x, wind_y, cols_a, cols_z,
-    )
+        u, v, b, hu, hv, hb, hp, planes, cols_z, cols_a,
+    )
+    near_z = swap(x, "lon", 1, 1, True)
     near_a = swap(x, "lon", 0, 1, True)
-    near_z = swap(x, "lon", 1, 1, True)
-    y = jnp.concatenate([near_a, x, near_z], 0)
+    y = jnp.concatenate([near_z, x, near_a], 0)
+    far_z = swap(y, "lon", 1, 3, True)
     far_a = swap(y, "lon", 0, 3, True)
-    far_z = swap(y, "lon", 1, 3, True)
     state = (2, (2 * REACH + 3) * COLS, LANES)
     new_u, new_v, surface = call(
-        substeps_kernel, [flat, flat, (COLS, LANES)], [state] * 13, y, far_a, far_z, star_u, star_v
+        substeps_kernel, [flat, flat, (COLS, LANES)], [state] * 16, y, far_a, far_z, star_u, star_v
     )
     return new_u.reshape(velocity_u.shape), new_v.reshape(velocity_v.shape), surface
 

time: 76.1 us -> 68.4 us (0.90)
  the two profiles are of different devices: /device:TPU:80 before, /device:TPU:8 now
where the time goes in v2:
time: 68.4 us; the launch traced here: 68.1 us
  starting transfers between devices  39.1 us (57%)
  waiting for transfers between devices  20.2 us (30%)
  Pallas kernels  8.11 us (12%)
  between operations  0.72 us (1%)
    ppermute x8, starting transfers between devices, swap(): return lax.ppermute(x, axis, pairs)  39.1 us
    ppermute x8, waiting for transfers between devices, swap(): return lax.ppermute(x, axis, pairs)  20.2 us
    pallas_call x4, Pallas kernels, call(): pl.pallas_call(kernel, out_shape=[jax.ShapeDtypeStruct(s, jnp.float32) fo...  8.11 us
  transfers between devices with their start and end apart: 8, of which 6 were waited for; matrix products, arithmetic and copies ran while one was open for 0% of the time, Pallas kernels for 0%

profile of v2, /device:TPU:8, one launch (start us, length us, event | category | flops | bytes accessed | tf_op | source)
XLA Modules:
  0.0 68.1 jit_solution(2557491579805564684)
XLA Ops:
  0.6 2.1 %shard_map.103 = (f32[296,128]{1,0:T(8,128)S(1)}, f32[296,128]{1,0:T(8,128)S(1)}, f32[384,128]{1,0:T(8,128)S(1)}, f32[384,128]{1,0:T(8,128)S(1)}, f32[384,128]{1,0:T(8,128)S(1)}, /*index=5*/f32[32,128]{1,0:T(8,128)S(1)}) custom-call(f32[384,128]{1,0:T(8,128)} %bitcast.5, f32[384,128]{1,0:T(8,128)} %bitcast.6, f32[384,128]{1,0:T(8,128)} %bitcast.7, ...), custom_call_target="tpu_custom_call" | custom-call | tf_op jit(solution)/shard_map/pallas_call | solution.py:360
  2.7 1.9 %collective-permute-start = (f32[296,128]{1,0:T(8,128)S(1)}, f32[296,128]{1,0:T(8,128)S(1)}, u32[]{:S(2)}, u32[]{:S(2)}) collective-permute-start(f32[296,128]{1,0:T(8,128)S(1)} %get-tuple-element.25), channel_id=1, source_target_pairs={{1,2},{2,1},{3,4},{4,3},{5,6},{6,5},{9,10},{10,9},{11,12},{12,11},... | collective-permute-start | bytes 454664 | tf_op jit(solution)/shard_map/ppermute | solution.py:376
  4.7 3.6 %collective-permute-start.1 = (f32[296,128]{1,0:T(8,128)S(1)}, f32[296,128]{1,0:T(8,128)S(1)}, u32[]{:S(2)}, u32[]{:S(2)}) collective-permute-start(f32[296,128]{1,0:T(8,128)S(1)} %get-tuple-element.26), channel_id=1, source_target_pairs={{0,1},{1,0},{2,3},{3,2},{4,5},{5,4},{6,7},{7,6},{8,9},{9,8},{10,11... | collective-permute-start | bytes 454664 | tf_op jit(solution)/shard_map/ppermute | solution.py:376
  8.3 1.0 %collective-permute-done.z_in = f32[296,128]{1,0:T(8,128)S(1)} collective-permute-done((f32[296,128]{1,0:T(8,128)S(1)}, f32[296,128]{1,0:T(8,128)S(1)}, u32[]{:S(2)}, u32[]{:S(2)}) %collective-permute-start) | collective-permute-done | bytes 151584 | tf_op jit(solution)/shard_map/ppermute | solution.py:376
  9.2 0.0 collective-permute-done.1.a_in
  9.2 0.4 shard_map.104
  9.6 20.9 %collective-permute-start.2 = (f32[248,128]{1,0:T(8,128)S(1)}, f32[248,128]{1,0:T(8,128)S(1)}, u32[]{:S(2)}, u32[]{:S(2)}) collective-permute-start(f32[248,128]{1,0:T(8,128)S(1)} %get-tuple-element.31), channel_id=1, source_target_pairs={{8,16},{16,8},{24,32},{32,24},{40,48},{48,40},{56,64},{64,56},{72,... | collective-permute-start | bytes 380936 | tf_op jit(solution)/shard_map/ppermute | solution.py:376
  30.5 1.9 %collective-permute-start.3 = (f32[248,128]{1,0:T(8,128)S(1)}, f32[248,128]{1,0:T(8,128)S(1)}, u32[]{:S(2)}, u32[]{:S(2)}) collective-permute-start(f32[248,128]{1,0:T(8,128)S(1)} %get-tuple-element.32), channel_id=1, source_target_pairs={{0,8},{8,0},{16,24},{24,16},{32,40},{40,32},{48,56},{56,48},{64,72... | collective-permute-start | bytes 380936 | tf_op jit(solution)/shard_map/ppermute | solution.py:376
  32.5 2.0 %collective-permute-done.2.z_in = f32[248,128]{1,0:T(8,128)S(1)} collective-permute-done((f32[248,128]{1,0:T(8,128)S(1)}, f32[248,128]{1,0:T(8,128)S(1)}, u32[]{:S(2)}, u32[]{:S(2)}) %collective-permute-start.2) | collective-permute-done | bytes 127008 | tf_op jit(solution)/shard_map/ppermute | solution.py:376
  34.4 3.4 %collective-permute-done.3.a_in = f32[248,128]{1,0:T(8,128)S(1)} collective-permute-done((f32[248,128]{1,0:T(8,128)S(1)}, f32[248,128]{1,0:T(8,128)S(1)}, u32[]{:S(2)}, u32[]{:S(2)}) %collective-permute-start.3) | collective-permute-done | bytes 127008 | tf_op jit(solution)/shard_map/ppermute | solution.py:376
  37.8 0.8 %shard_map.105 = (f32[72,128]{1,0:T(8,128)S(1)}, f32[384,128]{1,0:T(8,128)S(1)}, f32[384,128]{1,0:T(8,128)S(1)}) custom-call(f32[384,128]{1,0:T(8,128)S(1)} %get-tuple-element.21.u_ref, f32[384,128]{1,0:T(8,128)S(1)} %get-tuple-element.22.v_ref, f32[384,128]{1,0:T(8,128)S(1)} %get-tuple-element.23.b_ref, f32[384,128]{1,0:T(8,128)S(1)} %get-tuple-element.27.hu_ref, ...), custom_call_target="tpu_custom_call" | custom-call | tf_op jit(solution)/shard_map/pallas_call | solution.py:360
  38.6 3.6 %collective-permute-start.4 = (f32[72,128]{1,0:T(8,128)S(1)}, f32[72,128]{1,0:T(8,128)S(1)}, u32[]{:S(2)}, u32[]{:S(2)}) collective-permute-start(f32[72,128]{1,0:T(8,128)S(1)} %get-tuple-element.33), channel_id=1, source_target_pairs={{8,16},{16,8},{24,32},{32,24},{40,48},{48,40},{56,64},{64,56},{72,... | collective-permute-start | bytes 110600 | tf_op jit(solution)/shard_map/ppermute | solution.py:376
  42.2 1.9 %collective-permute-start.5 = (f32[72,128]{1,0:T(8,128)S(1)}, f32[72,128]{1,0:T(8,128)S(1)}, u32[]{:S(2)}, u32[]{:S(2)}) collective-permute-start(f32[72,128]{1,0:T(8,128)S(1)} %get-tuple-element.33), channel_id=1, source_target_pairs={{0,8},{8,0},{16,24},{24,16},{32,40},{40,32},{48,56},{56,48},{64,72... | collective-permute-start | bytes 110600 | tf_op jit(solution)/shard_map/ppermute | solution.py:376
  44.1 3.6 %collective-permute-done.4 = f32[72,128]{1,0:T(8,128)S(1)} collective-permute-done((f32[72,128]{1,0:T(8,128)S(1)}, f32[72,128]{1,0:T(8,128)S(1)}, u32[]{:S(2)}, u32[]{:S(2)}) %collective-permute-start.4) | collective-permute-done | bytes 36896 | tf_op jit(solution)/shard_map/ppermute | solution.py:376
  47.8 0.3 collective-permute-done.5
  48.1 3.3 %collective-permute-start.7 = (f32[216,128]{1,0:T(8,128)S(1)}, f32[216,128]{1,0:T(8,128)S(1)}, u32[]{:S(2)}, u32[]{:S(2)}) collective-permute-start(f32[216,128]{1,0:T(8,128)S(1)} %constant_dynamic-update-slice_fusion.y_ref), channel_id=1, source_target_pairs={{8,32},{32,8},{24,48},{48,24},{40,64},{64,40},{56,80},{80,56},{72,... | collective-permute-start | bytes 331784 | tf_op jit(solution)/shard_map/ppermute | solution.py:376
  51.4 1.9 %collective-permute-start.6 = (f32[216,128]{1,0:T(8,128)S(1)}, f32[216,128]{1,0:T(8,128)S(1)}, u32[]{:S(2)}, u32[]{:S(2)}) collective-permute-start(f32[216,128]{1,0:T(8,128)S(1)} %constant_dynamic-update-slice_fusion.y_ref), channel_id=1, source_target_pairs={{0,24},{24,0},{16,40},{40,16},{32,56},{56,32},{48,72},{72,48},{64,... | collective-permute-start | bytes 331784 | tf_op jit(solution)/shard_map/ppermute | solution.py:376
  53.3 9.9 %collective-permute-done.7.z_in = f32[216,128]{1,0:T(8,128)S(1)} collective-permute-done((f32[216,128]{1,0:T(8,128)S(1)}, f32[216,128]{1,0:T(8,128)S(1)}, u32[]{:S(2)}, u32[]{:S(2)}) %collective-permute-start.7) | collective-permute-done | bytes 110624 | tf_op jit(solution)/shard_map/ppermute | solution.py:376
  63.2 0.0 collective-permute-done.6.a_in
  63.2 4.8 %shard_map.106 = (f32[384,128]{1,0:T(8,128)}, f32[384,128]{1,0:T(8,128)}, f32[8,128]{1,0:T(8,128)}) custom-call(f32[216,128]{1,0:T(8,128)S(1)} %constant_dynamic-update-slice_fusion.y_ref, f32[216,128]{1,0:T(8,128)S(1)} %collective-permute-done.6.a_in, f32[216,128]{1,0:T(8,128)S(1)} %collective-permute-done.7.z_in, f32[384,128]{1,0:T(8,128)S(1)} %get-tuple-element.34.su_ref, ...), custom_call_target="tpu_custom_call" | custom-call | tf_op jit(solution)/shard_map/pallas_call | solution.py:360
  (3 shorter events, 0.0 us)
Async XLA Ops:
  2.7 6.5 %collective-permute-start = (f32[296,128]{1,0:T(8,128)S(1)}, f32[296,128]{1,0:T(8,128)S(1)}, u32[]{:S(2)}, u32[]{:S(2)}) collective-permute-start(f32[296,128]{1,0:T(8,128)S(1)} %get-tuple-element.25), channel_id=1, source_target_pairs={{1,2},{2,1},{3,4},{4,3},{5,6},{6,5},{9,10},{10,9},{11,12},{12,11},... | collective-permute-start | bytes 454664 | tf_op jit(solution)/shard_map/ppermute | solution.py:376
  4.7 4.6 %collective-permute-start.1 = (f32[296,128]{1,0:T(8,128)S(1)}, f32[296,128]{1,0:T(8,128)S(1)}, u32[]{:S(2)}, u32[]{:S(2)}) collective-permute-start(f32[296,128]{1,0:T(8,128)S(1)} %get-tuple-element.26), channel_id=1, source_target_pairs={{0,1},{1,0},{2,3},{3,2},{4,5},{5,4},{6,7},{7,6},{8,9},{9,8},{10,11... | collective-permute-start | bytes 454664 | tf_op jit(solution)/shard_map/ppermute | solution.py:376
  9.6 24.8 %collective-permute-start.2 = (f32[248,128]{1,0:T(8,128)S(1)}, f32[248,128]{1,0:T(8,128)S(1)}, u32[]{:S(2)}, u32[]{:S(2)}) collective-permute-start(f32[248,128]{1,0:T(8,128)S(1)} %get-tuple-element.31), channel_id=1, source_target_pairs={{8,16},{16,8},{24,32},{32,24},{40,48},{48,40},{56,64},{64,56},{72,... | collective-permute-start | bytes 380936 | tf_op jit(solution)/shard_map/ppermute | solution.py:376
  30.5 7.3 %collective-permute-start.3 = (f32[248,128]{1,0:T(8,128)S(1)}, f32[248,128]{1,0:T(8,128)S(1)}, u32[]{:S(2)}, u32[]{:S(2)}) collective-permute-start(f32[248,128]{1,0:T(8,128)S(1)} %get-tuple-element.32), channel_id=1, source_target_pairs={{0,8},{8,0},{16,24},{24,16},{32,40},{40,32},{48,56},{56,48},{64,72... | collective-permute-start | bytes 380936 | tf_op jit(solution)/shard_map/ppermute | solution.py:376
  38.6 9.2 %collective-permute-start.4 = (f32[72,128]{1,0:T(8,128)S(1)}, f32[72,128]{1,0:T(8,128)S(1)}, u32[]{:S(2)}, u32[]{:S(2)}) collective-permute-start(f32[72,128]{1,0:T(8,128)S(1)} %get-tuple-element.33), channel_id=1, source_target_pairs={{8,16},{16,8},{24,32},{32,24},{40,48},{48,40},{56,64},{64,56},{72,... | collective-permute-start | bytes 110600 | tf_op jit(solution)/shard_map/ppermute | solution.py:376
  42.2 5.9 %collective-permute-start.5 = (f32[72,128]{1,0:T(8,128)S(1)}, f32[72,128]{1,0:T(8,128)S(1)}, u32[]{:S(2)}, u32[]{:S(2)}) collective-permute-start(f32[72,128]{1,0:T(8,128)S(1)} %get-tuple-element.33), channel_id=1, source_target_pairs={{0,8},{8,0},{16,24},{24,16},{32,40},{40,32},{48,56},{56,48},{64,72... | collective-permute-start | bytes 110600 | tf_op jit(solution)/shard_map/ppermute | solution.py:376
  48.1 15.2 %collective-permute-start.7 = (f32[216,128]{1,0:T(8,128)S(1)}, f32[216,128]{1,0:T(8,128)S(1)}, u32[]{:S(2)}, u32[]{:S(2)}) collective-permute-start(f32[216,128]{1,0:T(8,128)S(1)} %constant_dynamic-update-slice_fusion.y_ref), channel_id=1, source_target_pairs={{8,32},{32,8},{24,48},{48,24},{40,64},{64,40},{56,80},{80,56},{72,... | collective-permute-start | bytes 331784 | tf_op jit(solution)/shard_map/ppermute | solution.py:376
  51.4 11.8 %collective-permute-start.6 = (f32[216,128]{1,0:T(8,128)S(1)}, f32[216,128]{1,0:T(8,128)S(1)}, u32[]{:S(2)}, u32[]{:S(2)}) collective-permute-start(f32[216,128]{1,0:T(8,128)S(1)} %constant_dynamic-update-slice_fusion.y_ref), channel_id=1, source_target_pairs={{0,24},{24,0},{16,40},{40,16},{32,56},{56,32},{48,72},{72,48},{64,... | collective-permute-start | bytes 331784 | tf_op jit(solution)/shard_map/ppermute | solution.py:376

commit v3 on v2

--- a/solution.py
+++ b/solution.py
@@ -233,7 +233,7 @@
 
 
 def substeps_kernel(
-    y_ref, a_in, z_in, su_ref, sv_ref, out_u, out_v, out_eta,
+    y_ref, z_in, a_in, su_ref, sv_ref, out_u, out_v, out_eta,
     eta_ref, u_ref, v_ref, w_ref, fu_ref, fv_ref, du_ref, dv_ref, cu_ref, cv_ref, tw_ref, q_ref, t_ref,
     eta_north_ref, u_north_ref, tw_north_ref,
 ):
@@ -247,9 +247,9 @@
         return pl.ds(COLS * (p + 1) + shift, COLS)
 
     places = (
-        ((z_in, 2), (a_in, 0)), ((z_in, 1), (a_in, 1)), ((z_in, 0), (a_in, 2)),
-        ((y_ref, 0), (y_ref, 2)), ((y_ref, 1), (y_ref, 1)), ((y_ref, 2), (y_ref, 0)),
-        ((a_in, 2), (z_in, 0)), ((a_in, 1), (z_in, 1)), ((a_in, 0), (z_in, 2)),
+        ((z_in, 2), (a_in, 0)), ((y_ref, 0), (y_ref, 2)), ((a_in, 2), (z_in, 0)),
+        ((z_in, 1), (a_in, 1)), ((y_ref, 1), (y_ref, 1)), ((a_in, 1), (z_in, 1)),
+        ((z_in, 0), (a_in, 2)), ((y_ref, 2), (y_ref, 0)), ((a_in, 0), (z_in, 2)),
     )
     for p, (for_even, for_odd) in enumerate(places):
         def tile(i):
@@ -403,14 +403,14 @@
         levels_kernel, [(FIELDS, LANES), flat, flat], [both, both],
         u, v, b, hu, hv, hb, hp, planes, cols_z, cols_a,
     )
-    near_z = swap(x, "lon", 1, 1, True)
-    near_a = swap(x, "lon", 0, 1, True)
-    y = jnp.concatenate([near_z, x, near_a], 0)
-    far_z = swap(y, "lon", 1, 3, True)
-    far_a = swap(y, "lon", 0, 3, True)
+    far_z = swap(x, "lon", 1, 3, True)
+    far_a = swap(x, "lon", 0, 3, True)
+    y = jnp.concatenate([far_z, x, far_a], 0)
+    near_z = swap(y, "lon", 1, 1, True)
+    near_a = swap(y, "lon", 0, 1, True)
     state = (2, (2 * REACH + 3) * COLS, LANES)
     new_u, new_v, surface = call(
-        substeps_kernel, [flat, flat, (COLS, LANES)], [state] * 16, y, far_a, far_z, star_u, star_v
+        substeps_kernel, [flat, flat, (COLS, LANES)], [state] * 16, y, near_z, near_a, star_u, star_v
     )
     return new_u.reshape(velocity_u.shape), new_v.reshape(velocity_v.shape), surface
 

time: 68.4 us -> 69.2 us (1.012)
  starting transfers between devices: 39.1 us -> 44.7 us
  waiting for transfers between devices: 20.2 us -> 15.3 us
    ppermute x8, starting transfers between devices: 39.1 us -> 44.7 us  [swap(): return lax.ppermute(x, axis, pairs)]
    ppermute x8, waiting for transfers between devices: 20.2 us -> 15.3 us  [swap(): return lax.ppermute(x, axis, pairs)]
where the time goes in v3:
time: 69.2 us; the launch traced here: 68.9 us
  starting transfers between devices  44.7 us (65%)
  waiting for transfers between devices  15.3 us (22%)
  Pallas kernels  8.11 us (12%)
  between operations  0.73 us (1%)
    ppermute x8, starting transfers between devices, swap(): return lax.ppermute(x, axis, pairs)  44.7 us
    ppermute x8, waiting for transfers between devices, swap(): return lax.ppermute(x, axis, pairs)  15.3 us
    pallas_call x4, Pallas kernels, call(): pl.pallas_call(kernel, out_shape=[jax.ShapeDtypeStruct(s, jnp.float32) fo...  8.11 us
  transfers between devices with their start and end apart: 8, of which 6 were waited for; matrix products, arithmetic and copies ran while one was open for 0% of the time, Pallas kernels for 0%

profile of v3, /device:TPU:8, one launch (start us, length us, event | category | flops | bytes accessed | tf_op | source)
XLA Modules:
  0.0 68.9 jit_solution(13770308691505467168)
XLA Ops:
  0.6 2.1 %shard_map.103 = (f32[296,128]{1,0:T(8,128)S(1)}, f32[296,128]{1,0:T(8,128)S(1)}, f32[384,128]{1,0:T(8,128)S(1)}, f32[384,128]{1,0:T(8,128)S(1)}, f32[384,128]{1,0:T(8,128)S(1)}, /*index=5*/f32[32,128]{1,0:T(8,128)S(1)}) custom-call(f32[384,128]{1,0:T(8,128)} %bitcast.5, f32[384,128]{1,0:T(8,128)} %bitcast.6, f32[384,128]{1,0:T(8,128)} %bitcast.7, ...), custom_call_target="tpu_custom_call" | custom-call | tf_op jit(solution)/shard_map/pallas_call | solution.py:360
  2.7 1.9 %collective-permute-start = (f32[296,128]{1,0:T(8,128)S(1)}, f32[296,128]{1,0:T(8,128)S(1)}, u32[]{:S(2)}, u32[]{:S(2)}) collective-permute-start(f32[296,128]{1,0:T(8,128)S(1)} %get-tuple-element.25), channel_id=1, source_target_pairs={{1,2},{2,1},{3,4},{4,3},{5,6},{6,5},{9,10},{10,9},{11,12},{12,11},... | collective-permute-start | bytes 454664 | tf_op jit(solution)/shard_map/ppermute | solution.py:376
  4.7 3.6 %collective-permute-start.1 = (f32[296,128]{1,0:T(8,128)S(1)}, f32[296,128]{1,0:T(8,128)S(1)}, u32[]{:S(2)}, u32[]{:S(2)}) collective-permute-start(f32[296,128]{1,0:T(8,128)S(1)} %get-tuple-element.26), channel_id=1, source_target_pairs={{0,1},{1,0},{2,3},{3,2},{4,5},{5,4},{6,7},{7,6},{8,9},{9,8},{10,11... | collective-permute-start | bytes 454664 | tf_op jit(solution)/shard_map/ppermute | solution.py:376
  8.3 1.0 %collective-permute-done.z_in = f32[296,128]{1,0:T(8,128)S(1)} collective-permute-done((f32[296,128]{1,0:T(8,128)S(1)}, f32[296,128]{1,0:T(8,128)S(1)}, u32[]{:S(2)}, u32[]{:S(2)}) %collective-permute-start) | collective-permute-done | bytes 151584 | tf_op jit(solution)/shard_map/ppermute | solution.py:376
  9.2 0.0 collective-permute-done.1.a_in
  9.2 0.4 shard_map.104
  9.6 20.9 %collective-permute-start.2 = (f32[248,128]{1,0:T(8,128)S(1)}, f32[248,128]{1,0:T(8,128)S(1)}, u32[]{:S(2)}, u32[]{:S(2)}) collective-permute-start(f32[248,128]{1,0:T(8,128)S(1)} %get-tuple-element.31), channel_id=1, source_target_pairs={{8,16},{16,8},{24,32},{32,24},{40,48},{48,40},{56,64},{64,56},{72,... | collective-permute-start | bytes 380936 | tf_op jit(solution)/shard_map/ppermute | solution.py:376
  30.5 1.9 %collective-permute-start.3 = (f32[248,128]{1,0:T(8,128)S(1)}, f32[248,128]{1,0:T(8,128)S(1)}, u32[]{:S(2)}, u32[]{:S(2)}) collective-permute-start(f32[248,128]{1,0:T(8,128)S(1)} %get-tuple-element.32), channel_id=1, source_target_pairs={{0,8},{8,0},{16,24},{24,16},{32,40},{40,32},{48,56},{56,48},{64,72... | collective-permute-start | bytes 380936 | tf_op jit(solution)/shard_map/ppermute | solution.py:376
  32.5 2.0 %collective-permute-done.2.z_in = f32[248,128]{1,0:T(8,128)S(1)} collective-permute-done((f32[248,128]{1,0:T(8,128)S(1)}, f32[248,128]{1,0:T(8,128)S(1)}, u32[]{:S(2)}, u32[]{:S(2)}) %collective-permute-start.2) | collective-permute-done | bytes 127008 | tf_op jit(solution)/shard_map/ppermute | solution.py:376
  34.4 3.4 %collective-permute-done.3.a_in = f32[248,128]{1,0:T(8,128)S(1)} collective-permute-done((f32[248,128]{1,0:T(8,128)S(1)}, f32[248,128]{1,0:T(8,128)S(1)}, u32[]{:S(2)}, u32[]{:S(2)}) %collective-permute-start.3) | collective-permute-done | bytes 127008 | tf_op jit(solution)/shard_map/ppermute | solution.py:376
  37.8 0.8 %shard_map.105 = (f32[72,128]{1,0:T(8,128)S(1)}, f32[384,128]{1,0:T(8,128)S(1)}, f32[384,128]{1,0:T(8,128)S(1)}) custom-call(f32[384,128]{1,0:T(8,128)S(1)} %get-tuple-element.21.u_ref, f32[384,128]{1,0:T(8,128)S(1)} %get-tuple-element.22.v_ref, f32[384,128]{1,0:T(8,128)S(1)} %get-tuple-element.23.b_ref, f32[384,128]{1,0:T(8,128)S(1)} %get-tuple-element.27.hu_ref, ...), custom_call_target="tpu_custom_call" | custom-call | tf_op jit(solution)/shard_map/pallas_call | solution.py:360
  38.6 4.3 %collective-permute-start.4 = (f32[72,128]{1,0:T(8,128)S(1)}, f32[72,128]{1,0:T(8,128)S(1)}, u32[]{:S(2)}, u32[]{:S(2)}) collective-permute-start(f32[72,128]{1,0:T(8,128)S(1)} %get-tuple-element.33), channel_id=1, source_target_pairs={{8,32},{32,8},{24,48},{48,24},{40,64},{64,40},{56,80},{80,56},{72,... | collective-permute-start | bytes 110600 | tf_op jit(solution)/shard_map/ppermute | solution.py:376
  42.9 1.9 %collective-permute-start.5 = (f32[72,128]{1,0:T(8,128)S(1)}, f32[72,128]{1,0:T(8,128)S(1)}, u32[]{:S(2)}, u32[]{:S(2)}) collective-permute-start(f32[72,128]{1,0:T(8,128)S(1)} %get-tuple-element.33), channel_id=1, source_target_pairs={{0,24},{24,0},{16,40},{40,16},{32,56},{56,32},{48,72},{72,48},{64,... | collective-permute-start | bytes 110600 | tf_op jit(solution)/shard_map/ppermute | solution.py:376
  44.8 4.7 %collective-permute-done.4 = f32[72,128]{1,0:T(8,128)S(1)} collective-permute-done((f32[72,128]{1,0:T(8,128)S(1)}, f32[72,128]{1,0:T(8,128)S(1)}, u32[]{:S(2)}, u32[]{:S(2)}) %collective-permute-start.4) | collective-permute-done | bytes 36896 | tf_op jit(solution)/shard_map/ppermute | solution.py:376
  49.6 1.1 %collective-permute-done.5 = f32[72,128]{1,0:T(8,128)S(1)} collective-permute-done((f32[72,128]{1,0:T(8,128)S(1)}, f32[72,128]{1,0:T(8,128)S(1)}, u32[]{:S(2)}, u32[]{:S(2)}) %collective-permute-start.5) | collective-permute-done | bytes 36896 | tf_op jit(solution)/shard_map/ppermute | solution.py:376
  50.7 3.4 %collective-permute-start.7 = (f32[216,128]{1,0:T(8,128)S(1)}, f32[216,128]{1,0:T(8,128)S(1)}, u32[]{:S(2)}, u32[]{:S(2)}) collective-permute-start(f32[216,128]{1,0:T(8,128)S(1)} %constant_dynamic-update-slice_fusion.y_ref), channel_id=1, source_target_pairs={{0,8},{8,0},{16,24},{24,16},{32,40},{40,32},{48,56},{56,48},{64,72... | collective-permute-start | bytes 331784 | tf_op jit(solution)/shard_map/ppermute | solution.py:376
  54.1 6.8 %collective-permute-start.6 = (f32[216,128]{1,0:T(8,128)S(1)}, f32[216,128]{1,0:T(8,128)S(1)}, u32[]{:S(2)}, u32[]{:S(2)}) collective-permute-start(f32[216,128]{1,0:T(8,128)S(1)} %constant_dynamic-update-slice_fusion.y_ref), channel_id=1, source_target_pairs={{8,16},{16,8},{24,32},{32,24},{40,48},{48,40},{56,64},{64,56},{72,... | collective-permute-start | bytes 331784 | tf_op jit(solution)/shard_map/ppermute | solution.py:376
  60.8 0.0 collective-permute-done.7.a_in
  60.9 3.2 %collective-permute-done.6.z_in = f32[216,128]{1,0:T(8,128)S(1)} collective-permute-done((f32[216,128]{1,0:T(8,128)S(1)}, f32[216,128]{1,0:T(8,128)S(1)}, u32[]{:S(2)}, u32[]{:S(2)}) %collective-permute-start.6) | collective-permute-done | bytes 110624 | tf_op jit(solution)/shard_map/ppermute | solution.py:376
  64.0 4.8 %shard_map.106 = (f32[384,128]{1,0:T(8,128)}, f32[384,128]{1,0:T(8,128)}, f32[8,128]{1,0:T(8,128)}) custom-call(f32[216,128]{1,0:T(8,128)S(1)} %constant_dynamic-update-slice_fusion.y_ref, f32[216,128]{1,0:T(8,128)S(1)} %collective-permute-done.6.z_in, f32[216,128]{1,0:T(8,128)S(1)} %collective-permute-done.7.a_in, f32[384,128]{1,0:T(8,128)S(1)} %get-tuple-element.34.su_ref, ...), custom_call_target="tpu_custom_call" | custom-call | tf_op jit(solution)/shard_map/pallas_call | solution.py:360
  (3 shorter events, 0.0 us)
Async XLA Ops:
  2.7 6.5 %collective-permute-start = (f32[296,128]{1,0:T(8,128)S(1)}, f32[296,128]{1,0:T(8,128)S(1)}, u32[]{:S(2)}, u32[]{:S(2)}) collective-permute-start(f32[296,128]{1,0:T(8,128)S(1)} %get-tuple-element.25), channel_id=1, source_target_pairs={{1,2},{2,1},{3,4},{4,3},{5,6},{6,5},{9,10},{10,9},{11,12},{12,11},... | collective-permute-start | bytes 454664 | tf_op jit(solution)/shard_map/ppermute | solution.py:376
  4.7 4.6 %collective-permute-start.1 = (f32[296,128]{1,0:T(8,128)S(1)}, f32[296,128]{1,0:T(8,128)S(1)}, u32[]{:S(2)}, u32[]{:S(2)}) collective-permute-start(f32[296,128]{1,0:T(8,128)S(1)} %get-tuple-element.26), channel_id=1, source_target_pairs={{0,1},{1,0},{2,3},{3,2},{4,5},{5,4},{6,7},{7,6},{8,9},{9,8},{10,11... | collective-permute-start | bytes 454664 | tf_op jit(solution)/shard_map/ppermute | solution.py:376
  9.6 24.8 %collective-permute-start.2 = (f32[248,128]{1,0:T(8,128)S(1)}, f32[248,128]{1,0:T(8,128)S(1)}, u32[]{:S(2)}, u32[]{:S(2)}) collective-permute-start(f32[248,128]{1,0:T(8,128)S(1)} %get-tuple-element.31), channel_id=1, source_target_pairs={{8,16},{16,8},{24,32},{32,24},{40,48},{48,40},{56,64},{64,56},{72,... | collective-permute-start | bytes 380936 | tf_op jit(solution)/shard_map/ppermute | solution.py:376
  30.5 7.3 %collective-permute-start.3 = (f32[248,128]{1,0:T(8,128)S(1)}, f32[248,128]{1,0:T(8,128)S(1)}, u32[]{:S(2)}, u32[]{:S(2)}) collective-permute-start(f32[248,128]{1,0:T(8,128)S(1)} %get-tuple-element.32), channel_id=1, source_target_pairs={{0,8},{8,0},{16,24},{24,16},{32,40},{40,32},{48,56},{56,48},{64,72... | collective-permute-start | bytes 380936 | tf_op jit(solution)/shard_map/ppermute | solution.py:376
  38.6 11.0 %collective-permute-start.4 = (f32[72,128]{1,0:T(8,128)S(1)}, f32[72,128]{1,0:T(8,128)S(1)}, u32[]{:S(2)}, u32[]{:S(2)}) collective-permute-start(f32[72,128]{1,0:T(8,128)S(1)} %get-tuple-element.33), channel_id=1, source_target_pairs={{8,32},{32,8},{24,48},{48,24},{40,64},{64,40},{56,80},{80,56},{72,... | collective-permute-start | bytes 110600 | tf_op jit(solution)/shard_map/ppermute | solution.py:376
  42.9 7.8 %collective-permute-start.5 = (f32[72,128]{1,0:T(8,128)S(1)}, f32[72,128]{1,0:T(8,128)S(1)}, u32[]{:S(2)}, u32[]{:S(2)}) collective-permute-start(f32[72,128]{1,0:T(8,128)S(1)} %get-tuple-element.33), channel_id=1, source_target_pairs={{0,24},{24,0},{16,40},{40,16},{32,56},{56,32},{48,72},{72,48},{64,... | collective-permute-start | bytes 110600 | tf_op jit(solution)/shard_map/ppermute | solution.py:376
  50.7 10.2 %collective-permute-start.7 = (f32[216,128]{1,0:T(8,128)S(1)}, f32[216,128]{1,0:T(8,128)S(1)}, u32[]{:S(2)}, u32[]{:S(2)}) collective-permute-start(f32[216,128]{1,0:T(8,128)S(1)} %constant_dynamic-update-slice_fusion.y_ref), channel_id=1, source_target_pairs={{0,8},{8,0},{16,24},{24,16},{32,40},{40,32},{48,56},{56,48},{64,72... | collective-permute-start | bytes 331784 | tf_op jit(solution)/shard_map/ppermute | solution.py:376
  54.1 10.0 %collective-permute-start.6 = (f32[216,128]{1,0:T(8,128)S(1)}, f32[216,128]{1,0:T(8,128)S(1)}, u32[]{:S(2)}, u32[]{:S(2)}) collective-permute-start(f32[216,128]{1,0:T(8,128)S(1)} %constant_dynamic-update-slice_fusion.y_ref), channel_id=1, source_target_pairs={{8,16},{16,8},{24,32},{32,24},{40,48},{48,40},{56,64},{64,56},{72,... | collective-permute-start | bytes 331784 | tf_op jit(solution)/shard_map/ppermute | solution.py:376

commit v4 on v3

--- a/solution.py
+++ b/solution.py
@@ -233,7 +233,7 @@
 
 
 def substeps_kernel(
-    y_ref, z_in, a_in, su_ref, sv_ref, out_u, out_v, out_eta,
+    y_ref, a_in, z_in, su_ref, sv_ref, out_u, out_v, out_eta,
     eta_ref, u_ref, v_ref, w_ref, fu_ref, fv_ref, du_ref, dv_ref, cu_ref, cv_ref, tw_ref, q_ref, t_ref,
     eta_north_ref, u_north_ref, tw_north_ref,
 ):
@@ -410,7 +410,7 @@
     near_a = swap(y, "lon", 0, 1, True)
     state = (2, (2 * REACH + 3) * COLS, LANES)
     new_u, new_v, surface = call(
-        substeps_kernel, [flat, flat, (COLS, LANES)], [state] * 16, y, near_z, near_a, star_u, star_v
+        substeps_kernel, [flat, flat, (COLS, LANES)], [state] * 16, y, near_a, near_z, star_u, star_v
     )
     return new_u.reshape(velocity_u.shape), new_v.reshape(velocity_v.shape), surface
 

time: 69.2 us -> 65.9 us (0.952)
  the two profiles are of different devices: /device:TPU:8 before, /device:TPU:40 now
where the time goes in v4:
time: 65.9 us; the launch traced here: 65.5 us
  starting transfers between devices  43.6 us (66%)
  waiting for transfers between devices  13 us (20%)
  Pallas kernels  8.11 us (12%)
  between operations  0.75 us (1%)
    ppermute x8, starting transfers between devices, swap(): return lax.ppermute(x, axis, pairs)  43.6 us
    ppermute x8, waiting for transfers between devices, swap(): return lax.ppermute(x, axis, pairs)  13 us
    pallas_call x4, Pallas kernels, call(): pl.pallas_call(kernel, out_shape=[jax.ShapeDtypeStruct(s, jnp.float32) fo...  8.11 us
  transfers between devices with their start and end apart: 8, of which 5 were waited for; matrix products, arithmetic and copies ran while one was open for 0% of the time, Pallas kernels for 0%

profile of v4, /device:TPU:40, one launch (start us, length us, event | category | flops | bytes accessed | tf_op | source)
XLA Modules:
  0.0 65.5 jit_solution(4385458327767110292)
XLA Ops:
  0.6 2.1 %shard_map.103 = (f32[296,128]{1,0:T(8,128)S(1)}, f32[296,128]{1,0:T(8,128)S(1)}, f32[384,128]{1,0:T(8,128)S(1)}, f32[384,128]{1,0:T(8,128)S(1)}, f32[384,128]{1,0:T(8,128)S(1)}, /*index=5*/f32[32,128]{1,0:T(8,128)S(1)}) custom-call(f32[384,128]{1,0:T(8,128)} %bitcast.5, f32[384,128]{1,0:T(8,128)} %bitcast.6, f32[384,128]{1,0:T(8,128)} %bitcast.7, ...), custom_call_target="tpu_custom_call" | custom-call | tf_op jit(solution)/shard_map/pallas_call | solution.py:360
  2.7 1.9 %collective-permute-start = (f32[296,128]{1,0:T(8,128)S(1)}, f32[296,128]{1,0:T(8,128)S(1)}, u32[]{:S(2)}, u32[]{:S(2)}) collective-permute-start(f32[296,128]{1,0:T(8,128)S(1)} %get-tuple-element.25), channel_id=1, source_target_pairs={{1,2},{2,1},{3,4},{4,3},{5,6},{6,5},{9,10},{10,9},{11,12},{12,11},... | collective-permute-start | bytes 454664 | tf_op jit(solution)/shard_map/ppermute | solution.py:376
  4.7 3.6 %collective-permute-start.1 = (f32[296,128]{1,0:T(8,128)S(1)}, f32[296,128]{1,0:T(8,128)S(1)}, u32[]{:S(2)}, u32[]{:S(2)}) collective-permute-start(f32[296,128]{1,0:T(8,128)S(1)} %get-tuple-element.26), channel_id=1, source_target_pairs={{0,1},{1,0},{2,3},{3,2},{4,5},{5,4},{6,7},{7,6},{8,9},{9,8},{10,11... | collective-permute-start | bytes 454664 | tf_op jit(solution)/shard_map/ppermute | solution.py:376
  8.3 1.0 %collective-permute-done.z_in = f32[296,128]{1,0:T(8,128)S(1)} collective-permute-done((f32[296,128]{1,0:T(8,128)S(1)}, f32[296,128]{1,0:T(8,128)S(1)}, u32[]{:S(2)}, u32[]{:S(2)}) %collective-permute-start) | collective-permute-done | bytes 151584 | tf_op jit(solution)/shard_map/ppermute | solution.py:376
  9.2 0.0 collective-permute-done.1.a_in
  9.2 0.4 shard_map.104
  9.6 3.8 %collective-permute-start.2 = (f32[248,128]{1,0:T(8,128)S(1)}, f32[248,128]{1,0:T(8,128)S(1)}, u32[]{:S(2)}, u32[]{:S(2)}) collective-permute-start(f32[248,128]{1,0:T(8,128)S(1)} %get-tuple-element.31), channel_id=1, source_target_pairs={{8,16},{16,8},{24,32},{32,24},{40,48},{48,40},{56,64},{64,56},{72,... | collective-permute-start | bytes 380936 | tf_op jit(solution)/shard_map/ppermute | solution.py:376
  13.5 19.1 %collective-permute-start.3 = (f32[248,128]{1,0:T(8,128)S(1)}, f32[248,128]{1,0:T(8,128)S(1)}, u32[]{:S(2)}, u32[]{:S(2)}) collective-permute-start(f32[248,128]{1,0:T(8,128)S(1)} %get-tuple-element.32), channel_id=1, source_target_pairs={{0,8},{8,0},{16,24},{24,16},{32,40},{40,32},{48,56},{56,48},{64,72... | collective-permute-start | bytes 380936 | tf_op jit(solution)/shard_map/ppermute | solution.py:376
  32.6 0.0 collective-permute-done.2.z_in
  32.6 3.6 %collective-permute-done.3.a_in = f32[248,128]{1,0:T(8,128)S(1)} collective-permute-done((f32[248,128]{1,0:T(8,128)S(1)}, f32[248,128]{1,0:T(8,128)S(1)}, u32[]{:S(2)}, u32[]{:S(2)}) %collective-permute-start.3) | collective-permute-done | bytes 127008 | tf_op jit(solution)/shard_map/ppermute | solution.py:376
  36.2 0.8 %shard_map.105 = (f32[72,128]{1,0:T(8,128)S(1)}, f32[384,128]{1,0:T(8,128)S(1)}, f32[384,128]{1,0:T(8,128)S(1)}) custom-call(f32[384,128]{1,0:T(8,128)S(1)} %get-tuple-element.21.u_ref, f32[384,128]{1,0:T(8,128)S(1)} %get-tuple-element.22.v_ref, f32[384,128]{1,0:T(8,128)S(1)} %get-tuple-element.23.b_ref, f32[384,128]{1,0:T(8,128)S(1)} %get-tuple-element.27.hu_ref, ...), custom_call_target="tpu_custom_call" | custom-call | tf_op jit(solution)/shard_map/pallas_call | solution.py:360
  37.0 1.9 %collective-permute-start.4 = (f32[72,128]{1,0:T(8,128)S(1)}, f32[72,128]{1,0:T(8,128)S(1)}, u32[]{:S(2)}, u32[]{:S(2)}) collective-permute-start(f32[72,128]{1,0:T(8,128)S(1)} %get-tuple-element.33), channel_id=1, source_target_pairs={{8,32},{32,8},{24,48},{48,24},{40,64},{64,40},{56,80},{80,56},{72,... | collective-permute-start | bytes 110600 | tf_op jit(solution)/shard_map/ppermute | solution.py:376
  38.9 7.6 %collective-permute-start.5 = (f32[72,128]{1,0:T(8,128)S(1)}, f32[72,128]{1,0:T(8,128)S(1)}, u32[]{:S(2)}, u32[]{:S(2)}) collective-permute-start(f32[72,128]{1,0:T(8,128)S(1)} %get-tuple-element.33), channel_id=1, source_target_pairs={{0,24},{24,0},{16,40},{40,16},{32,56},{56,32},{48,72},{72,48},{64,... | collective-permute-start | bytes 110600 | tf_op jit(solution)/shard_map/ppermute | solution.py:376
  46.6 0.0 collective-permute-done.4
  46.6 3.6 %collective-permute-done.5 = f32[72,128]{1,0:T(8,128)S(1)} collective-permute-done((f32[72,128]{1,0:T(8,128)S(1)}, f32[72,128]{1,0:T(8,128)S(1)}, u32[]{:S(2)}, u32[]{:S(2)}) %collective-permute-start.5) | collective-permute-done | bytes 36896 | tf_op jit(solution)/shard_map/ppermute | solution.py:376
  50.2 3.7 %collective-permute-start.7 = (f32[216,128]{1,0:T(8,128)S(1)}, f32[216,128]{1,0:T(8,128)S(1)}, u32[]{:S(2)}, u32[]{:S(2)}) collective-permute-start(f32[216,128]{1,0:T(8,128)S(1)} %constant_dynamic-update-slice_fusion.y_ref), channel_id=1, source_target_pairs={{8,16},{16,8},{24,32},{32,24},{40,48},{48,40},{56,64},{64,56},{72,... | collective-permute-start | bytes 331784 | tf_op jit(solution)/shard_map/ppermute | solution.py:376
  54.0 1.9 %collective-permute-start.6 = (f32[216,128]{1,0:T(8,128)S(1)}, f32[216,128]{1,0:T(8,128)S(1)}, u32[]{:S(2)}, u32[]{:S(2)}) collective-permute-start(f32[216,128]{1,0:T(8,128)S(1)} %constant_dynamic-update-slice_fusion.y_ref), channel_id=1, source_target_pairs={{0,8},{8,0},{16,24},{24,16},{32,40},{40,32},{48,56},{56,48},{64,72... | collective-permute-start | bytes 331784 | tf_op jit(solution)/shard_map/ppermute | solution.py:376
  55.9 0.9 %collective-permute-done.7.z_in = f32[216,128]{1,0:T(8,128)S(1)} collective-permute-done((f32[216,128]{1,0:T(8,128)S(1)}, f32[216,128]{1,0:T(8,128)S(1)}, u32[]{:S(2)}, u32[]{:S(2)}) %collective-permute-start.7) | collective-permute-done | bytes 110624 | tf_op jit(solution)/shard_map/ppermute | solution.py:376
  56.9 3.8 %collective-permute-done.6.a_in = f32[216,128]{1,0:T(8,128)S(1)} collective-permute-done((f32[216,128]{1,0:T(8,128)S(1)}, f32[216,128]{1,0:T(8,128)S(1)}, u32[]{:S(2)}, u32[]{:S(2)}) %collective-permute-start.6) | collective-permute-done | bytes 110624 | tf_op jit(solution)/shard_map/ppermute | solution.py:376
  60.6 4.8 %shard_map.106 = (f32[384,128]{1,0:T(8,128)}, f32[384,128]{1,0:T(8,128)}, f32[8,128]{1,0:T(8,128)}) custom-call(f32[216,128]{1,0:T(8,128)S(1)} %constant_dynamic-update-slice_fusion.y_ref, f32[216,128]{1,0:T(8,128)S(1)} %collective-permute-done.6.a_in, f32[216,128]{1,0:T(8,128)S(1)} %collective-permute-done.7.z_in, f32[384,128]{1,0:T(8,128)S(1)} %get-tuple-element.34.su_ref, ...), custom_call_target="tpu_custom_call" | custom-call | tf_op jit(solution)/shard_map/pallas_call | solution.py:360
  (3 shorter events, 0.0 us)
Async XLA Ops:
  2.7 6.5 %collective-permute-start = (f32[296,128]{1,0:T(8,128)S(1)}, f32[296,128]{1,0:T(8,128)S(1)}, u32[]{:S(2)}, u32[]{:S(2)}) collective-permute-start(f32[296,128]{1,0:T(8,128)S(1)} %get-tuple-element.25), channel_id=1, source_target_pairs={{1,2},{2,1},{3,4},{4,3},{5,6},{6,5},{9,10},{10,9},{11,12},{12,11},... | collective-permute-start | bytes 454664 | tf_op jit(solution)/shard_map/ppermute | solution.py:376
  4.7 4.6 %collective-permute-start.1 = (f32[296,128]{1,0:T(8,128)S(1)}, f32[296,128]{1,0:T(8,128)S(1)}, u32[]{:S(2)}, u32[]{:S(2)}) collective-permute-start(f32[296,128]{1,0:T(8,128)S(1)} %get-tuple-element.26), channel_id=1, source_target_pairs={{0,1},{1,0},{2,3},{3,2},{4,5},{5,4},{6,7},{7,6},{8,9},{9,8},{10,11... | collective-permute-start | bytes 454664 | tf_op jit(solution)/shard_map/ppermute | solution.py:376
  9.6 22.9 %collective-permute-start.2 = (f32[248,128]{1,0:T(8,128)S(1)}, f32[248,128]{1,0:T(8,128)S(1)}, u32[]{:S(2)}, u32[]{:S(2)}) collective-permute-start(f32[248,128]{1,0:T(8,128)S(1)} %get-tuple-element.31), channel_id=1, source_target_pairs={{8,16},{16,8},{24,32},{32,24},{40,48},{48,40},{56,64},{64,56},{72,... | collective-permute-start | bytes 380936 | tf_op jit(solution)/shard_map/ppermute | solution.py:376
  13.5 22.7 %collective-permute-start.3 = (f32[248,128]{1,0:T(8,128)S(1)}, f32[248,128]{1,0:T(8,128)S(1)}, u32[]{:S(2)}, u32[]{:S(2)}) collective-permute-start(f32[248,128]{1,0:T(8,128)S(1)} %get-tuple-element.32), channel_id=1, source_target_pairs={{0,8},{8,0},{16,24},{24,16},{32,40},{40,32},{48,56},{56,48},{64,72... | collective-permute-start | bytes 380936 | tf_op jit(solution)/shard_map/ppermute | solution.py:376
  37.0 9.6 %collective-permute-start.4 = (f32[72,128]{1,0:T(8,128)S(1)}, f32[72,128]{1,0:T(8,128)S(1)}, u32[]{:S(2)}, u32[]{:S(2)}) collective-permute-start(f32[72,128]{1,0:T(8,128)S(1)} %get-tuple-element.33), channel_id=1, source_target_pairs={{8,32},{32,8},{24,48},{48,24},{40,64},{64,40},{56,80},{80,56},{72,... | collective-permute-start | bytes 110600 | tf_op jit(solution)/shard_map/ppermute | solution.py:376
  38.9 11.3 %collective-permute-start.5 = (f32[72,128]{1,0:T(8,128)S(1)}, f32[72,128]{1,0:T(8,128)S(1)}, u32[]{:S(2)}, u32[]{:S(2)}) collective-permute-start(f32[72,128]{1,0:T(8,128)S(1)} %get-tuple-element.33), channel_id=1, source_target_pairs={{0,24},{24,0},{16,40},{40,16},{32,56},{56,32},{48,72},{72,48},{64,... | collective-permute-start | bytes 110600 | tf_op jit(solution)/shard_map/ppermute | solution.py:376
  50.2 6.6 %collective-permute-start.7 = (f32[216,128]{1,0:T(8,128)S(1)}, f32[216,128]{1,0:T(8,128)S(1)}, u32[]{:S(2)}, u32[]{:S(2)}) collective-permute-start(f32[216,128]{1,0:T(8,128)S(1)} %constant_dynamic-update-slice_fusion.y_ref), channel_id=1, source_target_pairs={{8,16},{16,8},{24,32},{32,24},{40,48},{48,40},{56,64},{64,56},{72,... | collective-permute-start | bytes 331784 | tf_op jit(solution)/shard_map/ppermute | solution.py:376
  54.0 6.6 %collective-permute-start.6 = (f32[216,128]{1,0:T(8,128)S(1)}, f32[216,128]{1,0:T(8,128)S(1)}, u32[]{:S(2)}, u32[]{:S(2)}) collective-permute-start(f32[216,128]{1,0:T(8,128)S(1)} %constant_dynamic-update-slice_fusion.y_ref), channel_id=1, source_target_pairs={{0,8},{8,0},{16,24},{24,16},{32,40},{40,32},{48,56},{56,48},{64,72... | collective-permute-start | bytes 331784 | tf_op jit(solution)/shard_map/ppermute | solution.py:376

commit v5 on v4

--- a/solution.py
+++ b/solution.py
@@ -13,7 +13,9 @@
 SLOTS = 4
 CHUNKS = 4
 REACH = 4
-FIELDS = 9 * COLS
+NEAR_ROWS = 9 * COLS
+FAR_ROWS = 8 * COLS
+TRIOS = (((2, 0, 21), (3, 43, 22), (0, 86, 21)), ((1, 0, 21), (4, 42, 21), (5, 84, 21)))
 STEP = 6.0
 VMEM_BYTES = 32 * 1024 * 1024
 
@@ -109,10 +111,14 @@
     send(3 * groups, [plane_ref[level(s), :] for s in range(SLOTS)])
 
 
-def pack_cols_kernel(u_ref, v_ref, b_ref, plane_ref, z_in, a_in, a_ref, z_ref, hu_ref, hv_ref, hb_ref, hp_ref):
+def pack_cols_kernel(
+    u_ref, v_ref, b_ref, plane_ref, z_in, a_in,
+    a_ref, z_ref, hu_ref, hv_ref, hplane_ref, p_ref, hp_ref,
+):
     even = is_even("lat")
     upper = lane_index() < LANES // 2
     levels = u_ref.shape[0] // COLS
+    thick = thickness(levels)
     groups = levels // SLOTS
 
     def receive(at, s):
@@ -123,25 +129,33 @@
         o = pltpu.roll(o, to_last, 1) if to_last else o
         return jnp.where(upper, n, o)
 
-    for f, ref in enumerate((hu_ref, hv_ref, hb_ref)):
-        for k in range(levels):
-            ref[level(k), :] = receive(f * groups + k // SLOTS, k % SLOTS)
+    own = rim = jnp.zeros((COLS, LANES), jnp.float32)
+    for k in range(levels):
+        dz = float(thick[k])
+        hu_ref[level(k), :] = receive(k // SLOTS, k % SLOTS)
+        hv_ref[level(k), :] = receive(groups + k // SLOTS, k % SLOTS)
+        own = own + dz * b_ref[level(k), :]
+        rim = rim + dz * receive(2 * groups + k // SLOTS, k % SLOTS)
+        p_ref[level(k), :] = own
+        hp_ref[level(k), :] = rim
     for s in range(SLOTS):
-        hp_ref[level(s), :] = receive(3 * groups, s)
+        hplane_ref[level(s), :] = receive(3 * groups, s)
+
+    def edge(ref, col):
+        return ref[pl.ds(col, levels, stride=COLS), :]
+
+    def store(col, out_ref):
+        own, rim = edge(u_ref, col), edge(hu_ref, col)
+        if col == 0:
+            own, rim = 0.05 * own - edge(p_ref, col), 0.05 * rim - edge(hp_ref, col)
+        out_ref[pl.ds(0, levels), :] = own
+        out_ref[pl.ds(levels, levels), :] = edge(v_ref, col)
+        out_ref[pl.ds(2 * levels, levels), :] = pair_rims(rim, edge(hv_ref, col))
+        out_ref[pl.ds(3 * levels, 1), :] = plane_ref[pl.ds(col, 1), :]
+        out_ref[pl.ds(3 * levels + 1, 1), :] = hplane_ref[pl.ds(col, 1), :]
+        out_ref[pl.ds(3 * levels + 2, 6), :] = jnp.zeros((6, LANES), jnp.float32)
+
     even_col = is_even("lon")
-
-    def edge(ref, rows, col):
-        return ref[pl.ds(col, rows, stride=COLS), :]
-
-    def store(col, out_ref):
-        out_ref[pl.ds(0, levels), :] = edge(u_ref, levels, col)
-        out_ref[pl.ds(levels, levels), :] = edge(v_ref, levels, col)
-        out_ref[pl.ds(2 * levels, levels), :] = edge(b_ref, levels, col)
-        out_ref[pl.ds(3 * levels, levels), :] = pair_rims(edge(hu_ref, levels, col), edge(hv_ref, levels, col))
-        out_ref[pl.ds(4 * levels, levels), :] = edge(hb_ref, levels, col)
-        out_ref[pl.ds(5 * levels, 1), :] = plane_ref[pl.ds(col, 1), :]
-        out_ref[pl.ds(5 * levels + 1, 1), :] = hp_ref[pl.ds(col, 1), :]
-        out_ref[pl.ds(5 * levels + 2, 6), :] = jnp.zeros((6, LANES), jnp.float32)
 
     @pl.when(even_col)
     def _():
@@ -155,59 +169,53 @@
 
 
 def levels_kernel(
-    u_ref, v_ref, b_ref, hu_ref, hv_ref, hb_ref, hp_ref, plane_ref, z_in, a_in,
-    x_ref, su_ref, sv_ref, east_ref, west_ref,
+    u_ref, v_ref, hu_ref, hv_ref, p_ref, hp_ref, plane_ref, hplane_ref, z_in, a_in,
+    far_ref, x_ref, su_ref, sv_ref, east_ref, west_ref,
 ):
     levels = u_ref.shape[0] // COLS
     thick = thickness(levels)
     even = is_even("lon")
     a, z = a_in[...], z_in[...]
-    east_ref[pl.ds(0, a.shape[0]), :] = jnp.where(even, a, z)
-    west_ref[pl.ds(0, a.shape[0]), :] = jnp.where(even, z, a)
+    rows = a.shape[0]
+    east_ref[pl.ds(0, rows), :] = jnp.where(even, a, z)
+    west_ref[pl.ds(0, rows), :] = jnp.where(even, z, a)
     for ref in (east_ref, west_ref):
-        ref[pl.ds(a.shape[0], levels), :] = pltpu.roll(ref[pl.ds(3 * levels, levels), :], LANES // 2, 1)
-    own_at = {"u": 0, "v": levels, "b": 2 * levels, "w": 5 * levels}
-    rim_at = {"u": 3 * levels, "v": a.shape[0], "b": 4 * levels, "w": 5 * levels + 1}
+        ref[pl.ds(rows, levels), :] = pltpu.roll(ref[pl.ds(2 * levels, levels), :], LANES // 2, 1)
+    U, V, W = (0, 2 * levels), (levels, rows), (3 * levels, 3 * levels + 1)
     col = col_index()
     top_col, bottom_col = col == COLS - 1, col == 0
 
     def row(ref, at):
         return jnp.broadcast_to(ref[pl.ds(at, 1), :], (COLS, LANES))
 
-    def east(pair, name, k):
-        own, rim = pair
-        return (
-            jnp.where(top_col, row(east_ref, own_at[name] + k), pltpu.roll(own, COLS - 1, 0)),
-            jnp.where(top_col, row(east_ref, rim_at[name] + k), pltpu.roll(rim, COLS - 1, 0)),
-        )
-
-    def west(pair, name, k):
-        own, rim = pair
-        return (
-            jnp.where(bottom_col, row(west_ref, own_at[name] + k), pltpu.roll(own, 1, 0)),
-            jnp.where(bottom_col, row(west_ref, rim_at[name] + k), pltpu.roll(rim, 1, 0)),
-        )
-
-    water, eta, wx, wy = [(plane_ref[level(i), :], hp_ref[level(i), :]) for i in range(SLOTS)]
-    open_u = [jnp.minimum(w, e) for w, e in zip(water, east(water, "w", 0))]
+    def east(pair, places, k):
+        return [
+            jnp.where(top_col, row(east_ref, at + k), pltpu.roll(x, COLS - 1, 0)) for x, at in zip(pair, places)
+        ]
+
+    def west(pair, places, k):
+        return [
+            jnp.where(bottom_col, row(west_ref, at + k), pltpu.roll(x, 1, 0)) for x, at in zip(pair, places)
+        ]
+
+    water, eta, wx, wy = [(plane_ref[level(i), :], hplane_ref[level(i), :]) for i in range(SLOTS)]
+    open_u = [jnp.minimum(w, e) for w, e in zip(water, east(water, W, 0))]
     open_v = [jnp.minimum(w, n) for w, n in zip(water, north(*water))]
     zero = jnp.zeros((COLS, LANES), jnp.float32)
-    slope_u, slope_v = [zero, zero], [zero, zero]
     forcing_u, forcing_v = [zero, zero], [zero, zero]
     flow_u, flow_v = [zero, zero], [zero, zero]
     for k in range(levels):
         dz = float(thick[k])
         u = (u_ref[level(k), :], hu_ref[level(k), :])
         v = (v_ref[level(k), :], hv_ref[level(k), :])
-        b = (b_ref[level(k), :], hb_ref[level(k), :])
-        around_u = list(zip(east(u, "u", k), west(u, "u", k), north(*u), south(*u)))
-        around_v = list(zip(east(v, "v", k), west(v, "v", k), north(*v), south(*v)))
-        b_east, b_north = east(b, "b", k), north(*b)
+        p = (p_ref[level(k), :], hp_ref[level(k), :])
+        push_east = east([0.05 * u[t] - p[t] for t in range(2)], U, k)
+        around_u = list(zip(west(u, U, k), north(*u), south(*u)))
+        around_v = list(zip(east(v, V, k), west(v, V, k), north(*v), south(*v)))
+        p_north = north(*p)
         for t in range(2):
-            slope_u[t] = slope_u[t] + dz * (b_east[t] - b[t])
-            slope_v[t] = slope_v[t] + dz * (b_north[t] - b[t])
-            force_u = 0.05 * (sum(around_u[t][1:], around_u[t][0]) - 4.0 * u[t]) - slope_u[t]
-            force_v = 0.05 * (sum(around_v[t][1:], around_v[t][0]) - 4.0 * v[t]) - slope_v[t]
+            force_u = push_east[t] + (0.05 * (sum(around_u[t][1:], around_u[t][0]) - 4.0 * u[t]) + p[t])
+            force_v = 0.05 * (sum(around_v[t][1:], around_v[t][0]) - 4.0 * v[t]) - (p_north[t] - p[t])
             if k == 0:
                 force_u = force_u + wx[t] / dz
                 force_v = force_v + wy[t] / dz
@@ -224,8 +232,15 @@
     fields = (forcing_u, forcing_v, flow_u, flow_v, water, eta)
     for i, f in enumerate(fields):
         x_ref[level(i), :] = f[0]
+        far_ref[level(i), :] = f[0]
     for i in range(3):
         x_ref[level(6 + i), :] = pair_rims(fields[2 * i][1], fields[2 * i + 1][1])
+    for i, trio in enumerate(TRIOS):
+        parts = [pltpu.roll(fields[f][1], at + count, 1) for f, at, count in trio]
+        lane = lane_index()
+        far_ref[level(6 + i), :] = jnp.where(
+            lane < trio[1][1], parts[0], jnp.where(lane < trio[2][1], parts[1], parts[2])
+        )
 
 
 def depth_of(count, levels):
@@ -233,7 +248,7 @@
 
 
 def substeps_kernel(
-    y_ref, a_in, z_in, su_ref, sv_ref, out_u, out_v, out_eta,
+    y_ref, a_in, z_in, x_ref, su_ref, sv_ref, out_u, out_v, out_eta,
     eta_ref, u_ref, v_ref, w_ref, fu_ref, fv_ref, du_ref, dv_ref, cu_ref, cv_ref, tw_ref, q_ref, t_ref,
     eta_north_ref, u_north_ref, tw_north_ref,
 ):
@@ -248,27 +263,37 @@
 
     places = (
         ((z_in, 2), (a_in, 0)), ((y_ref, 0), (y_ref, 2)), ((a_in, 2), (z_in, 0)),
-        ((z_in, 1), (a_in, 1)), ((y_ref, 1), (y_ref, 1)), ((a_in, 1), (z_in, 1)),
+        ((z_in, 1), (a_in, 1)), ((x_ref, 0), (x_ref, 0)), ((a_in, 1), (z_in, 1)),
         ((z_in, 0), (a_in, 2)), ((y_ref, 2), (y_ref, 0)), ((a_in, 0), (z_in, 2)),
     )
     for p, (for_even, for_odd) in enumerate(places):
         def tile(i):
-            first = for_even[0][pl.ds(for_even[1] * FIELDS + COLS * i, COLS), :]
-            if p == REACH:
-                return first
-            return jnp.where(even, first, for_odd[0][pl.ds(for_odd[1] * FIELDS + COLS * i, COLS), :])
+            def read(place):
+                ref, part = place
+                start = 0
+                if ref is not x_ref:
+                    start = (0, FAR_ROWS, FAR_ROWS + NEAR_ROWS)[part]
+                return ref[pl.ds(start + COLS * i, COLS), :]
+
+            first = read(for_even)
+            return first if p == REACH else jnp.where(even, first, read(for_odd))
 
         targets = (fu_ref, fv_ref, u_ref, v_ref, w_ref, eta_ref)
         for i, ref in enumerate(targets):
             value = tile(i)
             ref[0, at(p), :] = tau * value if i < 2 else value
-        for i in range(3):
-            value = tile(6 + i)
-            other = pltpu.roll(value, LANES // 2, 1)
-            if i == 0:
-                value, other = tau * value, tau * other
-            targets[2 * i][1, at(p), :] = value
-            targets[2 * i + 1][1, at(p), :] = other
+        rims = [None] * 6
+        if abs(p - REACH) <= 1:
+            for i in range(3):
+                rims[2 * i] = tile(6 + i)
+                rims[2 * i + 1] = pltpu.roll(rims[2 * i], LANES // 2, 1)
+        else:
+            for i, trio in enumerate(TRIOS):
+                shared = tile(6 + i)
+                for f, first_lane, count in trio:
+                    rims[f] = pltpu.roll(shared, LANES - first_lane - count, 1)
+        for i, ref in enumerate(targets):
+            ref[1, at(p), :] = tau * rims[i] if i < 2 else rims[i]
 
     total_rows = LANES * lax.axis_size("lat")
     base = (lax.axis_index("lat") * LANES).astype(jnp.float32)
@@ -392,25 +417,27 @@
     )
     rows_z = swap(rows_z, "lat", 1, 1, False)
     rows_a = swap(rows_a, "lat", 0, 1, False)
-    edge = (5 * levels + 8, LANES)
-    cols_a, cols_z, hu, hv, hb, hp = call(
-        pack_cols_kernel, [edge, edge, flat, flat, flat, (SLOTS * COLS, LANES)], [], u, v, b, planes, rows_z, rows_a
+    edge = (3 * levels + 8, LANES)
+    cols_a, cols_z, hu, hv, hplanes, p, hp = call(
+        pack_cols_kernel,
+        [edge, edge, flat, flat, (SLOTS * COLS, LANES), flat, flat], [],
+        u, v, b, planes, rows_z, rows_a,
     )
     cols_z = swap(cols_z, "lon", 1, 1, True)
     cols_a = swap(cols_a, "lon", 0, 1, True)
     both = (edge[0] + levels, LANES)
-    x, star_u, star_v = call(
-        levels_kernel, [(FIELDS, LANES), flat, flat], [both, both],
-        u, v, b, hu, hv, hb, hp, planes, cols_z, cols_a,
-    )
-    far_z = swap(x, "lon", 1, 3, True)
-    far_a = swap(x, "lon", 0, 3, True)
+    far, x, star_u, star_v = call(
+        levels_kernel, [(FAR_ROWS, LANES), (NEAR_ROWS, LANES), flat, flat], [both, both],
+        u, v, hu, hv, p, hp, planes, hplanes, cols_z, cols_a,
+    )
+    far_z = swap(far, "lon", 1, 3, True)
+    far_a = swap(far, "lon", 0, 3, True)
     y = jnp.concatenate([far_z, x, far_a], 0)
     near_z = swap(y, "lon", 1, 1, True)
     near_a = swap(y, "lon", 0, 1, True)
     state = (2, (2 * REACH + 3) * COLS, LANES)
     new_u, new_v, surface = call(
-        substeps_kernel, [flat, flat, (COLS, LANES)], [state] * 16, y, near_a, near_z, star_u, star_v
+        substeps_kernel, [flat, flat, (COLS, LANES)], [state] * 16, y, near_a, near_z, x, star_u, star_v
     )
     return new_u.reshape(velocity_u.shape), new_v.reshape(velocity_v.shape), surface
 

time: 65.9 us -> 64.6 us (0.980)
  the two profiles are of different devices: /device:TPU:40 before, /device:TPU:56 now
where the time goes in v5:
time: 64.6 us; the launch traced here: 64.1 us
  starting transfers between devices  42.5 us (66%)
  waiting for transfers between devices  12.7 us (20%)
  Pallas kernels  8.09 us (13%)
  between operations  0.75 us (1%)
    ppermute x8, starting transfers between devices, swap(): return lax.ppermute(x, axis, pairs)  42.5 us
    ppermute x8, waiting for transfers between devices, swap(): return lax.ppermute(x, axis, pairs)  12.7 us
    pallas_call x4, Pallas kernels, call(): pl.pallas_call(kernel, out_shape=[jax.ShapeDtypeStruct(s, jnp.float32) fo...  8.09 us
  transfers between devices with their start and end apart: 8, of which 5 were waited for; matrix products, arithmetic and copies ran while one was open for 0% of the time, Pallas kernels for 0%

profile of v5, /device:TPU:56, one launch (start us, length us, event | category | flops | bytes accessed | tf_op | source)
XLA Modules:
  0.0 64.1 jit_solution(1086820571516873297)
XLA Ops:
  0.6 2.1 %shard_map.103 = (f32[296,128]{1,0:T(8,128)S(1)}, f32[296,128]{1,0:T(8,128)S(1)}, f32[384,128]{1,0:T(8,128)S(1)}, f32[384,128]{1,0:T(8,128)S(1)}, f32[384,128]{1,0:T(8,128)S(1)}, /*index=5*/f32[32,128]{1,0:T(8,128)S(1)}) custom-call(f32[384,128]{1,0:T(8,128)} %bitcast.5, f32[384,128]{1,0:T(8,128)} %bitcast.6, f32[384,128]{1,0:T(8,128)} %bitcast.7, ...), custom_call_target="tpu_custom_call" | custom-call | tf_op jit(solution)/shard_map/pallas_call | solution.py:385
  2.7 2.1 %collective-permute-start = (f32[296,128]{1,0:T(8,128)S(1)}, f32[296,128]{1,0:T(8,128)S(1)}, u32[]{:S(2)}, u32[]{:S(2)}) collective-permute-start(f32[296,128]{1,0:T(8,128)S(1)} %get-tuple-element.27), channel_id=1, source_target_pairs={{1,2},{2,1},{3,4},{4,3},{5,6},{6,5},{9,10},{10,9},{11,12},{12,11},... | collective-permute-start | bytes 454664 | tf_op jit(solution)/shard_map/ppermute | solution.py:401
  4.8 1.9 %collective-permute-start.1 = (f32[296,128]{1,0:T(8,128)S(1)}, f32[296,128]{1,0:T(8,128)S(1)}, u32[]{:S(2)}, u32[]{:S(2)}) collective-permute-start(f32[296,128]{1,0:T(8,128)S(1)} %get-tuple-element.28), channel_id=1, source_target_pairs={{0,1},{1,0},{2,3},{3,2},{4,5},{5,4},{6,7},{7,6},{8,9},{9,8},{10,11... | collective-permute-start | bytes 454664 | tf_op jit(solution)/shard_map/ppermute | solution.py:401
  6.8 2.5 %collective-permute-done.z_in = f32[296,128]{1,0:T(8,128)S(1)} collective-permute-done((f32[296,128]{1,0:T(8,128)S(1)}, f32[296,128]{1,0:T(8,128)S(1)}, u32[]{:S(2)}, u32[]{:S(2)}) %collective-permute-start) | collective-permute-done | bytes 151584 | tf_op jit(solution)/shard_map/ppermute | solution.py:401
  9.2 0.0 collective-permute-done.1.a_in
  9.2 0.4 shard_map.104
  9.6 3.8 %collective-permute-start.2 = (f32[152,128]{1,0:T(8,128)S(1)}, f32[152,128]{1,0:T(8,128)S(1)}, u32[]{:S(2)}, u32[]{:S(2)}) collective-permute-start(f32[152,128]{1,0:T(8,128)S(1)} %get-tuple-element.34), channel_id=1, source_target_pairs={{8,16},{16,8},{24,32},{32,24},{40,48},{48,40},{56,64},{64,56},{72,... | collective-permute-start | bytes 233480 | tf_op jit(solution)/shard_map/ppermute | solution.py:401
  13.5 19.1 %collective-permute-start.3 = (f32[152,128]{1,0:T(8,128)S(1)}, f32[152,128]{1,0:T(8,128)S(1)}, u32[]{:S(2)}, u32[]{:S(2)}) collective-permute-start(f32[152,128]{1,0:T(8,128)S(1)} %get-tuple-element.35), channel_id=1, source_target_pairs={{0,8},{8,0},{16,24},{24,16},{32,40},{40,32},{48,56},{56,48},{64,72... | collective-permute-start | bytes 233480 | tf_op jit(solution)/shard_map/ppermute | solution.py:401
  32.5 0.0 collective-permute-done.2.z_in
  32.6 2.4 %collective-permute-done.3.a_in = f32[152,128]{1,0:T(8,128)S(1)} collective-permute-done((f32[152,128]{1,0:T(8,128)S(1)}, f32[152,128]{1,0:T(8,128)S(1)}, u32[]{:S(2)}, u32[]{:S(2)}) %collective-permute-start.3) | collective-permute-done | bytes 77856 | tf_op jit(solution)/shard_map/ppermute | solution.py:401
  34.9 0.8 %shard_map.105 = (f32[64,128]{1,0:T(8,128)S(1)}, f32[72,128]{1,0:T(8,128)S(1)}, f32[384,128]{1,0:T(8,128)S(1)}, f32[384,128]{1,0:T(8,128)S(1)}) custom-call(f32[384,128]{1,0:T(8,128)S(1)} %get-tuple-element.23.u_ref, f32[384,128]{1,0:T(8,128)S(1)} %get-tuple-element.24.v_ref, f32[384,128]{1,0:T(8,128)S(1)} %get-tuple-element.29.hu_ref, ...), custom_call_target="tpu_custom_call" | custom-call | tf_op jit(solution)/shard_map/pallas_call | solution.py:385
  35.7 1.9 %collective-permute-start.4 = (f32[64,128]{1,0:T(8,128)S(1)}, f32[64,128]{1,0:T(8,128)S(1)}, u32[]{:S(2)}, u32[]{:S(2)}) collective-permute-start(f32[64,128]{1,0:T(8,128)S(1)} %get-tuple-element.36), channel_id=1, source_target_pairs={{8,32},{32,8},{24,48},{48,24},{40,64},{64,40},{56,80},{80,56},{72,... | collective-permute-start | bytes 98312 | tf_op jit(solution)/shard_map/ppermute | solution.py:401
  37.6 7.9 %collective-permute-start.5 = (f32[64,128]{1,0:T(8,128)S(1)}, f32[64,128]{1,0:T(8,128)S(1)}, u32[]{:S(2)}, u32[]{:S(2)}) collective-permute-start(f32[64,128]{1,0:T(8,128)S(1)} %get-tuple-element.36), channel_id=1, source_target_pairs={{0,24},{24,0},{16,40},{40,16},{32,56},{56,32},{48,72},{72,48},{64,... | collective-permute-start | bytes 98312 | tf_op jit(solution)/shard_map/ppermute | solution.py:401
  45.5 0.0 collective-permute-done.4
  45.5 3.3 %collective-permute-done.5 = f32[64,128]{1,0:T(8,128)S(1)} collective-permute-done((f32[64,128]{1,0:T(8,128)S(1)}, f32[64,128]{1,0:T(8,128)S(1)}, u32[]{:S(2)}, u32[]{:S(2)}) %collective-permute-start.5) | collective-permute-done | bytes 32800 | tf_op jit(solution)/shard_map/ppermute | solution.py:401
  48.8 3.9 %collective-permute-start.7 = (f32[200,128]{1,0:T(8,128)S(1)}, f32[200,128]{1,0:T(8,128)S(1)}, u32[]{:S(2)}, u32[]{:S(2)}) collective-permute-start(f32[200,128]{1,0:T(8,128)S(1)} %constant_dynamic-update-slice_fusion.y_ref), channel_id=1, source_target_pairs={{8,16},{16,8},{24,32},{32,24},{40,48},{48,40},{56,64},{64,56},{72,... | collective-permute-start | bytes 307208 | tf_op jit(solution)/shard_map/ppermute | solution.py:401
  52.7 1.9 %collective-permute-start.6 = (f32[200,128]{1,0:T(8,128)S(1)}, f32[200,128]{1,0:T(8,128)S(1)}, u32[]{:S(2)}, u32[]{:S(2)}) collective-permute-start(f32[200,128]{1,0:T(8,128)S(1)} %constant_dynamic-update-slice_fusion.y_ref), channel_id=1, source_target_pairs={{0,8},{8,0},{16,24},{24,16},{32,40},{40,32},{48,56},{56,48},{64,72... | collective-permute-start | bytes 307208 | tf_op jit(solution)/shard_map/ppermute | solution.py:401
  54.7 0.7 %collective-permute-done.7.z_in = f32[200,128]{1,0:T(8,128)S(1)} collective-permute-done((f32[200,128]{1,0:T(8,128)S(1)}, f32[200,128]{1,0:T(8,128)S(1)}, u32[]{:S(2)}, u32[]{:S(2)}) %collective-permute-start.7) | collective-permute-done | bytes 102432 | tf_op jit(solution)/shard_map/ppermute | solution.py:401
  55.4 3.9 %collective-permute-done.6.a_in = f32[200,128]{1,0:T(8,128)S(1)} collective-permute-done((f32[200,128]{1,0:T(8,128)S(1)}, f32[200,128]{1,0:T(8,128)S(1)}, u32[]{:S(2)}, u32[]{:S(2)}) %collective-permute-start.6) | collective-permute-done | bytes 102432 | tf_op jit(solution)/shard_map/ppermute | solution.py:401
  59.3 4.9 %shard_map.106 = (f32[384,128]{1,0:T(8,128)}, f32[384,128]{1,0:T(8,128)}, f32[8,128]{1,0:T(8,128)}) custom-call(f32[200,128]{1,0:T(8,128)S(1)} %constant_dynamic-update-slice_fusion.y_ref, f32[200,128]{1,0:T(8,128)S(1)} %collective-permute-done.6.a_in, f32[200,128]{1,0:T(8,128)S(1)} %collective-permute-done.7.z_in, f32[72,128]{1,0:T(8,128)S(1)} %get-tuple-element.37.x_ref, ...), custom_call_target="tpu_custom_call" | custom-call | tf_op jit(solution)/shard_map/pallas_call | solution.py:385
  (3 shorter events, 0.0 us)
Async XLA Ops:
  2.7 6.5 %collective-permute-start = (f32[296,128]{1,0:T(8,128)S(1)}, f32[296,128]{1,0:T(8,128)S(1)}, u32[]{:S(2)}, u32[]{:S(2)}) collective-permute-start(f32[296,128]{1,0:T(8,128)S(1)} %get-tuple-element.27), channel_id=1, source_target_pairs={{1,2},{2,1},{3,4},{4,3},{5,6},{6,5},{9,10},{10,9},{11,12},{12,11},... | collective-permute-start | bytes 454664 | tf_op jit(solution)/shard_map/ppermute | solution.py:401
  4.8 4.4 %collective-permute-start.1 = (f32[296,128]{1,0:T(8,128)S(1)}, f32[296,128]{1,0:T(8,128)S(1)}, u32[]{:S(2)}, u32[]{:S(2)}) collective-permute-start(f32[296,128]{1,0:T(8,128)S(1)} %get-tuple-element.28), channel_id=1, source_target_pairs={{0,1},{1,0},{2,3},{3,2},{4,5},{5,4},{6,7},{7,6},{8,9},{9,8},{10,11... | collective-permute-start | bytes 454664 | tf_op jit(solution)/shard_map/ppermute | solution.py:401
  9.6 22.9 %collective-permute-start.2 = (f32[152,128]{1,0:T(8,128)S(1)}, f32[152,128]{1,0:T(8,128)S(1)}, u32[]{:S(2)}, u32[]{:S(2)}) collective-permute-start(f32[152,128]{1,0:T(8,128)S(1)} %get-tuple-element.34), channel_id=1, source_target_pairs={{8,16},{16,8},{24,32},{32,24},{40,48},{48,40},{56,64},{64,56},{72,... | collective-permute-start | bytes 233480 | tf_op jit(solution)/shard_map/ppermute | solution.py:401
  13.5 21.4 %collective-permute-start.3 = (f32[152,128]{1,0:T(8,128)S(1)}, f32[152,128]{1,0:T(8,128)S(1)}, u32[]{:S(2)}, u32[]{:S(2)}) collective-permute-start(f32[152,128]{1,0:T(8,128)S(1)} %get-tuple-element.35), channel_id=1, source_target_pairs={{0,8},{8,0},{16,24},{24,16},{32,40},{40,32},{48,56},{56,48},{64,72... | collective-permute-start | bytes 233480 | tf_op jit(solution)/shard_map/ppermute | solution.py:401
  35.7 9.8 %collective-permute-start.4 = (f32[64,128]{1,0:T(8,128)S(1)}, f32[64,128]{1,0:T(8,128)S(1)}, u32[]{:S(2)}, u32[]{:S(2)}) collective-permute-start(f32[64,128]{1,0:T(8,128)S(1)} %get-tuple-element.36), channel_id=1, source_target_pairs={{8,32},{32,8},{24,48},{48,24},{40,64},{64,40},{56,80},{80,56},{72,... | collective-permute-start | bytes 98312 | tf_op jit(solution)/shard_map/ppermute | solution.py:401
  37.6 11.2 %collective-permute-start.5 = (f32[64,128]{1,0:T(8,128)S(1)}, f32[64,128]{1,0:T(8,128)S(1)}, u32[]{:S(2)}, u32[]{:S(2)}) collective-permute-start(f32[64,128]{1,0:T(8,128)S(1)} %get-tuple-element.36), channel_id=1, source_target_pairs={{0,24},{24,0},{16,40},{40,16},{32,56},{56,32},{48,72},{72,48},{64,... | collective-permute-start | bytes 98312 | tf_op jit(solution)/shard_map/ppermute | solution.py:401
  48.8 6.5 %collective-permute-start.7 = (f32[200,128]{1,0:T(8,128)S(1)}, f32[200,128]{1,0:T(8,128)S(1)}, u32[]{:S(2)}, u32[]{:S(2)}) collective-permute-start(f32[200,128]{1,0:T(8,128)S(1)} %constant_dynamic-update-slice_fusion.y_ref), channel_id=1, source_target_pairs={{8,16},{16,8},{24,32},{32,24},{40,48},{48,40},{56,64},{64,56},{72,... | collective-permute-start | bytes 307208 | tf_op jit(solution)/shard_map/ppermute | solution.py:401
  52.7 6.6 %collective-permute-start.6 = (f32[200,128]{1,0:T(8,128)S(1)}, f32[200,128]{1,0:T(8,128)S(1)}, u32[]{:S(2)}, u32[]{:S(2)}) collective-permute-start(f32[200,128]{1,0:T(8,128)S(1)} %constant_dynamic-update-slice_fusion.y_ref), channel_id=1, source_target_pairs={{0,8},{8,0},{16,24},{24,16},{32,40},{40,32},{48,56},{56,48},{64,72... | collective-permute-start | bytes 307208 | tf_op jit(solution)/shard_map/ppermute | solution.py:401

commit v6 on v4

v6 whole, which is shorter than its diff:
```python
import jax
import jax.numpy as jnp
import numpy as np
from jax import lax
from jax.experimental import pallas as pl
from jax.experimental.pallas import tpu as pltpu
from jax.sharding import PartitionSpec as P

SUBSTEPS = 30
LANES = 128
COLS = 8
RIM = 32
SLOTS = 4
REACH = 4
BLOCKS = 2 * REACH + 1
FIELDS = 6
BLOCK_ROWS = FIELDS * COLS
RIM_TILES = -(-BLOCKS * FIELDS // SLOTS)
STEP = 6.0
VMEM_BYTES = 32 * 1024 * 1024


def thickness(levels):
    index = np.arange(levels, dtype=np.float32)
    return (np.float32(1.0) + np.float32(2.0) * index / np.float32(levels)) / np.float32(levels)


def lane_index():
    return lax.broadcasted_iota(jnp.int32, (COLS, LANES), 1)


def col_index():
    return lax.broadcasted_iota(jnp.int32, (COLS, LANES), 0)


def is_even(axis):
    return lax.rem(lax.axis_index(axis), 2) == 0


def level(k):
    return pl.ds(COLS * k, COLS)


def north(own, rim):
    last = lane_index() == LANES - 1
    a, b = pltpu.roll(own, LANES - 1, 1), pltpu.roll(rim, LANES - 1, 1)
    return jnp.where(last, b, a), jnp.where(last, a, b)


def south(own, rim):
    first = lane_index() == 0
    a, b = pltpu.roll(own, 1, 1), pltpu.roll(rim, 1, 1)
    return jnp.where(first, b, a), jnp.where(first, a, b)


def strips(parts, shifts):
    slot = lane_index() // RIM
    moved = [pltpu.roll(p, s, 1) if s else p for p, s in zip(parts, shifts)]
    return jnp.where(
        slot < 2, jnp.where(slot == 0, moved[0], moved[1]), jnp.where(slot == 2, moved[2], moved[3])
    )


def pack_edges_kernel(
    u_in, v_in, b_in, land_in, bottom_in, eta_in, wx_in, wy_in,
    col_a_ref, col_z_ref, row_a_ref, row_z_ref, u_ref, v_ref, p_ref, plane_ref,
    b_ref, land_ref, bottom_ref, sems,
):
    levels = u_in.shape[0] // COLS
    thick = thickness(levels)
    copies = [
        pltpu.make_async_copy(src, dst, sems.at[i])
        for i, (src, dst) in enumerate(
            (
                (u_in, u_ref), (v_in, v_ref), (b_in, b_ref), (land_in, land_ref), (bottom_in, bottom_ref),
                (eta_in, plane_ref.at[level(1)]), (wx_in, plane_ref.at[level(2)]), (wy_in, plane_ref.at[level(3)]),
            )
        )
    ]
    for copy in copies:
        copy.start()
    for copy in copies:
        copy.wait()
    lane = lane_index()
    water = (land_ref[...] * bottom_ref[...]).astype(jnp.float32)
    plane_ref[level(0), :] = water
    upper = jnp.zeros((COLS, LANES), jnp.float32)
    lower = jnp.where(lane == 2 * levels, pltpu.roll(water, 2 * levels, 1), 0.0)
    p = jnp.zeros((COLS, LANES), jnp.float32)
    for k in range(levels):
        u, v = u_ref[level(k), :], v_ref[level(k), :]
        p = p + float(thick[k]) * b_ref[level(k), :]
        p_ref[level(k), :] = p
        for at, up, low in ((k, u, u), (levels + k, v, 0.05 * v - p)):
            upper = jnp.where(lane == at, pltpu.roll(up, at + 1, 1), upper)
            lower = jnp.where(lane == at, pltpu.roll(low, at, 1) if at else low, lower)
    even_row = is_even("lat")
    row_a_ref[...] = jnp.where(even_row, upper, lower)
    row_z_ref[...] = jnp.where(even_row, lower, upper)

    def edge(ref, col):
        return ref[pl.ds(col, levels, stride=COLS), :]

    def store(col, out_ref):
        first = edge(u_ref, col)
        out_ref[pl.ds(0, levels), :] = first if col else 0.05 * first - edge(p_ref, col)
        out_ref[pl.ds(levels, levels), :] = edge(v_ref, col)
        out_ref[pl.ds(2 * levels, COLS), :] = water

    even_col = is_even("lon")

    @pl.when(even_col)
    def _():
        store(COLS - 1, col_a_ref)
        store(0, col_z_ref)

    @pl.when(jnp.logical_not(even_col))
    def _():
        store(0, col_a_ref)
        store(COLS - 1, col_z_ref)


def levels_kernel(
    u_ref, v_ref, p_ref, plane_ref, col_z, col_a, row_z, row_a, x_ref, su_ref, sv_ref, east_ref, west_ref
):
    levels = u_ref.shape[0] // COLS
    thick = thickness(levels)
    even_col, even_row = is_even("lon"), is_even("lat")
    east_ref[...] = jnp.where(even_col, col_a[...], col_z[...])
    west_ref[...] = jnp.where(even_col, col_z[...], col_a[...])
    from_north = jnp.where(even_row, row_a[...], row_z[...])
    from_south = jnp.where(even_row, row_z[...], row_a[...])
    col, lane = col_index(), lane_index()
    top_col, bottom_col = col == COLS - 1, col == 0
    top_row, bottom_row = lane == LANES - 1, lane == 0

    def row(ref, at):
        return jnp.broadcast_to(ref[pl.ds(at, 1), :], (COLS, LANES))

    def east(x, at):
        return jnp.where(top_col, row(east_ref, at), pltpu.roll(x, COLS - 1, 0))

    def west(x, at):
        return jnp.where(bottom_col, row(west_ref, at), pltpu.roll(x, 1, 0))

    def northern(x, at):
        return jnp.where(top_row, pltpu.roll(from_north, LANES - 1 - at, 1), pltpu.roll(x, LANES - 1, 1))

    def southern(x, at):
        edge = pltpu.roll(from_south, LANES - at, 1) if at else from_south
        return jnp.where(bottom_row, edge, pltpu.roll(x, 1, 1))

    water, eta, wx, wy = [plane_ref[level(i), :] for i in range(4)]
    open_u = jnp.minimum(water, east(water, 2 * levels))
    open_v = jnp.minimum(water, northern(water, 2 * levels))
    zero = jnp.zeros((COLS, LANES), jnp.float32)
    forcing_u = forcing_v = flow_u = flow_v = zero
    for k in range(levels):
        dz = float(thick[k])
        u, v, p = u_ref[level(k), :], v_ref[level(k), :], p_ref[level(k), :]
        force_u = east(0.05 * u - p, k) + (
            0.05 * (west(u, k) + northern(u, k) + southern(u, k) - 4.0 * u) + p
        )
        force_v = northern(0.05 * v - p, levels + k) + (
            0.05 * (east(v, levels + k) + west(v, levels + k) + southern(v, levels + k) - 4.0 * v) + p
        )
        if k == 0:
            force_u = force_u + wx / dz
            force_v = force_v + wy / dz
        wet_u, wet_v = open_u > float(k), open_v > float(k)
        force_u, vel_u = jnp.where(wet_u, force_u, 0.0), jnp.where(wet_u, u, 0.0)
        force_v, vel_v = jnp.where(wet_v, force_v, 0.0), jnp.where(wet_v, v, 0.0)
        forcing_u = forcing_u + dz * force_u
        forcing_v = forcing_v + dz * force_v
        flow_u = flow_u + dz * vel_u
        flow_v = flow_v + dz * vel_v
        su_ref[level(k), :] = vel_u + STEP * force_u
        sv_ref[level(k), :] = vel_v + STEP * force_v
    for i, f in enumerate((forcing_u, forcing_v, flow_u, flow_v, water, eta)):
        x_ref[level(i), :] = f


def pack_rims_kernel(y_ref, a_in, z_in, own_ref, row_a_ref, row_z_ref):
    even_col, even_row = is_even("lon"), is_even("lat")
    places = (
        ((z_in, 2), (a_in, 0)), ((y_ref, 0), (y_ref, 2)), ((a_in, 2), (z_in, 0)),
        ((z_in, 1), (a_in, 1)), ((y_ref, 1), (y_ref, 1)), ((a_in, 1), (z_in, 1)),
        ((z_in, 0), (a_in, 2)), ((y_ref, 2), (y_ref, 0)), ((a_in, 0), (z_in, 2)),
    )
    parts = []
    for p, sources in enumerate(places):
        for f in range(FIELDS):
            even, odd = [ref[pl.ds(part * BLOCK_ROWS + COLS * f, COLS), :] for ref, part in sources]
            value = even if p == REACH else jnp.where(even_col, even, odd)
            own_ref[level(f * BLOCKS + p), :] = value
            parts.append(value)
    parts += parts[: RIM_TILES * SLOTS - len(parts)]
    for t in range(RIM_TILES):
        group = parts[SLOTS * t : SLOTS * (t + 1)]
        upper, lower = strips(group, (32, 64, 96, 0)), strips(group, (0, 32, 64, 96))
        row_a_ref[level(t), :] = jnp.where(even_row, upper, lower)
        row_z_ref[level(t), :] = jnp.where(even_row, lower, upper)


def depth_of(count, levels):
    return (count + count * (count - 1.0) * (1.0 / levels)) * (1.0 / levels)


def substeps_kernel(
    own_ref, z_in, a_in, su_ref, sv_ref, out_u, out_v, out_eta,
    eta_ref, u_ref, v_ref, w_ref, fu_ref, fv_ref, du_ref, dv_ref, cu_ref, cv_ref, tw_ref, q_ref, t_ref,
    eta_north_ref, u_north_ref, tw_north_ref,
):
    levels = su_ref.shape[0] // COLS
    tau = STEP / SUBSTEPS
    even_row = is_even("lat")
    lane = lane_index()
    northern = lane < LANES // 2

    def at(p, shift=0):
        return pl.ds(COLS * (p + 1) + shift, COLS)

    def rim(q):
        a, z, s = a_in[level(q // SLOTS), :], z_in[level(q // SLOTS), :], q % SLOTS
        n, o = jnp.where(even_row, a, z), jnp.where(even_row, z, a)
        n = pltpu.roll(n, LANES - RIM * s, 1) if s else n
        o = pltpu.roll(o, LANES - RIM - RIM * s, 1) if s < SLOTS - 1 else o
        return jnp.where(northern, n, o)

    for p in range(BLOCKS):
        for f, ref in enumerate((fu_ref, fv_ref, u_ref, v_ref, w_ref, eta_ref)):
            pair = own_ref[level(f * BLOCKS + p), :], rim(FIELDS * p + f)
            for t in range(2):
                ref[t, at(p), :] = tau * pair[t] if f < 2 else pair[t]

    total_rows = LANES * lax.axis_size("lat")
    base = (lax.axis_index("lat") * LANES).astype(jnp.float32)
    own_row = lane.astype(jnp.float32) + base
    rim_row = jnp.where(lane < LANES // 2, lane + LANES, lane - LANES).astype(jnp.float32) + base
    spin = [
        [0.25 * tau * 0.4 * (2.0 * (r + half) * (1.0 / total_rows) - 1.0) for half in (0.5, 1.0)]
        for r in (own_row, rim_row)
    ]
    for p in range(BLOCKS):
        water = [w_ref[t, at(p), :] for t in range(2)]
        water_north = north(*water)
        eta_north = north(eta_ref[0, at(p), :], eta_ref[1, at(p), :])
        for t in range(2):
            eta_north_ref[t, at(p), :] = eta_north[t]
            tw_north_ref[t, at(p), :] = jnp.where(water_north[t] > 0.0, tau, 0.0)
            open_u = jnp.minimum(water[t], w_ref[t, at(p, 1), :])
            open_v = jnp.minimum(water[t], water_north[t])
            du_ref[t, at(p), :] = tau * depth_of(open_u, levels)
            dv_ref[t, at(p), :] = tau * depth_of(open_v, levels)
            cu_ref[t, at(p), :] = jnp.where(open_u > 0.0, spin[t][0], 0.0)
            cv_ref[t, at(p), :] = jnp.where(open_v > 0.0, spin[t][1], 0.0)
            tw_ref[t, at(p), :] = jnp.where(water[t] > 0.0, tau, 0.0)

    flow_u, flow_v = u_ref[0, at(REACH), :], v_ref[0, at(REACH), :]
    zero = jnp.zeros((COLS, LANES), jnp.float32)

    def substep(first, last):
        def body(_, carry):
            total_u, total_v = carry
            for p in range(first, last):
                u = [u_ref[t, at(p), :] for t in range(2)]
                u_west = [u_ref[t, at(p, -1), :] for t in range(2)]
                v = [v_ref[t, at(p), :] for t in range(2)]
                v_south, v_north, u_north = south(*v), north(*v), north(*u)
                for t in range(2):
                    u_north_ref[t, at(p), :] = u_north[t]
                for t in range(2):
                    u_north_west = u_north_ref[t, at(p, -1), :]
                    spread = (u[t] - u_west[t]) + (v[t] - v_south[t])
                    spread_north = (u_north[t] - u_north_west) + (v_north[t] - v[t])
                    eta_ref[t, at(p), :] = eta_ref[t, at(p), :] - tw_ref[t, at(p), :] * spread
                    eta_north_ref[t, at(p), :] = (
                        eta_north_ref[t, at(p), :] - tw_north_ref[t, at(p), :] * spread_north
                    )
                    q_ref[t, at(p), :] = v[t] + v_south[t]
                    t_ref[t, at(p), :] = (u[t] + u_west[t]) + (u_north[t] + u_north_west)
            for p in range(first, last):
                eta = [eta_ref[t, at(p), :] for t in range(2)]
                eta_north = [eta_north_ref[t, at(p), :] for t in range(2)]
                for t in range(2):
                    vbar = q_ref[t, at(p), :] + q_ref[t, at(p, 1), :]
                    rise_u = eta_ref[t, at(p, 1), :] - eta[t]
                    rise_v = eta_north[t] - eta[t]
                    next_u = (u_ref[t, at(p), :] + fu_ref[t, at(p), :]) + (
                        cu_ref[t, at(p), :] * vbar - du_ref[t, at(p), :] * rise_u
                    )
                    next_v = (v_ref[t, at(p), :] + fv_ref[t, at(p), :]) - (
                        cv_ref[t, at(p), :] * t_ref[t, at(p), :] + dv_ref[t, at(p), :] * rise_v
                    )
                    u_ref[t, at(p), :] = next_u
                    v_ref[t, at(p), :] = next_v
                    if p == REACH and t == 0:
                        total_u, total_v = total_u + next_u, total_v + next_v
            return total_u, total_v

        return body

    carry = (zero, zero)
    done = 0
    for ring in range(REACH):
        until = SUBSTEPS - COLS * (REACH - 1 - ring)
        carry = lax.fori_loop(0, until - done, substep(ring, BLOCKS - ring), carry, unroll=2)
        done = until
    out_eta[...] = eta_ref[0, at(REACH), :]
    water = [w_ref[t, at(REACH), :] for t in range(2)]
    open_u = jnp.minimum(water[0], w_ref[0, at(REACH, 1), :])
    open_v = jnp.minimum(water[0], north(*water)[0])
    star_u = flow_u + (STEP / tau) * fu_ref[0, at(REACH), :]
    star_v = flow_v + (STEP / tau) * fv_ref[0, at(REACH), :]
    lift_u = (carry[0] / SUBSTEPS - star_u) / jnp.maximum(depth_of(open_u, levels), 0.25)
    lift_v = (carry[1] / SUBSTEPS - star_v) / jnp.maximum(depth_of(open_v, levels), 0.25)
    for k in range(levels):
        out_u[level(k), :] = su_ref[level(k), :] + jnp.where(open_u > float(k), lift_u, 0.0)
        out_v[level(k), :] = sv_ref[level(k), :] + jnp.where(open_v > float(k), lift_v, 0.0)


def call(kernel, shapes, scratch, *operands, **specs):
    return pl.pallas_call(
        kernel,
        out_shape=[jax.ShapeDtypeStruct(s, jnp.float32) for s in shapes],
        scratch_shapes=[pltpu.VMEM(s, jnp.float32) if isinstance(s, tuple) else s for s in scratch],
        compiler_params=pltpu.CompilerParams(vmem_limit_bytes=VMEM_BYTES),
        **specs,
    )(*operands)


def swap(x, axis, first, hop, wraps):
    count = lax.axis_size(axis)
    pairs = []
    for i in range(first, count, 2):
        j = i + hop
        if wraps or 0 <= j < count:
            pairs += [(i, j % count), (j % count, i)]
    return lax.ppermute(x, axis, pairs)


def local(velocity_u, velocity_v, buoyancy, wind_x, wind_y, free_surface, land_sea, bottom_level):
    levels = velocity_u.shape[0]
    flat = (levels * COLS, LANES)
    u, v, b = (a.reshape(flat) for a in (velocity_u, velocity_v, buoyancy))
    inputs = (u, v, b, land_sea, bottom_level, free_surface, wind_x, wind_y)
    edge, tile = (2 * levels + COLS, LANES), (COLS, LANES)
    whole = pltpu.VMEM(tile, jnp.int32)
    col_a, col_z, row_a, row_z, u, v, p, planes = call(
        pack_edges_kernel,
        [edge, edge, tile, tile, flat, flat, flat, (4 * COLS, LANES)],
        [flat, whole, whole, pltpu.SemaphoreType.DMA((len(inputs),))],
        *[pltpu.with_memory_space_constraint(a, pltpu.HBM) for a in inputs],
        in_specs=[pl.BlockSpec(memory_space=pltpu.HBM)] * len(inputs),
    )
    col_z = swap(col_z, "lon", 1, 1, True)
    col_a = swap(col_a, "lon", 0, 1, True)
    row_z = swap(row_z, "lat", 1, 1, False)
    row_a = swap(row_a, "lat", 0, 1, False)
    x, star_u, star_v = call(
        levels_kernel, [(BLOCK_ROWS, LANES), flat, flat], [edge, edge],
        u, v, p, planes, col_z, col_a, row_z, row_a,
    )
    far_z = swap(x, "lon", 1, 3, True)
    far_a = swap(x, "lon", 0, 3, True)
    y = jnp.concatenate([far_z, x, far_a], 0)
    near_z = swap(y, "lon", 1, 1, True)
    near_a = swap(y, "lon", 0, 1, True)
    rims = (RIM_TILES * COLS, LANES)
    own, rim_a, rim_z = call(
        pack_rims_kernel, [(FIELDS * BLOCKS * COLS, LANES), rims, rims], [], y, near_a, near_z
    )
    rim_z = swap(rim_z, "lat", 1, 1, False)
    rim_a = swap(rim_a, "lat", 0, 1, False)
    state = (2, (2 * REACH + 3) * COLS, LANES)
    new_u, new_v, surface = call(
        substeps_kernel, [flat, flat, tile], [state] * 16, own, rim_z, rim_a, star_u, star_v
    )
    return new_u.reshape(velocity_u.shape), new_v.reshape(velocity_v.shape), surface


def solution(mesh):
    return jax.shard_map(
        local,
        mesh=mesh,
        in_specs=(P(None, "lon", "lat"),) * 3 + (P("lon", "lat"),) * 5,
        out_specs=(P(None, "lon", "lat"), P(None, "lon", "lat"), P("lon", "lat")),
        check_vma=False,
    )
```

time: 65.9 us -> 68.4 us (1.038)
  the two profiles are of different devices: /device:TPU:40 before, /device:TPU:1 now
where the time goes in v6:
time: 68.4 us; the launch traced here: 67.9 us
  starting transfers between devices  50.2 us (73%)
  waiting for transfers between devices  9.97 us (15%)
  Pallas kernels  7.03 us (10%)
  between operations  0.76 us (1%)
    ppermute x10, starting transfers between devices, swap(): return lax.ppermute(x, axis, pairs)  50.2 us
    ppermute x10, waiting for transfers between devices, swap(): return lax.ppermute(x, axis, pairs)  9.97 us
    pallas_call x4, Pallas kernels, call(): pl.pallas_call(kernel, out_shape=[jax.ShapeDtypeStruct(s, jnp.float32) fo...  7.03 us
  transfers between devices with their start and end apart: 10, of which 5 were waited for; matrix products, arithmetic and copies ran while one was open for 0% of the time, Pallas kernels for 0%

profile of v6, /device:TPU:1, one launch (start us, length us, event | category | flops | bytes accessed | tf_op | source)
XLA Modules:
  0.0 67.9 jit_solution(17778829409296829213)
XLA Ops:
  0.6 1.5 %shard_map.103 = (f32[104,128]{1,0:T(8,128)S(1)}, f32[104,128]{1,0:T(8,128)S(1)}, f32[8,128]{1,0:T(8,128)S(1)}, f32[8,128]{1,0:T(8,128)S(1)}, f32[384,128]{1,0:T...) custom-call(f32[384,128]{1,0:T(8,128)} %bitcast.5, f32[384,128]{1,0:T(8,128)} %bitcast.6, ...), custom_call_target="tpu_custom_call" | custom-call | tf_op jit(solution)/shard_map/pallas_call | solution.py:323
  2.1 21.4 %collective-permute-start = (f32[104,128]{1,0:T(8,128)S(1)}, f32[104,128]{1,0:T(8,128)S(1)}, u32[]{:S(2)}, u32[]{:S(2)}) collective-permute-start(f32[104,128]{1,0:T(8,128)S(1)} %get-tuple-element.24), channel_id=1, source_target_pairs={{8,16},{16,8},{24,32},{32,24},{40,48},{48,40},{56,64},{64,56},{72,... | collective-permute-start | bytes 159752 | tf_op jit(solution)/shard_map/ppermute | solution.py:339
  23.6 1.9 %collective-permute-start.1 = (f32[104,128]{1,0:T(8,128)S(1)}, f32[104,128]{1,0:T(8,128)S(1)}, u32[]{:S(2)}, u32[]{:S(2)}) collective-permute-start(f32[104,128]{1,0:T(8,128)S(1)} %get-tuple-element.25), channel_id=1, source_target_pairs={{0,8},{8,0},{16,24},{24,16},{32,40},{40,32},{48,56},{56,48},{64,72... | collective-permute-start | bytes 159752 | tf_op jit(solution)/shard_map/ppermute | solution.py:339
  25.5 4.0 %collective-permute-start.2 = (f32[8,128]{1,0:T(8,128)S(1)}, f32[8,128]{1,0:T(8,128)S(1)}, u32[]{:S(2)}, u32[]{:S(2)}) collective-permute-start(f32[8,128]{1,0:T(8,128)S(1)} %get-tuple-element.26), channel_id=1, source_target_pairs={{1,2},{2,1},{3,4},{4,3},{5,6},{6,5},{9,10},{10,9},{11,12},{12,11},... | collective-permute-start | bytes 12296 | tf_op jit(solution)/shard_map/ppermute | solution.py:339
  29.5 1.9 %collective-permute-start.3 = (f32[8,128]{1,0:T(8,128)S(1)}, f32[8,128]{1,0:T(8,128)S(1)}, u32[]{:S(2)}, u32[]{:S(2)}) collective-permute-start(f32[8,128]{1,0:T(8,128)S(1)} %get-tuple-element.27), channel_id=1, source_target_pairs={{0,1},{1,0},{2,3},{3,2},{4,5},{5,4},{6,7},{7,6},{8,9},{9,8},{10,11... | collective-permute-start | bytes 12296 | tf_op jit(solution)/shard_map/ppermute | solution.py:339
  31.5 0.0 collective-permute-done.2.row_z
  31.5 1.1 %collective-permute-done.3.row_a = f32[8,128]{1,0:T(8,128)S(1)} collective-permute-done((f32[8,128]{1,0:T(8,128)S(1)}, f32[8,128]{1,0:T(8,128)S(1)}, u32[]{:S(2)}, u32[]{:S(2)}) %collective-permute-start.3) | collective-permute-done | bytes 4128 | tf_op jit(solution)/shard_map/ppermute | solution.py:339
  32.6 0.0 collective-permute-done.col_z
  32.6 0.0 collective-permute-done.1.col_a
  32.6 0.5 shard_map.104
  33.1 5.7 %collective-permute-start.4 = (f32[48,128]{1,0:T(8,128)S(1)}, f32[48,128]{1,0:T(8,128)S(1)}, u32[]{:S(2)}, u32[]{:S(2)}) collective-permute-start(f32[48,128]{1,0:T(8,128)S(1)} %get-tuple-element.28), channel_id=1, source_target_pairs={{8,32},{32,8},{24,48},{48,24},{40,64},{64,40},{56,80},{80,56},{72,... | collective-permute-start | bytes 73736 | tf_op jit(solution)/shard_map/ppermute | solution.py:339
  38.9 1.9 %collective-permute-start.5 = (f32[48,128]{1,0:T(8,128)S(1)}, f32[48,128]{1,0:T(8,128)S(1)}, u32[]{:S(2)}, u32[]{:S(2)}) collective-permute-start(f32[48,128]{1,0:T(8,128)S(1)} %get-tuple-element.28), channel_id=1, source_target_pairs={{0,24},{24,0},{16,40},{40,16},{32,56},{56,32},{48,72},{72,48},{64,... | collective-permute-start | bytes 73736 | tf_op jit(solution)/shard_map/ppermute | solution.py:339
  40.8 2.0 %collective-permute-done.4 = f32[48,128]{1,0:T(8,128)S(1)} collective-permute-done((f32[48,128]{1,0:T(8,128)S(1)}, f32[48,128]{1,0:T(8,128)S(1)}, u32[]{:S(2)}, u32[]{:S(2)}) %collective-permute-start.4) | collective-permute-done | bytes 24608 | tf_op jit(solution)/shard_map/ppermute | solution.py:339
  42.8 2.5 %collective-permute-done.5 = f32[48,128]{1,0:T(8,128)S(1)} collective-permute-done((f32[48,128]{1,0:T(8,128)S(1)}, f32[48,128]{1,0:T(8,128)S(1)}, u32[]{:S(2)}, u32[]{:S(2)}) %collective-permute-start.5) | collective-permute-done | bytes 24608 | tf_op jit(solution)/shard_map/ppermute | solution.py:339
  45.3 2.1 %collective-permute-start.7 = (f32[144,128]{1,0:T(8,128)S(1)}, f32[144,128]{1,0:T(8,128)S(1)}, u32[]{:S(2)}, u32[]{:S(2)}) collective-permute-start(f32[144,128]{1,0:T(8,128)S(1)} %constant_dynamic-update-slice_fusion.y_ref), channel_id=1, source_target_pairs={{8,16},{16,8},{24,32},{32,24},{40,48},{48,40},{56,64},{64,56},{72,... | collective-permute-start | bytes 221192 | tf_op jit(solution)/shard_map/ppermute | solution.py:339
  47.5 3.2 %collective-permute-start.6 = (f32[144,128]{1,0:T(8,128)S(1)}, f32[144,128]{1,0:T(8,128)S(1)}, u32[]{:S(2)}, u32[]{:S(2)}) collective-permute-start(f32[144,128]{1,0:T(8,128)S(1)} %constant_dynamic-update-slice_fusion.y_ref), channel_id=1, source_target_pairs={{0,8},{8,0},{16,24},{24,16},{32,40},{40,32},{48,56},{56,48},{64,72... | collective-permute-start | bytes 221192 | tf_op jit(solution)/shard_map/ppermute | solution.py:339
  50.6 3.1 %collective-permute-done.7.z_in = f32[144,128]{1,0:T(8,128)S(1)} collective-permute-done((f32[144,128]{1,0:T(8,128)S(1)}, f32[144,128]{1,0:T(8,128)S(1)}, u32[]{:S(2)}, u32[]{:S(2)}) %collective-permute-start.7) | collective-permute-done | bytes 73760 | tf_op jit(solution)/shard_map/ppermute | solution.py:339
  53.7 0.0 collective-permute-done.6.a_in
  53.7 0.2 shard_map.105
  53.9 6.0 %collective-permute-start.8 = (f32[112,128]{1,0:T(8,128)S(1)}, f32[112,128]{1,0:T(8,128)S(1)}, u32[]{:S(2)}, u32[]{:S(2)}) collective-permute-start(f32[112,128]{1,0:T(8,128)S(1)} %get-tuple-element.30), channel_id=1, source_target_pairs={{1,2},{2,1},{3,4},{4,3},{5,6},{6,5},{9,10},{10,9},{11,12},{12,11},... | collective-permute-start | bytes 172040 | tf_op jit(solution)/shard_map/ppermute | solution.py:339
  59.9 1.9 %collective-permute-start.9 = (f32[112,128]{1,0:T(8,128)S(1)}, f32[112,128]{1,0:T(8,128)S(1)}, u32[]{:S(2)}, u32[]{:S(2)}) collective-permute-start(f32[112,128]{1,0:T(8,128)S(1)} %get-tuple-element.31), channel_id=1, source_target_pairs={{0,1},{1,0},{2,3},{3,2},{4,5},{5,4},{6,7},{7,6},{8,9},{9,8},{10,11... | collective-permute-start | bytes 172040 | tf_op jit(solution)/shard_map/ppermute | solution.py:339
  61.9 0.0 collective-permute-done.8.z_in
  61.9 1.2 %collective-permute-done.9.a_in = f32[112,128]{1,0:T(8,128)S(1)} collective-permute-done((f32[112,128]{1,0:T(8,128)S(1)}, f32[112,128]{1,0:T(8,128)S(1)}, u32[]{:S(2)}, u32[]{:S(2)}) %collective-permute-start.9) | collective-permute-done | bytes 57376 | tf_op jit(solution)/shard_map/ppermute | solution.py:339
  63.1 4.9 %shard_map.106 = (f32[384,128]{1,0:T(8,128)}, f32[384,128]{1,0:T(8,128)}, f32[8,128]{1,0:T(8,128)}) custom-call(f32[432,128]{1,0:T(8,128)S(1)} %get-tuple-element.29.own_ref, f32[112,128]{1,0:T(8,128)S(1)} %collective-permute-done.8.z_in, f32[112,128]{1,0:T(8,128)S(1)} %collective-permute-done.9.a_in, f32[384,128]{1,0:T(8,128)S(1)} %get-tuple-element.32.su_ref, ...), custom_call_target="tpu_custom_call" | custom-call | tf_op jit(solution)/shard_map/pallas_call | solution.py:323
  (3 shorter events, 0.0 us)
Async XLA Ops:
  2.1 30.5 %collective-permute-start = (f32[104,128]{1,0:T(8,128)S(1)}, f32[104,128]{1,0:T(8,128)S(1)}, u32[]{:S(2)}, u32[]{:S(2)}) collective-permute-start(f32[104,128]{1,0:T(8,128)S(1)} %get-tuple-element.24), channel_id=1, source_target_pairs={{8,16},{16,8},{24,32},{32,24},{40,48},{48,40},{56,64},{64,56},{72,... | collective-permute-start | bytes 159752 | tf_op jit(solution)/shard_map/ppermute | solution.py:339
  23.6 9.0 %collective-permute-start.1 = (f32[104,128]{1,0:T(8,128)S(1)}, f32[104,128]{1,0:T(8,128)S(1)}, u32[]{:S(2)}, u32[]{:S(2)}) collective-permute-start(f32[104,128]{1,0:T(8,128)S(1)} %get-tuple-element.25), channel_id=1, source_target_pairs={{0,8},{8,0},{16,24},{24,16},{32,40},{40,32},{48,56},{56,48},{64,72... | collective-permute-start | bytes 159752 | tf_op jit(solution)/shard_map/ppermute | solution.py:339
  25.5 6.0 %collective-permute-start.2 = (f32[8,128]{1,0:T(8,128)S(1)}, f32[8,128]{1,0:T(8,128)S(1)}, u32[]{:S(2)}, u32[]{:S(2)}) collective-permute-start(f32[8,128]{1,0:T(8,128)S(1)} %get-tuple-element.26), channel_id=1, source_target_pairs={{1,2},{2,1},{3,4},{4,3},{5,6},{6,5},{9,10},{10,9},{11,12},{12,11},... | collective-permute-start | bytes 12296 | tf_op jit(solution)/shard_map/ppermute | solution.py:339
  29.5 3.1 %collective-permute-start.3 = (f32[8,128]{1,0:T(8,128)S(1)}, f32[8,128]{1,0:T(8,128)S(1)}, u32[]{:S(2)}, u32[]{:S(2)}) collective-permute-start(f32[8,128]{1,0:T(8,128)S(1)} %get-tuple-element.27), channel_id=1, source_target_pairs={{0,1},{1,0},{2,3},{3,2},{4,5},{5,4},{6,7},{7,6},{8,9},{9,8},{10,11... | collective-permute-start | bytes 12296 | tf_op jit(solution)/shard_map/ppermute | solution.py:339
  33.1 9.7 %collective-permute-start.4 = (f32[48,128]{1,0:T(8,128)S(1)}, f32[48,128]{1,0:T(8,128)S(1)}, u32[]{:S(2)}, u32[]{:S(2)}) collective-permute-start(f32[48,128]{1,0:T(8,128)S(1)} %get-tuple-element.28), channel_id=1, source_target_pairs={{8,32},{32,8},{24,48},{48,24},{40,64},{64,40},{56,80},{80,56},{72,... | collective-permute-start | bytes 73736 | tf_op jit(solution)/shard_map/ppermute | solution.py:339
  38.9 6.5 %collective-permute-start.5 = (f32[48,128]{1,0:T(8,128)S(1)}, f32[48,128]{1,0:T(8,128)S(1)}, u32[]{:S(2)}, u32[]{:S(2)}) collective-permute-start(f32[48,128]{1,0:T(8,128)S(1)} %get-tuple-element.28), channel_id=1, source_target_pairs={{0,24},{24,0},{16,40},{40,16},{32,56},{56,32},{48,72},{72,48},{64,... | collective-permute-start | bytes 73736 | tf_op jit(solution)/shard_map/ppermute | solution.py:339
  45.3 8.4 %collective-permute-start.7 = (f32[144,128]{1,0:T(8,128)S(1)}, f32[144,128]{1,0:T(8,128)S(1)}, u32[]{:S(2)}, u32[]{:S(2)}) collective-permute-start(f32[144,128]{1,0:T(8,128)S(1)} %constant_dynamic-update-slice_fusion.y_ref), channel_id=1, source_target_pairs={{8,16},{16,8},{24,32},{32,24},{40,48},{48,40},{56,64},{64,56},{72,... | collective-permute-start | bytes 221192 | tf_op jit(solution)/shard_map/ppermute | solution.py:339
  47.5 6.3 %collective-permute-start.6 = (f32[144,128]{1,0:T(8,128)S(1)}, f32[144,128]{1,0:T(8,128)S(1)}, u32[]{:S(2)}, u32[]{:S(2)}) collective-permute-start(f32[144,128]{1,0:T(8,128)S(1)} %constant_dynamic-update-slice_fusion.y_ref), channel_id=1, source_target_pairs={{0,8},{8,0},{16,24},{24,16},{32,40},{40,32},{48,56},{56,48},{64,72... | collective-permute-start | bytes 221192 | tf_op jit(solution)/shard_map/ppermute | solution.py:339
  53.9 7.9 %collective-permute-start.8 = (f32[112,128]{1,0:T(8,128)S(1)}, f32[112,128]{1,0:T(8,128)S(1)}, u32[]{:S(2)}, u32[]{:S(2)}) collective-permute-start(f32[112,128]{1,0:T(8,128)S(1)} %get-tuple-element.30), channel_id=1, source_target_pairs={{1,2},{2,1},{3,4},{4,3},{5,6},{6,5},{9,10},{10,9},{11,12},{12,11},... | collective-permute-start | bytes 172040 | tf_op jit(solution)/shard_map/ppermute | solution.py:339
  59.9 3.1 %collective-permute-start.9 = (f32[112,128]{1,0:T(8,128)S(1)}, f32[112,128]{1,0:T(8,128)S(1)}, u32[]{:S(2)}, u32[]{:S(2)}) collective-permute-start(f32[112,128]{1,0:T(8,128)S(1)} %get-tuple-element.31), channel_id=1, source_target_pairs={{0,1},{1,0},{2,3},{3,2},{4,5},{5,4},{6,7},{7,6},{8,9},{9,8},{10,11... | collective-permute-start | bytes 172040 | tf_op jit(solution)/shard_map/ppermute | solution.py:339

commit v7 on v5

--- a/solution.py
+++ b/solution.py
@@ -11,7 +11,6 @@
 COLS = 8
 RIM = 32
 SLOTS = 4
-CHUNKS = 4
 REACH = 4
 NEAR_ROWS = 9 * COLS
 FAR_ROWS = 8 * COLS
@@ -59,129 +58,122 @@
 
 
 def strips(parts, shifts):
-    slot = lane_index() // RIM
+    slot = lax.broadcasted_iota(jnp.int32, parts[0].shape, 1) // RIM
     moved = [pltpu.roll(p, s, 1) if s else p for p, s in zip(parts, shifts)]
     return jnp.where(
         slot < 2, jnp.where(slot == 0, moved[0], moved[1]), jnp.where(slot == 2, moved[2], moved[3])
     )
 
 
-def pack_rows_kernel(
+def pack_edges_kernel(
     u_in, v_in, b_in, land_in, bottom_in, eta_in, wx_in, wy_in,
-    a_ref, z_ref, u_ref, v_ref, b_ref, plane_ref, land_ref, bottom_ref, sems, plane_sem,
+    col_a_ref, col_z_ref, u_ref, v_ref, p_ref, plane_ref,
+    b_ref, land_ref, bottom_ref, sems,
 ):
     levels = u_in.shape[0] // COLS
-    groups = levels // SLOTS
-    chunks = sems.shape[0]
-    fields = ((u_in, u_ref), (v_in, v_ref), (b_in, b_ref))
-    part = u_in.shape[0] // chunks
+    thick = thickness(levels)
     copies = [
-        [
-            pltpu.make_async_copy(src.at[pl.ds(c * part, part)], dst.at[pl.ds(c * part, part)], sems.at[c, f])
-            for f, (src, dst) in enumerate(fields)
-        ]
-        for c in range(chunks)
-    ]
-    planes = [
-        pltpu.make_async_copy(src, dst, plane_sem.at[i])
+        pltpu.make_async_copy(src, dst, sems.at[i])
         for i, (src, dst) in enumerate(
             (
-                (land_in, land_ref), (bottom_in, bottom_ref), (eta_in, plane_ref.at[level(1)]),
-                (wx_in, plane_ref.at[level(2)]), (wy_in, plane_ref.at[level(3)]),
+                (u_in, u_ref), (v_in, v_ref), (b_in, b_ref), (land_in, land_ref), (bottom_in, bottom_ref),
+                (eta_in, plane_ref.at[level(1)]), (wx_in, plane_ref.at[level(2)]), (wy_in, plane_ref.at[level(3)]),
             )
         )
     ]
-    for copy in sum(copies, []) + planes:
+    for copy in copies:
         copy.start()
+    for copy in copies:
+        copy.wait()
+    water = (land_ref[...] * bottom_ref[...]).astype(jnp.float32)
+    plane_ref[level(0), :] = water
+    p = jnp.zeros((COLS, LANES), jnp.float32)
+    for k in range(levels):
+        p = p + float(thick[k]) * b_ref[level(k), :]
+        p_ref[level(k), :] = p
+
+    def edge(ref, col):
+        return ref[pl.ds(col, levels, stride=COLS), :]
+
+    def store(col, out_ref):
+        first = edge(u_ref, col)
+        out_ref[pl.ds(0, levels), :] = first if col else 0.05 * first - edge(p_ref, col)
+        out_ref[pl.ds(levels, levels), :] = edge(v_ref, col)
+        out_ref[pl.ds(2 * levels, COLS), :] = water
+
+    even_col = is_even("lon")
+
+    @pl.when(even_col)
+    def _():
+        store(COLS - 1, col_a_ref)
+        store(0, col_z_ref)
+
+    @pl.when(jnp.logical_not(even_col))
+    def _():
+        store(0, col_a_ref)
+        store(COLS - 1, col_z_ref)
+
+
+def pack_rows_kernel(u_ref, v_ref, p_ref, plane_ref, a_ref, z_ref):
     even = is_even("lat")
+    groups = u_ref.shape[0] // COLS // SLOTS
 
     def send(at, parts):
         upper, lower = strips(parts, (32, 64, 96, 0)), strips(parts, (0, 32, 64, 96))
         a_ref[level(at), :] = jnp.where(even, upper, lower)
         z_ref[level(at), :] = jnp.where(even, lower, upper)
 
-    for c in range(chunks):
-        for f, (_, ref) in enumerate(fields):
-            copies[c][f].wait()
-            for g in range(c * groups // chunks, (c + 1) * groups // chunks):
-                send(f * groups + g, [ref[level(SLOTS * g + s), :] for s in range(SLOTS)])
-    for copy in planes:
-        copy.wait()
-    plane_ref[level(0), :] = (land_ref[...] * bottom_ref[...]).astype(jnp.float32)
+    for f, ref in enumerate((u_ref, v_ref, p_ref)):
+        for g in range(groups):
+            send(f * groups + g, [ref[level(SLOTS * g + s), :] for s in range(SLOTS)])
     send(3 * groups, [plane_ref[level(s), :] for s in range(SLOTS)])
 
 
-def pack_cols_kernel(
-    u_ref, v_ref, b_ref, plane_ref, z_in, a_in,
-    a_ref, z_ref, hu_ref, hv_ref, hplane_ref, p_ref, hp_ref,
-):
-    even = is_even("lat")
-    upper = lane_index() < LANES // 2
-    levels = u_ref.shape[0] // COLS
-    thick = thickness(levels)
-    groups = levels // SLOTS
-
-    def receive(at, s):
-        a, z = a_in[level(at), :], z_in[level(at), :]
-        n, o = jnp.where(even, a, z), jnp.where(even, z, a)
-        to_first, to_last = (LANES - RIM * s) % LANES, (LANES - RIM - RIM * s) % LANES
-        n = pltpu.roll(n, to_first, 1) if to_first else n
-        o = pltpu.roll(o, to_last, 1) if to_last else o
-        return jnp.where(upper, n, o)
-
-    own = rim = jnp.zeros((COLS, LANES), jnp.float32)
-    for k in range(levels):
-        dz = float(thick[k])
-        hu_ref[level(k), :] = receive(k // SLOTS, k % SLOTS)
-        hv_ref[level(k), :] = receive(groups + k // SLOTS, k % SLOTS)
-        own = own + dz * b_ref[level(k), :]
-        rim = rim + dz * receive(2 * groups + k // SLOTS, k % SLOTS)
-        p_ref[level(k), :] = own
-        hp_ref[level(k), :] = rim
-    for s in range(SLOTS):
-        hplane_ref[level(s), :] = receive(3 * groups, s)
-
-    def edge(ref, col):
-        return ref[pl.ds(col, levels, stride=COLS), :]
-
-    def store(col, out_ref):
-        own, rim = edge(u_ref, col), edge(hu_ref, col)
-        if col == 0:
-            own, rim = 0.05 * own - edge(p_ref, col), 0.05 * rim - edge(hp_ref, col)
-        out_ref[pl.ds(0, levels), :] = own
-        out_ref[pl.ds(levels, levels), :] = edge(v_ref, col)
-        out_ref[pl.ds(2 * levels, levels), :] = pair_rims(rim, edge(hv_ref, col))
-        out_ref[pl.ds(3 * levels, 1), :] = plane_ref[pl.ds(col, 1), :]
-        out_ref[pl.ds(3 * levels + 1, 1), :] = hplane_ref[pl.ds(col, 1), :]
-        out_ref[pl.ds(3 * levels + 2, 6), :] = jnp.zeros((6, LANES), jnp.float32)
-
-    even_col = is_even("lon")
-
-    @pl.when(even_col)
-    def _():
-        store(COLS - 1, a_ref)
-        store(0, z_ref)
-
-    @pl.when(jnp.logical_not(even_col))
-    def _():
-        store(0, a_ref)
-        store(COLS - 1, z_ref)
+def pack_corners_kernel(rows_a, rows_z, col_z, col_a, a_ref, z_ref):
+    even_row, even_col = is_even("lat"), is_even("lon")
+    a, z = col_a[...], col_z[...]
+    east, west = jnp.where(even_col, a, z), jnp.where(even_col, z, a)
+    levels = (a.shape[0] - COLS) // 2
+    done = rows_a.shape[0]
+    a_ref[pl.ds(0, done), :] = rows_a[...]
+    z_ref[pl.ds(0, done), :] = rows_z[...]
+
+    def send(at, parts):
+        upper, lower = strips(parts, (32, 64, 96, 0)), strips(parts, (0, 32, 64, 96))
+        a_ref[pl.ds(at, parts[0].shape[0]), :] = jnp.where(even_row, upper, lower)
+        z_ref[pl.ds(at, parts[0].shape[0]), :] = jnp.where(even_row, lower, upper)
+
+    send(done, [east[:levels], east[levels : 2 * levels], west[:levels], west[levels : 2 * levels]])
+    send(done + levels, [east[2 * levels :]] * SLOTS)
 
 
 def levels_kernel(
-    u_ref, v_ref, hu_ref, hv_ref, p_ref, hp_ref, plane_ref, hplane_ref, z_in, a_in,
+    u_ref, v_ref, p_ref, plane_ref, col_z, col_a, z_in, a_in,
     far_ref, x_ref, su_ref, sv_ref, east_ref, west_ref,
 ):
     levels = u_ref.shape[0] // COLS
     thick = thickness(levels)
-    even = is_even("lon")
-    a, z = a_in[...], z_in[...]
+    groups = levels // SLOTS
+    even_col, even_row = is_even("lon"), is_even("lat")
+
+    def receive(at, s, rows=COLS):
+        a, z = a_in[pl.ds(at, rows), :], z_in[pl.ds(at, rows), :]
+        n, o = jnp.where(even_row, a, z), jnp.where(even_row, z, a)
+        n = pltpu.roll(n, LANES - RIM * s, 1) if s else n
+        o = pltpu.roll(o, LANES - RIM - RIM * s, 1) if s < SLOTS - 1 else o
+        return jnp.where(lax.broadcasted_iota(jnp.int32, (rows, LANES), 1) < LANES // 2, n, o)
+
+    a, z = col_a[...], col_z[...]
     rows = a.shape[0]
-    east_ref[pl.ds(0, rows), :] = jnp.where(even, a, z)
-    west_ref[pl.ds(0, rows), :] = jnp.where(even, z, a)
-    for ref in (east_ref, west_ref):
-        ref[pl.ds(rows, levels), :] = pltpu.roll(ref[pl.ds(2 * levels, levels), :], LANES // 2, 1)
-    U, V, W = (0, 2 * levels), (levels, rows), (3 * levels, 3 * levels + 1)
+    corners = (3 * groups + 1) * COLS
+    for i, (ref, value) in enumerate(
+        ((east_ref, jnp.where(even_col, a, z)), (west_ref, jnp.where(even_col, z, a)))
+    ):
+        ref[pl.ds(0, rows), :] = value
+        ref[pl.ds(rows, levels), :] = receive(corners, 2 * i, levels)
+        ref[pl.ds(rows + levels, levels), :] = receive(corners, 2 * i + 1, levels)
+        ref[pl.ds(rows + 2 * levels, COLS), :] = receive(corners + levels, 0)
+    U, V, W = (0, rows), (levels, rows + levels), (2 * levels, rows + 2 * levels)
     col = col_index()
     top_col, bottom_col = col == COLS - 1, col == 0
 
@@ -198,7 +190,7 @@
             jnp.where(bottom_col, row(west_ref, at + k), pltpu.roll(x, 1, 0)) for x, at in zip(pair, places)
         ]
 
-    water, eta, wx, wy = [(plane_ref[level(i), :], hplane_ref[level(i), :]) for i in range(SLOTS)]
+    water, eta, wx, wy = [(plane_ref[level(i), :], receive(3 * groups * COLS, i)) for i in range(SLOTS)]
     open_u = [jnp.minimum(w, e) for w, e in zip(water, east(water, W, 0))]
     open_v = [jnp.minimum(w, n) for w, n in zip(water, north(*water))]
     zero = jnp.zeros((COLS, LANES), jnp.float32)
@@ -206,9 +198,10 @@
     flow_u, flow_v = [zero, zero], [zero, zero]
     for k in range(levels):
         dz = float(thick[k])
-        u = (u_ref[level(k), :], hu_ref[level(k), :])
-        v = (v_ref[level(k), :], hv_ref[level(k), :])
-        p = (p_ref[level(k), :], hp_ref[level(k), :])
+        u, v, p = [
+            (ref[level(k), :], receive((f * groups + k // SLOTS) * COLS, k % SLOTS))
+            for f, ref in enumerate((u_ref, v_ref, p_ref))
+        ]
         push_east = east([0.05 * u[t] - p[t] for t in range(2)], U, k)
         around_u = list(zip(west(u, U, k), north(*u), south(*u)))
         around_v = list(zip(east(v, V, k), west(v, V, k), north(*v), south(*v)))
@@ -405,30 +398,29 @@
     levels = velocity_u.shape[0]
     flat = (levels * COLS, LANES)
     u, v, b = (a.reshape(flat) for a in (velocity_u, velocity_v, buoyancy))
-    send = (3 * levels // SLOTS * COLS + COLS, LANES)
     inputs = (u, v, b, land_sea, bottom_level, free_surface, wind_x, wind_y)
-    whole = pltpu.VMEM((COLS, LANES), jnp.int32)
-    rows_a, rows_z, u, v, b, planes = call(
-        pack_rows_kernel,
-        [send, send, flat, flat, flat, (SLOTS * COLS, LANES)],
-        [whole, whole, pltpu.SemaphoreType.DMA((CHUNKS, 3)), pltpu.SemaphoreType.DMA((5,))],
+    edge, tile = (2 * levels + COLS, LANES), (COLS, LANES)
+    whole = pltpu.VMEM(tile, jnp.int32)
+    col_a, col_z, u, v, p, planes = call(
+        pack_edges_kernel,
+        [edge, edge, flat, flat, flat, (SLOTS * COLS, LANES)],
+        [flat, whole, whole, pltpu.SemaphoreType.DMA((len(inputs),))],
         *[pltpu.with_memory_space_constraint(a, pltpu.HBM) for a in inputs],
-        in_specs=[pl.BlockSpec(memory_space=pltpu.HBM)] * 8,
+        in_specs=[pl.BlockSpec(memory_space=pltpu.HBM)] * len(inputs),
+    )
+    col_z = swap(col_z, "lon", 1, 1, True)
+    col_a = swap(col_a, "lon", 0, 1, True)
+    rims = (3 * levels // SLOTS + 1) * COLS
+    rows_a, rows_z = call(pack_rows_kernel, [(rims, LANES)] * 2, [], u, v, p, planes)
+    rows_a, rows_z = call(
+        pack_corners_kernel, [(rims + levels + COLS, LANES)] * 2, [], rows_a, rows_z, col_z, col_a
     )
     rows_z = swap(rows_z, "lat", 1, 1, False)
     rows_a = swap(rows_a, "lat", 0, 1, False)
-    edge = (3 * levels + 8, LANES)
-    cols_a, cols_z, hu, hv, hplanes, p, hp = call(
-        pack_cols_kernel,
-        [edge, edge, flat, flat, (SLOTS * COLS, LANES), flat, flat], [],
-        u, v, b, planes, rows_z, rows_a,
-    )
-    cols_z = swap(cols_z, "lon", 1, 1, True)
-    cols_a = swap(cols_a, "lon", 0, 1, True)
-    both = (edge[0] + levels, LANES)
+    both = (2 * edge[0], LANES)
     far, x, star_u, star_v = call(
         levels_kernel, [(FAR_ROWS, LANES), (NEAR_ROWS, LANES), flat, flat], [both, both],
-        u, v, hu, hv, p, hp, planes, hplanes, cols_z, cols_a,
+        u, v, p, planes, col_z, col_a, rows_z, rows_a,
     )
     far_z = swap(far, "lon", 1, 3, True)
     far_a = swap(far, "lon", 0, 3, True)

time: 64.6 us -> 66 us (1.022)
  Pallas kernels: 8.09 us -> 9.95 us
    pallas_call x4 -> x5, Pallas kernels: 8.09 us -> 9.95 us  [call(): pl.pallas_call(kernel, out_shape=[jax.ShapeDtypeStruct(s, jnp.float32) fo...]
where the time goes in v7:
time: 66 us; the launch traced here: 65.6 us
  starting transfers between devices  42.3 us (64%)
  waiting for transfers between devices  12.7 us (19%)
  Pallas kernels  9.95 us (15%)
  between operations  0.76 us (1%)
    ppermute x8, starting transfers between devices, swap(): return lax.ppermute(x, axis, pairs)  42.3 us
    ppermute x8, waiting for transfers between devices, swap(): return lax.ppermute(x, axis, pairs)  12.7 us
    pallas_call x5, Pallas kernels, call(): pl.pallas_call(kernel, out_shape=[jax.ShapeDtypeStruct(s, jnp.float32) fo...  9.95 us
  transfers between devices with their start and end apart: 8, of which 5 were waited for; matrix products, arithmetic and copies ran while one was open for 0% of the time, Pallas kernels for 0%

profile of v7, /device:TPU:56, one launch (start us, length us, event | category | flops | bytes accessed | tf_op | source)
XLA Modules:
  0.0 65.6 jit_solution(16857706720384322605)
XLA Ops:
  0.6 1.3 %shard_map.103 = (f32[104,128]{1,0:T(8,128)S(1)}, f32[104,128]{1,0:T(8,128)S(1)}, f32[384,128]{1,0:T(8,128)S(1)}, f32[384,128]{1,0:T(8,128)S(1)}, f32[384,128]{1,0:T(8,128)S(1)}, /*index=5*/f32[32,128]{1,0:T(8,128)S(1)}) custom-call(f32[384,128]{1,0:T(8,128)} %bitcast.5, f32[384,128]{1,0:T(8,128)} %bitcast.6, f32[384,128]{1,0:T(8,128)} %bitcast.7, ...), custom_call_target="tpu_custom_call" | custom-call | tf_op jit(solution)/shard_map/pallas_call | solution.py:378
  1.9 3.8 %collective-permute-start = (f32[104,128]{1,0:T(8,128)S(1)}, f32[104,128]{1,0:T(8,128)S(1)}, u32[]{:S(2)}, u32[]{:S(2)}) collective-permute-start(f32[104,128]{1,0:T(8,128)S(1)} %get-tuple-element.24), channel_id=1, source_target_pairs={{8,16},{16,8},{24,32},{32,24},{40,48},{48,40},{56,64},{64,56},{72,... | collective-permute-start | bytes 159752 | tf_op jit(solution)/shard_map/ppermute | solution.py:394
  5.7 19.1 %collective-permute-start.1 = (f32[104,128]{1,0:T(8,128)S(1)}, f32[104,128]{1,0:T(8,128)S(1)}, u32[]{:S(2)}, u32[]{:S(2)}) collective-permute-start(f32[104,128]{1,0:T(8,128)S(1)} %get-tuple-element.25), channel_id=1, source_target_pairs={{0,8},{8,0},{16,24},{24,16},{32,40},{40,32},{48,56},{56,48},{64,72... | collective-permute-start | bytes 159752 | tf_op jit(solution)/shard_map/ppermute | solution.py:394
  24.8 0.3 shard_map.104
  25.1 0.0 collective-permute-done.col_z
  25.1 1.8 %collective-permute-done.1.col_a = f32[104,128]{1,0:T(8,128)S(1)} collective-permute-done((f32[104,128]{1,0:T(8,128)S(1)}, f32[104,128]{1,0:T(8,128)S(1)}, u32[]{:S(2)}, u32[]{:S(2)}) %collective-permute-start.1) | collective-permute-done | bytes 53280 | tf_op jit(solution)/shard_map/ppermute | solution.py:394
  26.9 0.1 shard_map.105
  27.0 1.9 %collective-permute-start.2 = (f32[352,128]{1,0:T(8,128)S(1)}, f32[352,128]{1,0:T(8,128)S(1)}, u32[]{:S(2)}, u32[]{:S(2)}) collective-permute-start(f32[352,128]{1,0:T(8,128)S(1)} %get-tuple-element.28), channel_id=1, source_target_pairs={{1,2},{2,1},{3,4},{4,3},{5,6},{6,5},{9,10},{10,9},{11,12},{12,11},... | collective-permute-start | bytes 540680 | tf_op jit(solution)/shard_map/ppermute | solution.py:394
  29.0 1.9 %collective-permute-start.3 = (f32[352,128]{1,0:T(8,128)S(1)}, f32[352,128]{1,0:T(8,128)S(1)}, u32[]{:S(2)}, u32[]{:S(2)}) collective-permute-start(f32[352,128]{1,0:T(8,128)S(1)} %get-tuple-element.29), channel_id=1, source_target_pairs={{0,1},{1,0},{2,3},{3,2},{4,5},{5,4},{6,7},{7,6},{8,9},{9,8},{10,11... | collective-permute-start | bytes 540680 | tf_op jit(solution)/shard_map/ppermute | solution.py:394
  30.9 3.0 %collective-permute-done.2.z_in = f32[352,128]{1,0:T(8,128)S(1)} collective-permute-done((f32[352,128]{1,0:T(8,128)S(1)}, f32[352,128]{1,0:T(8,128)S(1)}, u32[]{:S(2)}, u32[]{:S(2)}) %collective-permute-start.2) | collective-permute-done | bytes 180256 | tf_op jit(solution)/shard_map/ppermute | solution.py:394
  33.9 0.0 collective-permute-done.3.a_in
  33.9 3.4 %shard_map.106 = (f32[64,128]{1,0:T(8,128)S(1)}, f32[72,128]{1,0:T(8,128)S(1)}, f32[384,128]{1,0:T(8,128)S(1)}, f32[384,128]{1,0:T(8,128)S(1)}) custom-call(f32[384,128]{1,0:T(8,128)S(1)} %get-tuple-element.20.u_ref, f32[384,128]{1,0:T(8,128)S(1)} %get-tuple-element.21.v_ref, f32[384,128]{1,0:T(8,128)S(1)} %get-tuple-element.22.p_ref, ...), custom_call_target="tpu_custom_call" | custom-call | tf_op jit(solution)/shard_map/pallas_call | solution.py:378
  37.3 1.9 %collective-permute-start.4 = (f32[64,128]{1,0:T(8,128)S(1)}, f32[64,128]{1,0:T(8,128)S(1)}, u32[]{:S(2)}, u32[]{:S(2)}) collective-permute-start(f32[64,128]{1,0:T(8,128)S(1)} %get-tuple-element.30), channel_id=1, source_target_pairs={{8,32},{32,8},{24,48},{48,24},{40,64},{64,40},{56,80},{80,56},{72,... | collective-permute-start | bytes 98312 | tf_op jit(solution)/shard_map/ppermute | solution.py:394
  39.2 7.9 %collective-permute-start.5 = (f32[64,128]{1,0:T(8,128)S(1)}, f32[64,128]{1,0:T(8,128)S(1)}, u32[]{:S(2)}, u32[]{:S(2)}) collective-permute-start(f32[64,128]{1,0:T(8,128)S(1)} %get-tuple-element.30), channel_id=1, source_target_pairs={{0,24},{24,0},{16,40},{40,16},{32,56},{56,32},{48,72},{72,48},{64,... | collective-permute-start | bytes 98312 | tf_op jit(solution)/shard_map/ppermute | solution.py:394
  47.1 0.0 collective-permute-done.4
  47.1 3.3 %collective-permute-done.5 = f32[64,128]{1,0:T(8,128)S(1)} collective-permute-done((f32[64,128]{1,0:T(8,128)S(1)}, f32[64,128]{1,0:T(8,128)S(1)}, u32[]{:S(2)}, u32[]{:S(2)}) %collective-permute-start.5) | collective-permute-done | bytes 32800 | tf_op jit(solution)/shard_map/ppermute | solution.py:394
  50.4 3.8 %collective-permute-start.7 = (f32[200,128]{1,0:T(8,128)S(1)}, f32[200,128]{1,0:T(8,128)S(1)}, u32[]{:S(2)}, u32[]{:S(2)}) collective-permute-start(f32[200,128]{1,0:T(8,128)S(1)} %constant_dynamic-update-slice_fusion.y_ref), channel_id=1, source_target_pairs={{8,16},{16,8},{24,32},{32,24},{40,48},{48,40},{56,64},{64,56},{72,... | collective-permute-start | bytes 307208 | tf_op jit(solution)/shard_map/ppermute | solution.py:394
  54.2 1.9 %collective-permute-start.6 = (f32[200,128]{1,0:T(8,128)S(1)}, f32[200,128]{1,0:T(8,128)S(1)}, u32[]{:S(2)}, u32[]{:S(2)}) collective-permute-start(f32[200,128]{1,0:T(8,128)S(1)} %constant_dynamic-update-slice_fusion.y_ref), channel_id=1, source_target_pairs={{0,8},{8,0},{16,24},{24,16},{32,40},{40,32},{48,56},{56,48},{64,72... | collective-permute-start | bytes 307208 | tf_op jit(solution)/shard_map/ppermute | solution.py:394
  56.2 0.8 %collective-permute-done.7.z_in = f32[200,128]{1,0:T(8,128)S(1)} collective-permute-done((f32[200,128]{1,0:T(8,128)S(1)}, f32[200,128]{1,0:T(8,128)S(1)}, u32[]{:S(2)}, u32[]{:S(2)}) %collective-permute-start.7) | collective-permute-done | bytes 102432 | tf_op jit(solution)/shard_map/ppermute | solution.py:394
  57.0 3.8 %collective-permute-done.6.a_in = f32[200,128]{1,0:T(8,128)S(1)} collective-permute-done((f32[200,128]{1,0:T(8,128)S(1)}, f32[200,128]{1,0:T(8,128)S(1)}, u32[]{:S(2)}, u32[]{:S(2)}) %collective-permute-start.6) | collective-permute-done | bytes 102432 | tf_op jit(solution)/shard_map/ppermute | solution.py:394
  60.8 4.9 %shard_map.107 = (f32[384,128]{1,0:T(8,128)}, f32[384,128]{1,0:T(8,128)}, f32[8,128]{1,0:T(8,128)}) custom-call(f32[200,128]{1,0:T(8,128)S(1)} %constant_dynamic-update-slice_fusion.y_ref, f32[200,128]{1,0:T(8,128)S(1)} %collective-permute-done.6.a_in, f32[200,128]{1,0:T(8,128)S(1)} %collective-permute-done.7.z_in, f32[72,128]{1,0:T(8,128)S(1)} %get-tuple-element.31.x_ref, ...), custom_call_target="tpu_custom_call" | custom-call | tf_op jit(solution)/shard_map/pallas_call | solution.py:378
  (3 shorter events, 0.0 us)
Async XLA Ops:
  1.9 23.2 %collective-permute-start = (f32[104,128]{1,0:T(8,128)S(1)}, f32[104,128]{1,0:T(8,128)S(1)}, u32[]{:S(2)}, u32[]{:S(2)}) collective-permute-start(f32[104,128]{1,0:T(8,128)S(1)} %get-tuple-element.24), channel_id=1, source_target_pairs={{8,16},{16,8},{24,32},{32,24},{40,48},{48,40},{56,64},{64,56},{72,... | collective-permute-start | bytes 159752 | tf_op jit(solution)/shard_map/ppermute | solution.py:394
  5.7 21.2 %collective-permute-start.1 = (f32[104,128]{1,0:T(8,128)S(1)}, f32[104,128]{1,0:T(8,128)S(1)}, u32[]{:S(2)}, u32[]{:S(2)}) collective-permute-start(f32[104,128]{1,0:T(8,128)S(1)} %get-tuple-element.25), channel_id=1, source_target_pairs={{0,8},{8,0},{16,24},{24,16},{32,40},{40,32},{48,56},{56,48},{64,72... | collective-permute-start | bytes 159752 | tf_op jit(solution)/shard_map/ppermute | solution.py:394
  27.0 6.8 %collective-permute-start.2 = (f32[352,128]{1,0:T(8,128)S(1)}, f32[352,128]{1,0:T(8,128)S(1)}, u32[]{:S(2)}, u32[]{:S(2)}) collective-permute-start(f32[352,128]{1,0:T(8,128)S(1)} %get-tuple-element.28), channel_id=1, source_target_pairs={{1,2},{2,1},{3,4},{4,3},{5,6},{6,5},{9,10},{10,9},{11,12},{12,11},... | collective-permute-start | bytes 540680 | tf_op jit(solution)/shard_map/ppermute | solution.py:394
  29.0 4.9 %collective-permute-start.3 = (f32[352,128]{1,0:T(8,128)S(1)}, f32[352,128]{1,0:T(8,128)S(1)}, u32[]{:S(2)}, u32[]{:S(2)}) collective-permute-start(f32[352,128]{1,0:T(8,128)S(1)} %get-tuple-element.29), channel_id=1, source_target_pairs={{0,1},{1,0},{2,3},{3,2},{4,5},{5,4},{6,7},{7,6},{8,9},{9,8},{10,11... | collective-permute-start | bytes 540680 | tf_op jit(solution)/shard_map/ppermute | solution.py:394
  37.3 9.8 %collective-permute-start.4 = (f32[64,128]{1,0:T(8,128)S(1)}, f32[64,128]{1,0:T(8,128)S(1)}, u32[]{:S(2)}, u32[]{:S(2)}) collective-permute-start(f32[64,128]{1,0:T(8,128)S(1)} %get-tuple-element.30), channel_id=1, source_target_pairs={{8,32},{32,8},{24,48},{48,24},{40,64},{64,40},{56,80},{80,56},{72,... | collective-permute-start | bytes 98312 | tf_op jit(solution)/shard_map/ppermute | solution.py:394
  39.2 11.2 %collective-permute-start.5 = (f32[64,128]{1,0:T(8,128)S(1)}, f32[64,128]{1,0:T(8,128)S(1)}, u32[]{:S(2)}, u32[]{:S(2)}) collective-permute-start(f32[64,128]{1,0:T(8,128)S(1)} %get-tuple-element.30), channel_id=1, source_target_pairs={{0,24},{24,0},{16,40},{40,16},{32,56},{56,32},{48,72},{72,48},{64,... | collective-permute-start | bytes 98312 | tf_op jit(solution)/shard_map/ppermute | solution.py:394
  50.4 6.5 %collective-permute-start.7 = (f32[200,128]{1,0:T(8,128)S(1)}, f32[200,128]{1,0:T(8,128)S(1)}, u32[]{:S(2)}, u32[]{:S(2)}) collective-permute-start(f32[200,128]{1,0:T(8,128)S(1)} %constant_dynamic-update-slice_fusion.y_ref), channel_id=1, source_target_pairs={{8,16},{16,8},{24,32},{32,24},{40,48},{48,40},{56,64},{64,56},{72,... | collective-permute-start | bytes 307208 | tf_op jit(solution)/shard_map/ppermute | solution.py:394
  54.2 6.6 %collective-permute-start.6 = (f32[200,128]{1,0:T(8,128)S(1)}, f32[200,128]{1,0:T(8,128)S(1)}, u32[]{:S(2)}, u32[]{:S(2)}) collective-permute-start(f32[200,128]{1,0:T(8,128)S(1)} %constant_dynamic-update-slice_fusion.y_ref), channel_id=1, source_target_pairs={{0,8},{8,0},{16,24},{24,16},{32,40},{40,32},{48,56},{56,48},{64,72... | collective-permute-start | bytes 307208 | tf_op jit(solution)/shard_map/ppermute | solution.py:394

commit v8 on v7

--- a/solution.py
+++ b/solution.py
@@ -149,7 +149,7 @@
 
 def levels_kernel(
     u_ref, v_ref, p_ref, plane_ref, col_z, col_a, z_in, a_in,
-    far_ref, x_ref, su_ref, sv_ref, east_ref, west_ref,
+    far_ref, x_ref, su_ref, sv_ref, east_ref, west_ref, hu_ref, hv_ref, hp_ref,
 ):
     levels = u_ref.shape[0] // COLS
     thick = thickness(levels)
@@ -173,6 +173,9 @@
         ref[pl.ds(rows, levels), :] = receive(corners, 2 * i, levels)
         ref[pl.ds(rows + levels, levels), :] = receive(corners, 2 * i + 1, levels)
         ref[pl.ds(rows + 2 * levels, COLS), :] = receive(corners + levels, 0)
+    for f, ref in enumerate((hu_ref, hv_ref, hp_ref)):
+        for k in range(levels):
+            ref[level(k), :] = receive((f * groups + k // SLOTS) * COLS, k % SLOTS)
     U, V, W = (0, rows), (levels, rows + levels), (2 * levels, rows + 2 * levels)
     col = col_index()
     top_col, bottom_col = col == COLS - 1, col == 0
@@ -199,8 +202,8 @@
     for k in range(levels):
         dz = float(thick[k])
         u, v, p = [
-            (ref[level(k), :], receive((f * groups + k // SLOTS) * COLS, k % SLOTS))
-            for f, ref in enumerate((u_ref, v_ref, p_ref))
+            (own[level(k), :], rim[level(k), :])
+            for own, rim in ((u_ref, hu_ref), (v_ref, hv_ref), (p_ref, hp_ref))
         ]
         push_east = east([0.05 * u[t] - p[t] for t in range(2)], U, k)
         around_u = list(zip(west(u, U, k), north(*u), south(*u)))
@@ -419,7 +422,7 @@
     rows_a = swap(rows_a, "lat", 0, 1, False)
     both = (2 * edge[0], LANES)
     far, x, star_u, star_v = call(
-        levels_kernel, [(FAR_ROWS, LANES), (NEAR_ROWS, LANES), flat, flat], [both, both],
+        levels_kernel, [(FAR_ROWS, LANES), (NEAR_ROWS, LANES), flat, flat], [both, both, flat, flat, flat],
         u, v, p, planes, col_z, col_a, rows_z, rows_a,
     )
     far_z = swap(far, "lon", 1, 3, True)

time: 66 us -> 63.7 us (0.965)
  Pallas kernels: 9.95 us -> 7.65 us
    pallas_call x5, Pallas kernels: 9.95 us -> 7.65 us  [call(): pl.pallas_call(kernel, out_shape=[jax.ShapeDtypeStruct(s, jnp.float32) fo...]
where the time goes in v8:
time: 63.7 us; the launch traced here: 63.3 us
  starting transfers between devices  42.3 us (66%)
  waiting for transfers between devices  12.7 us (20%)
  Pallas kernels  7.65 us (12%)
  between operations  0.76 us (1%)
    ppermute x8, starting transfers between devices, swap(): return lax.ppermute(x, axis, pairs)  42.3 us
    ppermute x8, waiting for transfers between devices, swap(): return lax.ppermute(x, axis, pairs)  12.7 us
    pallas_call x5, Pallas kernels, call(): pl.pallas_call(kernel, out_shape=[jax.ShapeDtypeStruct(s, jnp.float32) fo...  7.65 us
  transfers between devices with their start and end apart: 8, of which 5 were waited for; matrix products, arithmetic and copies ran while one was open for 0% of the time, Pallas kernels for 0%

profile of v8, /device:TPU:56, one launch (start us, length us, event | category | flops | bytes accessed | tf_op | source)
XLA Modules:
  0.0 63.3 jit_solution(6300628778946742346)
XLA Ops:
  0.6 1.3 %shard_map.103 = (f32[104,128]{1,0:T(8,128)S(1)}, f32[104,128]{1,0:T(8,128)S(1)}, f32[384,128]{1,0:T(8,128)S(1)}, f32[384,128]{1,0:T(8,128)S(1)}, f32[384,128]{1,0:T(8,128)S(1)}, /*index=5*/f32[32,128]{1,0:T(8,128)S(1)}) custom-call(f32[384,128]{1,0:T(8,128)} %bitcast.5, f32[384,128]{1,0:T(8,128)} %bitcast.6, f32[384,128]{1,0:T(8,128)} %bitcast.7, ...), custom_call_target="tpu_custom_call" | custom-call | tf_op jit(solution)/shard_map/pallas_call | solution.py:381
  1.9 3.8 %collective-permute-start = (f32[104,128]{1,0:T(8,128)S(1)}, f32[104,128]{1,0:T(8,128)S(1)}, u32[]{:S(2)}, u32[]{:S(2)}) collective-permute-start(f32[104,128]{1,0:T(8,128)S(1)} %get-tuple-element.24), channel_id=1, source_target_pairs={{8,16},{16,8},{24,32},{32,24},{40,48},{48,40},{56,64},{64,56},{72,... | collective-permute-start | bytes 159752 | tf_op jit(solution)/shard_map/ppermute | solution.py:397
  5.7 19.1 %collective-permute-start.1 = (f32[104,128]{1,0:T(8,128)S(1)}, f32[104,128]{1,0:T(8,128)S(1)}, u32[]{:S(2)}, u32[]{:S(2)}) collective-permute-start(f32[104,128]{1,0:T(8,128)S(1)} %get-tuple-element.25), channel_id=1, source_target_pairs={{0,8},{8,0},{16,24},{24,16},{32,40},{40,32},{48,56},{56,48},{64,72... | collective-permute-start | bytes 159752 | tf_op jit(solution)/shard_map/ppermute | solution.py:397
  24.8 0.3 shard_map.104
  25.1 0.0 collective-permute-done.col_z
  25.1 1.8 %collective-permute-done.1.col_a = f32[104,128]{1,0:T(8,128)S(1)} collective-permute-done((f32[104,128]{1,0:T(8,128)S(1)}, f32[104,128]{1,0:T(8,128)S(1)}, u32[]{:S(2)}, u32[]{:S(2)}) %collective-permute-start.1) | collective-permute-done | bytes 53280 | tf_op jit(solution)/shard_map/ppermute | solution.py:397
  26.9 0.1 shard_map.105
  27.0 1.9 %collective-permute-start.2 = (f32[352,128]{1,0:T(8,128)S(1)}, f32[352,128]{1,0:T(8,128)S(1)}, u32[]{:S(2)}, u32[]{:S(2)}) collective-permute-start(f32[352,128]{1,0:T(8,128)S(1)} %get-tuple-element.28), channel_id=1, source_target_pairs={{1,2},{2,1},{3,4},{4,3},{5,6},{6,5},{9,10},{10,9},{11,12},{12,11},... | collective-permute-start | bytes 540680 | tf_op jit(solution)/shard_map/ppermute | solution.py:397
  29.0 1.9 %collective-permute-start.3 = (f32[352,128]{1,0:T(8,128)S(1)}, f32[352,128]{1,0:T(8,128)S(1)}, u32[]{:S(2)}, u32[]{:S(2)}) collective-permute-start(f32[352,128]{1,0:T(8,128)S(1)} %get-tuple-element.29), channel_id=1, source_target_pairs={{0,1},{1,0},{2,3},{3,2},{4,5},{5,4},{6,7},{7,6},{8,9},{9,8},{10,11... | collective-permute-start | bytes 540680 | tf_op jit(solution)/shard_map/ppermute | solution.py:397
  30.9 3.0 %collective-permute-done.2.z_in = f32[352,128]{1,0:T(8,128)S(1)} collective-permute-done((f32[352,128]{1,0:T(8,128)S(1)}, f32[352,128]{1,0:T(8,128)S(1)}, u32[]{:S(2)}, u32[]{:S(2)}) %collective-permute-start.2) | collective-permute-done | bytes 180256 | tf_op jit(solution)/shard_map/ppermute | solution.py:397
  33.9 0.0 collective-permute-done.3.a_in
  33.9 1.1 %shard_map.106 = (f32[64,128]{1,0:T(8,128)S(1)}, f32[72,128]{1,0:T(8,128)S(1)}, f32[384,128]{1,0:T(8,128)S(1)}, f32[384,128]{1,0:T(8,128)S(1)}) custom-call(f32[384,128]{1,0:T(8,128)S(1)} %get-tuple-element.20.u_ref, f32[384,128]{1,0:T(8,128)S(1)} %get-tuple-element.21.v_ref, f32[384,128]{1,0:T(8,128)S(1)} %get-tuple-element.22.p_ref, ...), custom_call_target="tpu_custom_call" | custom-call | tf_op jit(solution)/shard_map/pallas_call | solution.py:381
  35.0 1.9 %collective-permute-start.4 = (f32[64,128]{1,0:T(8,128)S(1)}, f32[64,128]{1,0:T(8,128)S(1)}, u32[]{:S(2)}, u32[]{:S(2)}) collective-permute-start(f32[64,128]{1,0:T(8,128)S(1)} %get-tuple-element.30), channel_id=1, source_target_pairs={{8,32},{32,8},{24,48},{48,24},{40,64},{64,40},{56,80},{80,56},{72,... | collective-permute-start | bytes 98312 | tf_op jit(solution)/shard_map/ppermute | solution.py:397
  36.9 7.9 %collective-permute-start.5 = (f32[64,128]{1,0:T(8,128)S(1)}, f32[64,128]{1,0:T(8,128)S(1)}, u32[]{:S(2)}, u32[]{:S(2)}) collective-permute-start(f32[64,128]{1,0:T(8,128)S(1)} %get-tuple-element.30), channel_id=1, source_target_pairs={{0,24},{24,0},{16,40},{40,16},{32,56},{56,32},{48,72},{72,48},{64,... | collective-permute-start | bytes 98312 | tf_op jit(solution)/shard_map/ppermute | solution.py:397
  44.8 0.0 collective-permute-done.4
  44.8 3.3 %collective-permute-done.5 = f32[64,128]{1,0:T(8,128)S(1)} collective-permute-done((f32[64,128]{1,0:T(8,128)S(1)}, f32[64,128]{1,0:T(8,128)S(1)}, u32[]{:S(2)}, u32[]{:S(2)}) %collective-permute-start.5) | collective-permute-done | bytes 32800 | tf_op jit(solution)/shard_map/ppermute | solution.py:397
  48.1 3.8 %collective-permute-start.7 = (f32[200,128]{1,0:T(8,128)S(1)}, f32[200,128]{1,0:T(8,128)S(1)}, u32[]{:S(2)}, u32[]{:S(2)}) collective-permute-start(f32[200,128]{1,0:T(8,128)S(1)} %constant_dynamic-update-slice_fusion.y_ref), channel_id=1, source_target_pairs={{8,16},{16,8},{24,32},{32,24},{40,48},{48,40},{56,64},{64,56},{72,... | collective-permute-start | bytes 307208 | tf_op jit(solution)/shard_map/ppermute | solution.py:397
  51.9 1.9 %collective-permute-start.6 = (f32[200,128]{1,0:T(8,128)S(1)}, f32[200,128]{1,0:T(8,128)S(1)}, u32[]{:S(2)}, u32[]{:S(2)}) collective-permute-start(f32[200,128]{1,0:T(8,128)S(1)} %constant_dynamic-update-slice_fusion.y_ref), channel_id=1, source_target_pairs={{0,8},{8,0},{16,24},{24,16},{32,40},{40,32},{48,56},{56,48},{64,72... | collective-permute-start | bytes 307208 | tf_op jit(solution)/shard_map/ppermute | solution.py:397
  53.9 0.8 %collective-permute-done.7.z_in = f32[200,128]{1,0:T(8,128)S(1)} collective-permute-done((f32[200,128]{1,0:T(8,128)S(1)}, f32[200,128]{1,0:T(8,128)S(1)}, u32[]{:S(2)}, u32[]{:S(2)}) %collective-permute-start.7) | collective-permute-done | bytes 102432 | tf_op jit(solution)/shard_map/ppermute | solution.py:397
  54.7 3.8 %collective-permute-done.6.a_in = f32[200,128]{1,0:T(8,128)S(1)} collective-permute-done((f32[200,128]{1,0:T(8,128)S(1)}, f32[200,128]{1,0:T(8,128)S(1)}, u32[]{:S(2)}, u32[]{:S(2)}) %collective-permute-start.6) | collective-permute-done | bytes 102432 | tf_op jit(solution)/shard_map/ppermute | solution.py:397
  58.5 4.9 %shard_map.107 = (f32[384,128]{1,0:T(8,128)}, f32[384,128]{1,0:T(8,128)}, f32[8,128]{1,0:T(8,128)}) custom-call(f32[200,128]{1,0:T(8,128)S(1)} %constant_dynamic-update-slice_fusion.y_ref, f32[200,128]{1,0:T(8,128)S(1)} %collective-permute-done.6.a_in, f32[200,128]{1,0:T(8,128)S(1)} %collective-permute-done.7.z_in, f32[72,128]{1,0:T(8,128)S(1)} %get-tuple-element.31.x_ref, ...), custom_call_target="tpu_custom_call" | custom-call | tf_op jit(solution)/shard_map/pallas_call | solution.py:381
  (3 shorter events, 0.0 us)
Async XLA Ops:
  1.9 23.2 %collective-permute-start = (f32[104,128]{1,0:T(8,128)S(1)}, f32[104,128]{1,0:T(8,128)S(1)}, u32[]{:S(2)}, u32[]{:S(2)}) collective-permute-start(f32[104,128]{1,0:T(8,128)S(1)} %get-tuple-element.24), channel_id=1, source_target_pairs={{8,16},{16,8},{24,32},{32,24},{40,48},{48,40},{56,64},{64,56},{72,... | collective-permute-start | bytes 159752 | tf_op jit(solution)/shard_map/ppermute | solution.py:397
  5.7 21.2 %collective-permute-start.1 = (f32[104,128]{1,0:T(8,128)S(1)}, f32[104,128]{1,0:T(8,128)S(1)}, u32[]{:S(2)}, u32[]{:S(2)}) collective-permute-start(f32[104,128]{1,0:T(8,128)S(1)} %get-tuple-element.25), channel_id=1, source_target_pairs={{0,8},{8,0},{16,24},{24,16},{32,40},{40,32},{48,56},{56,48},{64,72... | collective-permute-start | bytes 159752 | tf_op jit(solution)/shard_map/ppermute | solution.py:397
  27.0 6.8 %collective-permute-start.2 = (f32[352,128]{1,0:T(8,128)S(1)}, f32[352,128]{1,0:T(8,128)S(1)}, u32[]{:S(2)}, u32[]{:S(2)}) collective-permute-start(f32[352,128]{1,0:T(8,128)S(1)} %get-tuple-element.28), channel_id=1, source_target_pairs={{1,2},{2,1},{3,4},{4,3},{5,6},{6,5},{9,10},{10,9},{11,12},{12,11},... | collective-permute-start | bytes 540680 | tf_op jit(solution)/shard_map/ppermute | solution.py:397
  29.0 4.9 %collective-permute-start.3 = (f32[352,128]{1,0:T(8,128)S(1)}, f32[352,128]{1,0:T(8,128)S(1)}, u32[]{:S(2)}, u32[]{:S(2)}) collective-permute-start(f32[352,128]{1,0:T(8,128)S(1)} %get-tuple-element.29), channel_id=1, source_target_pairs={{0,1},{1,0},{2,3},{3,2},{4,5},{5,4},{6,7},{7,6},{8,9},{9,8},{10,11... | collective-permute-start | bytes 540680 | tf_op jit(solution)/shard_map/ppermute | solution.py:397
  35.0 9.8 %collective-permute-start.4 = (f32[64,128]{1,0:T(8,128)S(1)}, f32[64,128]{1,0:T(8,128)S(1)}, u32[]{:S(2)}, u32[]{:S(2)}) collective-permute-start(f32[64,128]{1,0:T(8,128)S(1)} %get-tuple-element.30), channel_id=1, source_target_pairs={{8,32},{32,8},{24,48},{48,24},{40,64},{64,40},{56,80},{80,56},{72,... | collective-permute-start | bytes 98312 | tf_op jit(solution)/shard_map/ppermute | solution.py:397
  36.9 11.2 %collective-permute-start.5 = (f32[64,128]{1,0:T(8,128)S(1)}, f32[64,128]{1,0:T(8,128)S(1)}, u32[]{:S(2)}, u32[]{:S(2)}) collective-permute-start(f32[64,128]{1,0:T(8,128)S(1)} %get-tuple-element.30), channel_id=1, source_target_pairs={{0,24},{24,0},{16,40},{40,16},{32,56},{56,32},{48,72},{72,48},{64,... | collective-permute-start | bytes 98312 | tf_op jit(solution)/shard_map/ppermute | solution.py:397
  48.1 6.5 %collective-permute-start.7 = (f32[200,128]{1,0:T(8,128)S(1)}, f32[200,128]{1,0:T(8,128)S(1)}, u32[]{:S(2)}, u32[]{:S(2)}) collective-permute-start(f32[200,128]{1,0:T(8,128)S(1)} %constant_dynamic-update-slice_fusion.y_ref), channel_id=1, source_target_pairs={{8,16},{16,8},{24,32},{32,24},{40,48},{48,40},{56,64},{64,56},{72,... | collective-permute-start | bytes 307208 | tf_op jit(solution)/shard_map/ppermute | solution.py:397
  51.9 6.6 %collective-permute-start.6 = (f32[200,128]{1,0:T(8,128)S(1)}, f32[200,128]{1,0:T(8,128)S(1)}, u32[]{:S(2)}, u32[]{:S(2)}) collective-permute-start(f32[200,128]{1,0:T(8,128)S(1)} %constant_dynamic-update-slice_fusion.y_ref), channel_id=1, source_target_pairs={{0,8},{8,0},{16,24},{24,16},{32,40},{40,32},{48,56},{56,48},{64,72... | collective-permute-start | bytes 307208 | tf_op jit(solution)/shard_map/ppermute | solution.py:397

commit v9 on v8

--- a/solution.py
+++ b/solution.py
@@ -57,12 +57,15 @@
     return jnp.where((lane >= RIM) & (lane < LANES - RIM), pltpu.roll(second, LANES // 2, 1), first)
 
 
-def strips(parts, shifts):
+def strips(parts):
     slot = lax.broadcasted_iota(jnp.int32, parts[0].shape, 1) // RIM
-    moved = [pltpu.roll(p, s, 1) if s else p for p, s in zip(parts, shifts)]
-    return jnp.where(
-        slot < 2, jnp.where(slot == 0, moved[0], moved[1]), jnp.where(slot == 2, moved[2], moved[3])
-    )
+    moved = [pltpu.roll(p, RIM * s, 1) if s else p for s, p in enumerate(parts)]
+
+    def choose(order):
+        first, second, third, fourth = [moved[s] for s in order]
+        return jnp.where(slot < 2, jnp.where(slot == 0, first, second), jnp.where(slot == 2, third, fourth))
+
+    return choose((1, 2, 3, 0)), choose((0, 1, 2, 3))
 
 
 def pack_edges_kernel(
@@ -119,7 +122,7 @@
     groups = u_ref.shape[0] // COLS // SLOTS
 
     def send(at, parts):
-        upper, lower = strips(parts, (32, 64, 96, 0)), strips(parts, (0, 32, 64, 96))
+        upper, lower = strips(parts)
         a_ref[level(at), :] = jnp.where(even, upper, lower)
         z_ref[level(at), :] = jnp.where(even, lower, upper)
 
@@ -139,7 +142,7 @@
     z_ref[pl.ds(0, done), :] = rows_z[...]
 
     def send(at, parts):
-        upper, lower = strips(parts, (32, 64, 96, 0)), strips(parts, (0, 32, 64, 96))
+        upper, lower = strips(parts)
         a_ref[pl.ds(at, parts[0].shape[0]), :] = jnp.where(even_row, upper, lower)
         z_ref[pl.ds(at, parts[0].shape[0]), :] = jnp.where(even_row, lower, upper)
 
@@ -154,14 +157,19 @@
     levels = u_ref.shape[0] // COLS
     thick = thickness(levels)
     groups = levels // SLOTS
-    even_col, even_row = is_even("lon"), is_even("lat")
+    even_col = is_even("lon")
+    even_number = 1 - lax.rem(lax.axis_index("lat"), 2)
+
+    def from_a(s, rows):
+        slot = lax.broadcasted_iota(jnp.int32, (rows, LANES), 1) // RIM
+        return jnp.where(slot == s, even_number, 1 - even_number) == 1
+
+    masks = [from_a(s, COLS) for s in range(SLOTS)]
 
     def receive(at, s, rows=COLS):
-        a, z = a_in[pl.ds(at, rows), :], z_in[pl.ds(at, rows), :]
-        n, o = jnp.where(even_row, a, z), jnp.where(even_row, z, a)
-        n = pltpu.roll(n, LANES - RIM * s, 1) if s else n
-        o = pltpu.roll(o, LANES - RIM - RIM * s, 1) if s < SLOTS - 1 else o
-        return jnp.where(lax.broadcasted_iota(jnp.int32, (rows, LANES), 1) < LANES // 2, n, o)
+        mask = masks[s] if rows == COLS else from_a(s, rows)
+        both = jnp.where(mask, a_in[pl.ds(at, rows), :], z_in[pl.ds(at, rows), :])
+        return pltpu.roll(both, LANES - RIM * s, 1) if s else both
 
     a, z = col_a[...], col_z[...]
     rows = a.shape[0]
@@ -362,7 +370,7 @@
     done = 0
     for ring in range(REACH):
         until = SUBSTEPS - COLS * (REACH - 1 - ring)
-        carry = lax.fori_loop(0, until - done, substep(ring, blocks - ring), carry, unroll=2)
+        carry = lax.fori_loop(0, until - done, substep(ring, blocks - ring), carry, unroll=until - done)
         done = until
     out_eta[...] = eta_ref[0, at(REACH), :]
     water = [w_ref[t, at(REACH), :] for t in range(2)]

time: 63.7 us -> 63.1 us (level)
  Pallas kernels: 7.65 us -> 6.94 us
    pallas_call x5, Pallas kernels: 7.65 us -> 6.94 us  [call(): pl.pallas_call(kernel, out_shape=[jax.ShapeDtypeStruct(s, jnp.float32) fo...]
where the time goes in v9:
time: 63.1 us; the launch traced here: 62.7 us
  starting transfers between devices  42.3 us (67%)
  waiting for transfers between devices  12.8 us (20%)
  Pallas kernels  6.94 us (11%)
  between operations  0.75 us (1%)
    ppermute x8, starting transfers between devices, swap(): return lax.ppermute(x, axis, pairs)  42.3 us
    ppermute x8, waiting for transfers between devices, swap(): return lax.ppermute(x, axis, pairs)  12.8 us
    pallas_call x5, Pallas kernels, call(): pl.pallas_call(kernel, out_shape=[jax.ShapeDtypeStruct(s, jnp.float32) fo...  6.94 us
  transfers between devices with their start and end apart: 8, of which 5 were waited for; matrix products, arithmetic and copies ran while one was open for 0% of the time, Pallas kernels for 0%

profile of v9, /device:TPU:56, one launch (start us, length us, event | category | flops | bytes accessed | tf_op | source)
XLA Modules:
  0.0 62.7 jit_solution(7037319533500849595)
XLA Ops:
  0.6 1.3 %shard_map.103 = (f32[104,128]{1,0:T(8,128)S(1)}, f32[104,128]{1,0:T(8,128)S(1)}, f32[384,128]{1,0:T(8,128)S(1)}, f32[384,128]{1,0:T(8,128)S(1)}, f32[384,128]{1,0:T(8,128)S(1)}, /*index=5*/f32[32,128]{1,0:T(8,128)S(1)}) custom-call(f32[384,128]{1,0:T(8,128)} %bitcast.5, f32[384,128]{1,0:T(8,128)} %bitcast.6, f32[384,128]{1,0:T(8,128)} %bitcast.7, ...), custom_call_target="tpu_custom_call" | custom-call | tf_op jit(solution)/shard_map/pallas_call | solution.py:389
  1.9 3.8 %collective-permute-start = (f32[104,128]{1,0:T(8,128)S(1)}, f32[104,128]{1,0:T(8,128)S(1)}, u32[]{:S(2)}, u32[]{:S(2)}) collective-permute-start(f32[104,128]{1,0:T(8,128)S(1)} %get-tuple-element.24), channel_id=1, source_target_pairs={{8,16},{16,8},{24,32},{32,24},{40,48},{48,40},{56,64},{64,56},{72,... | collective-permute-start | bytes 159752 | tf_op jit(solution)/shard_map/ppermute | solution.py:405
  5.7 19.1 %collective-permute-start.1 = (f32[104,128]{1,0:T(8,128)S(1)}, f32[104,128]{1,0:T(8,128)S(1)}, u32[]{:S(2)}, u32[]{:S(2)}) collective-permute-start(f32[104,128]{1,0:T(8,128)S(1)} %get-tuple-element.25), channel_id=1, source_target_pairs={{0,8},{8,0},{16,24},{24,16},{32,40},{40,32},{48,56},{56,48},{64,72... | collective-permute-start | bytes 159752 | tf_op jit(solution)/shard_map/ppermute | solution.py:405
  24.8 0.2 shard_map.104
  25.0 0.0 collective-permute-done.col_z
  25.0 1.9 %collective-permute-done.1.col_a = f32[104,128]{1,0:T(8,128)S(1)} collective-permute-done((f32[104,128]{1,0:T(8,128)S(1)}, f32[104,128]{1,0:T(8,128)S(1)}, u32[]{:S(2)}, u32[]{:S(2)}) %collective-permute-start.1) | collective-permute-done | bytes 53280 | tf_op jit(solution)/shard_map/ppermute | solution.py:405
  26.9 0.1 shard_map.105
  27.0 1.9 %collective-permute-start.2 = (f32[352,128]{1,0:T(8,128)S(1)}, f32[352,128]{1,0:T(8,128)S(1)}, u32[]{:S(2)}, u32[]{:S(2)}) collective-permute-start(f32[352,128]{1,0:T(8,128)S(1)} %get-tuple-element.28), channel_id=1, source_target_pairs={{1,2},{2,1},{3,4},{4,3},{5,6},{6,5},{9,10},{10,9},{11,12},{12,11},... | collective-permute-start | bytes 540680 | tf_op jit(solution)/shard_map/ppermute | solution.py:405
  29.0 1.9 %collective-permute-start.3 = (f32[352,128]{1,0:T(8,128)S(1)}, f32[352,128]{1,0:T(8,128)S(1)}, u32[]{:S(2)}, u32[]{:S(2)}) collective-permute-start(f32[352,128]{1,0:T(8,128)S(1)} %get-tuple-element.29), channel_id=1, source_target_pairs={{0,1},{1,0},{2,3},{3,2},{4,5},{5,4},{6,7},{7,6},{8,9},{9,8},{10,11... | collective-permute-start | bytes 540680 | tf_op jit(solution)/shard_map/ppermute | solution.py:405
  30.9 3.0 %collective-permute-done.2.z_in = f32[352,128]{1,0:T(8,128)S(1)} collective-permute-done((f32[352,128]{1,0:T(8,128)S(1)}, f32[352,128]{1,0:T(8,128)S(1)}, u32[]{:S(2)}, u32[]{:S(2)}) %collective-permute-start.2) | collective-permute-done | bytes 180256 | tf_op jit(solution)/shard_map/ppermute | solution.py:405
  33.8 0.0 collective-permute-done.3.a_in
  33.8 0.9 %shard_map.106 = (f32[64,128]{1,0:T(8,128)S(1)}, f32[72,128]{1,0:T(8,128)S(1)}, f32[384,128]{1,0:T(8,128)S(1)}, f32[384,128]{1,0:T(8,128)S(1)}) custom-call(f32[384,128]{1,0:T(8,128)S(1)} %get-tuple-element.20.u_ref, f32[384,128]{1,0:T(8,128)S(1)} %get-tuple-element.21.v_ref, f32[384,128]{1,0:T(8,128)S(1)} %get-tuple-element.22.p_ref, ...), custom_call_target="tpu_custom_call" | custom-call | tf_op jit(solution)/shard_map/pallas_call | solution.py:389
  34.7 1.9 %collective-permute-start.4 = (f32[64,128]{1,0:T(8,128)S(1)}, f32[64,128]{1,0:T(8,128)S(1)}, u32[]{:S(2)}, u32[]{:S(2)}) collective-permute-start(f32[64,128]{1,0:T(8,128)S(1)} %get-tuple-element.30), channel_id=1, source_target_pairs={{8,32},{32,8},{24,48},{48,24},{40,64},{64,40},{56,80},{80,56},{72,... | collective-permute-start | bytes 98312 | tf_op jit(solution)/shard_map/ppermute | solution.py:405
  36.7 7.9 %collective-permute-start.5 = (f32[64,128]{1,0:T(8,128)S(1)}, f32[64,128]{1,0:T(8,128)S(1)}, u32[]{:S(2)}, u32[]{:S(2)}) collective-permute-start(f32[64,128]{1,0:T(8,128)S(1)} %get-tuple-element.30), channel_id=1, source_target_pairs={{0,24},{24,0},{16,40},{40,16},{32,56},{56,32},{48,72},{72,48},{64,... | collective-permute-start | bytes 98312 | tf_op jit(solution)/shard_map/ppermute | solution.py:405
  44.6 0.0 collective-permute-done.4
  44.6 3.3 %collective-permute-done.5 = f32[64,128]{1,0:T(8,128)S(1)} collective-permute-done((f32[64,128]{1,0:T(8,128)S(1)}, f32[64,128]{1,0:T(8,128)S(1)}, u32[]{:S(2)}, u32[]{:S(2)}) %collective-permute-start.5) | collective-permute-done | bytes 32800 | tf_op jit(solution)/shard_map/ppermute | solution.py:405
  47.9 3.8 %collective-permute-start.7 = (f32[200,128]{1,0:T(8,128)S(1)}, f32[200,128]{1,0:T(8,128)S(1)}, u32[]{:S(2)}, u32[]{:S(2)}) collective-permute-start(f32[200,128]{1,0:T(8,128)S(1)} %constant_dynamic-update-slice_fusion.y_ref), channel_id=1, source_target_pairs={{8,16},{16,8},{24,32},{32,24},{40,48},{48,40},{56,64},{64,56},{72,... | collective-permute-start | bytes 307208 | tf_op jit(solution)/shard_map/ppermute | solution.py:405
  51.7 1.9 %collective-permute-start.6 = (f32[200,128]{1,0:T(8,128)S(1)}, f32[200,128]{1,0:T(8,128)S(1)}, u32[]{:S(2)}, u32[]{:S(2)}) collective-permute-start(f32[200,128]{1,0:T(8,128)S(1)} %constant_dynamic-update-slice_fusion.y_ref), channel_id=1, source_target_pairs={{0,8},{8,0},{16,24},{24,16},{32,40},{40,32},{48,56},{56,48},{64,72... | collective-permute-start | bytes 307208 | tf_op jit(solution)/shard_map/ppermute | solution.py:405
  53.6 0.8 %collective-permute-done.7.z_in = f32[200,128]{1,0:T(8,128)S(1)} collective-permute-done((f32[200,128]{1,0:T(8,128)S(1)}, f32[200,128]{1,0:T(8,128)S(1)}, u32[]{:S(2)}, u32[]{:S(2)}) %collective-permute-start.7) | collective-permute-done | bytes 102432 | tf_op jit(solution)/shard_map/ppermute | solution.py:405
  54.4 3.8 %collective-permute-done.6.a_in = f32[200,128]{1,0:T(8,128)S(1)} collective-permute-done((f32[200,128]{1,0:T(8,128)S(1)}, f32[200,128]{1,0:T(8,128)S(1)}, u32[]{:S(2)}, u32[]{:S(2)}) %collective-permute-start.6) | collective-permute-done | bytes 102432 | tf_op jit(solution)/shard_map/ppermute | solution.py:405
  58.2 4.5 %shard_map.107 = (f32[384,128]{1,0:T(8,128)}, f32[384,128]{1,0:T(8,128)}, f32[8,128]{1,0:T(8,128)}) custom-call(f32[200,128]{1,0:T(8,128)S(1)} %constant_dynamic-update-slice_fusion.y_ref, f32[200,128]{1,0:T(8,128)S(1)} %collective-permute-done.6.a_in, f32[200,128]{1,0:T(8,128)S(1)} %collective-permute-done.7.z_in, f32[72,128]{1,0:T(8,128)S(1)} %get-tuple-element.31.x_ref, ...), custom_call_target="tpu_custom_call" | custom-call | tf_op jit(solution)/shard_map/pallas_call | solution.py:389
  (3 shorter events, 0.0 us)
Async XLA Ops:
  1.9 23.1 %collective-permute-start = (f32[104,128]{1,0:T(8,128)S(1)}, f32[104,128]{1,0:T(8,128)S(1)}, u32[]{:S(2)}, u32[]{:S(2)}) collective-permute-start(f32[104,128]{1,0:T(8,128)S(1)} %get-tuple-element.24), channel_id=1, source_target_pairs={{8,16},{16,8},{24,32},{32,24},{40,48},{48,40},{56,64},{64,56},{72,... | collective-permute-start | bytes 159752 | tf_op jit(solution)/shard_map/ppermute | solution.py:405
  5.7 21.2 %collective-permute-start.1 = (f32[104,128]{1,0:T(8,128)S(1)}, f32[104,128]{1,0:T(8,128)S(1)}, u32[]{:S(2)}, u32[]{:S(2)}) collective-permute-start(f32[104,128]{1,0:T(8,128)S(1)} %get-tuple-element.25), channel_id=1, source_target_pairs={{0,8},{8,0},{16,24},{24,16},{32,40},{40,32},{48,56},{56,48},{64,72... | collective-permute-start | bytes 159752 | tf_op jit(solution)/shard_map/ppermute | solution.py:405
  27.0 6.8 %collective-permute-start.2 = (f32[352,128]{1,0:T(8,128)S(1)}, f32[352,128]{1,0:T(8,128)S(1)}, u32[]{:S(2)}, u32[]{:S(2)}) collective-permute-start(f32[352,128]{1,0:T(8,128)S(1)} %get-tuple-element.28), channel_id=1, source_target_pairs={{1,2},{2,1},{3,4},{4,3},{5,6},{6,5},{9,10},{10,9},{11,12},{12,11},... | collective-permute-start | bytes 540680 | tf_op jit(solution)/shard_map/ppermute | solution.py:405
  29.0 4.9 %collective-permute-start.3 = (f32[352,128]{1,0:T(8,128)S(1)}, f32[352,128]{1,0:T(8,128)S(1)}, u32[]{:S(2)}, u32[]{:S(2)}) collective-permute-start(f32[352,128]{1,0:T(8,128)S(1)} %get-tuple-element.29), channel_id=1, source_target_pairs={{0,1},{1,0},{2,3},{3,2},{4,5},{5,4},{6,7},{7,6},{8,9},{9,8},{10,11... | collective-permute-start | bytes 540680 | tf_op jit(solution)/shard_map/ppermute | solution.py:405
  34.7 9.8 %collective-permute-start.4 = (f32[64,128]{1,0:T(8,128)S(1)}, f32[64,128]{1,0:T(8,128)S(1)}, u32[]{:S(2)}, u32[]{:S(2)}) collective-permute-start(f32[64,128]{1,0:T(8,128)S(1)} %get-tuple-element.30), channel_id=1, source_target_pairs={{8,32},{32,8},{24,48},{48,24},{40,64},{64,40},{56,80},{80,56},{72,... | collective-permute-start | bytes 98312 | tf_op jit(solution)/shard_map/ppermute | solution.py:405
  36.7 11.2 %collective-permute-start.5 = (f32[64,128]{1,0:T(8,128)S(1)}, f32[64,128]{1,0:T(8,128)S(1)}, u32[]{:S(2)}, u32[]{:S(2)}) collective-permute-start(f32[64,128]{1,0:T(8,128)S(1)} %get-tuple-element.30), channel_id=1, source_target_pairs={{0,24},{24,0},{16,40},{40,16},{32,56},{56,32},{48,72},{72,48},{64,... | collective-permute-start | bytes 98312 | tf_op jit(solution)/shard_map/ppermute | solution.py:405
  47.9 6.5 %collective-permute-start.7 = (f32[200,128]{1,0:T(8,128)S(1)}, f32[200,128]{1,0:T(8,128)S(1)}, u32[]{:S(2)}, u32[]{:S(2)}) collective-permute-start(f32[200,128]{1,0:T(8,128)S(1)} %constant_dynamic-update-slice_fusion.y_ref), channel_id=1, source_target_pairs={{8,16},{16,8},{24,32},{32,24},{40,48},{48,40},{56,64},{64,56},{72,... | collective-permute-start | bytes 307208 | tf_op jit(solution)/shard_map/ppermute | solution.py:405
  51.7 6.6 %collective-permute-start.6 = (f32[200,128]{1,0:T(8,128)S(1)}, f32[200,128]{1,0:T(8,128)S(1)}, u32[]{:S(2)}, u32[]{:S(2)}) collective-permute-start(f32[200,128]{1,0:T(8,128)S(1)} %constant_dynamic-update-slice_fusion.y_ref), channel_id=1, source_target_pairs={{0,8},{8,0},{16,24},{24,16},{32,40},{40,32},{48,56},{56,48},{64,72... | collective-permute-start | bytes 307208 | tf_op jit(solution)/shard_map/ppermute | solution.py:405

commit v10 on v9

--- a/solution.py
+++ b/solution.py
@@ -14,6 +14,7 @@
 REACH = 4
 NEAR_ROWS = 9 * COLS
 FAR_ROWS = 8 * COLS
+PAIRS = 1
 TRIOS = (((2, 0, 21), (3, 43, 22), (0, 86, 21)), ((1, 0, 21), (4, 42, 21), (5, 84, 21)))
 STEP = 6.0
 VMEM_BYTES = 32 * 1024 * 1024
@@ -55,6 +56,15 @@
 def pair_rims(first, second):
     lane = lax.broadcasted_iota(jnp.int32, first.shape, 1)
     return jnp.where((lane >= RIM) & (lane < LANES - RIM), pltpu.roll(second, LANES // 2, 1), first)
+
+
+def shifted(own, rim, rows):
+    if rows == 0:
+        return own, rim
+    lane = lane_index()
+    wraps = lane >= LANES - rows if rows > 0 else lane < -rows
+    a, b = pltpu.roll(own, -rows % LANES, 1), pltpu.roll(rim, -rows % LANES, 1)
+    return jnp.where(wraps, b, a), jnp.where(wraps, a, b)
 
 
 def strips(parts):
@@ -79,14 +89,14 @@
         pltpu.make_async_copy(src, dst, sems.at[i])
         for i, (src, dst) in enumerate(
             (
-                (u_in, u_ref), (v_in, v_ref), (b_in, b_ref), (land_in, land_ref), (bottom_in, bottom_ref),
+                (b_in, b_ref), (land_in, land_ref), (bottom_in, bottom_ref), (u_in, u_ref), (v_in, v_ref),
                 (eta_in, plane_ref.at[level(1)]), (wx_in, plane_ref.at[level(2)]), (wy_in, plane_ref.at[level(3)]),
             )
         )
     ]
     for copy in copies:
         copy.start()
-    for copy in copies:
+    for copy in copies[:3]:
         copy.wait()
     water = (land_ref[...] * bottom_ref[...]).astype(jnp.float32)
     plane_ref[level(0), :] = water
@@ -94,6 +104,8 @@
     for k in range(levels):
         p = p + float(thick[k]) * b_ref[level(k), :]
         p_ref[level(k), :] = p
+    for copy in copies[3:]:
+        copy.wait()
 
     def edge(ref, col):
         return ref[pl.ds(col, levels, stride=COLS), :]
@@ -254,7 +266,7 @@
 def substeps_kernel(
     y_ref, a_in, z_in, x_ref, su_ref, sv_ref, out_u, out_v, out_eta,
     eta_ref, u_ref, v_ref, w_ref, fu_ref, fv_ref, du_ref, dv_ref, cu_ref, cv_ref, tw_ref, q_ref, t_ref,
-    eta_north_ref, u_north_ref, tw_north_ref,
+    eta_north_ref, u_north_ref, tw_north_ref, more_ref,
 ):
     levels = su_ref.shape[0] // COLS
     tau = STEP / SUBSTEPS
@@ -325,9 +337,29 @@
     flow_u, flow_v = u_ref[0, at(REACH), :], v_ref[0, at(REACH), :]
     zero = jnp.zeros((COLS, LANES), jnp.float32)
 
+    def finish(first, last, carry, u_from, v_from):
+        total_u, total_v = carry
+        for p in range(first, last):
+            eta = [eta_ref[t, at(p), :] for t in range(2)]
+            eta_north = [eta_north_ref[t, at(p), :] for t in range(2)]
+            for t in range(2):
+                vbar = q_ref[t, at(p), :] + q_ref[t, at(p, 1), :]
+                rise_u = eta_ref[t, at(p, 1), :] - eta[t]
+                rise_v = eta_north[t] - eta[t]
+                next_u = (u_from[t, at(p), :] + fu_ref[t, at(p), :]) + (
+                    cu_ref[t, at(p), :] * vbar - du_ref[t, at(p), :] * rise_u
+                )
+                next_v = (v_from[t, at(p), :] + fv_ref[t, at(p), :]) - (
+                    cv_ref[t, at(p), :] * t_ref[t, at(p), :] + dv_ref[t, at(p), :] * rise_v
+                )
+                u_ref[t, at(p), :] = next_u
+                v_ref[t, at(p), :] = next_v
+                if p == REACH and t == 0:
+                    total_u, total_v = total_u + next_u, total_v + next_v
+        return total_u, total_v
+
     def substep(first, last):
         def body(_, carry):
-            total_u, total_v = carry
             for p in range(first, last):
                 u = [u_ref[t, at(p), :] for t in range(2)]
                 u_west = [u_ref[t, at(p, -1), :] for t in range(2)]
@@ -345,32 +377,95 @@
                     )
                     q_ref[t, at(p), :] = v[t] + v_south[t]
                     t_ref[t, at(p), :] = (u[t] + u_west[t]) + (u_north[t] + u_north_west)
-            for p in range(first, last):
-                eta = [eta_ref[t, at(p), :] for t in range(2)]
-                eta_north = [eta_north_ref[t, at(p), :] for t in range(2)]
-                for t in range(2):
-                    vbar = q_ref[t, at(p), :] + q_ref[t, at(p, 1), :]
-                    rise_u = eta_ref[t, at(p, 1), :] - eta[t]
-                    rise_v = eta_north[t] - eta[t]
-                    next_u = (u_ref[t, at(p), :] + fu_ref[t, at(p), :]) + (
-                        cu_ref[t, at(p), :] * vbar - du_ref[t, at(p), :] * rise_u
+            return finish(first, last, carry, u_ref, v_ref)
+
+        return body
+
+    names = ("u-1", "u2", "v-1", "v1", "e-1", "e0", "e1", "e2", "q1", "t-1", "t1", "U0", "U1", "V-1", "V0", "V1") + (
+        "fu1", "cu1", "du1", "fv-1", "fv1", "cv-1", "cv1", "dv-1", "dv1", "tw-1", "tw2"
+    )
+    kept = {"u0": u_ref, "u1": u_north_ref, "v0": v_ref, "q0": q_ref, "t0": t_ref, "tw0": tw_ref, "tw1": tw_north_ref}
+    kept |= {"fu0": fu_ref, "cu0": cu_ref, "du0": du_ref, "fv0": fv_ref, "cv0": cv_ref, "dv0": dv_ref}
+    kept |= {name: more_ref.at[i] for i, name in enumerate(names)}
+
+    def get(name, rows, p, t, shift=0):
+        return kept[f"{name}{rows}"][t, at(p, shift), :]
+
+    def put(name, rows, p, t, value):
+        kept[f"{name}{rows}"][t, at(p), :] = value
+
+    for p in range(PAIRS, blocks - PAIRS):
+        for name, where in (
+            ("fu", (1,)), ("cu", (1,)), ("du", (1,)), ("fv", (-1, 1)), ("cv", (-1, 1)), ("dv", (-1, 1)), ("tw", (-1, 2))
+        ):
+            here = [get(name, 0, p, t) for t in range(2)]
+            for rows in where:
+                for t, value in enumerate(shifted(*here, rows)):
+                    put(name, rows, p, t, value)
+
+    def pair_of_steps(first, last, carry):
+        total_u, total_v = carry
+        tiles = range(first, last)
+        for p in tiles:
+            u, v, eta = [[ref[t, at(p), :] for t in range(2)] for ref in (u_ref, v_ref, eta_ref)]
+            us = {r: shifted(*u, r) for r in (0, -1, 1, 2)}
+            vs = {r: shifted(*v, r) for r in (0, -1, -2, 1, 2)}
+            es = {r: shifted(*eta, r) for r in (0, -1, 1, 2)}
+            for t in range(2):
+                for r in (-1, 1, 2):
+                    put("u", r, p, t, us[r][t])
+                for r in (-1, 1):
+                    put("v", r, p, t, vs[r][t])
+                both = {}
+                for r in (-1, 0, 1, 2):
+                    u_west = get("u", r, p, t, -1)
+                    both[r] = us[r][t] + u_west
+                    spread = (us[r][t] - u_west) + (vs[r][t] - vs[r - 1][t])
+                    put("e", r, p, t, es[r][t] - get("tw", r, p, t) * spread)
+                for r in (0, 1):
+                    put("q", r, p, t, vs[r][t] + vs[r - 1][t])
+                for r in (-1, 0, 1):
+                    put("t", r, p, t, both[r] + both[r + 1])
+        for p in tiles:
+            for t in range(2):
+                e = {r: get("e", r, p, t) for r in (-1, 0, 1, 2)}
+                for r in (0, 1):
+                    vbar = get("q", r, p, t) + get("q", r, p, t, 1)
+                    rise = get("e", r, p, t, 1) - e[r]
+                    next_u = (get("u", r, p, t) + get("fu", r, p, t)) + (
+                        get("cu", r, p, t) * vbar - get("du", r, p, t) * rise
                     )
-                    next_v = (v_ref[t, at(p), :] + fv_ref[t, at(p), :]) - (
-                        cv_ref[t, at(p), :] * t_ref[t, at(p), :] + dv_ref[t, at(p), :] * rise_v
+                    put("U", r, p, t, next_u)
+                    if p == REACH and t == 0 and r == 0:
+                        total_u = total_u + next_u
+                for r in (-1, 0, 1):
+                    next_v = (get("v", r, p, t) + get("fv", r, p, t)) - (
+                        get("cv", r, p, t) * get("t", r, p, t) + get("dv", r, p, t) * (e[r + 1] - e[r])
                     )
-                    u_ref[t, at(p), :] = next_u
-                    v_ref[t, at(p), :] = next_v
-                    if p == REACH and t == 0:
-                        total_u, total_v = total_u + next_u, total_v + next_v
-            return total_u, total_v
-
-        return body
+                    put("V", r, p, t, next_v)
+                    if p == REACH and t == 0 and r == 0:
+                        total_v = total_v + next_v
+        for p in tiles:
+            for t in range(2):
+                both = []
+                for r, ref in ((0, eta_ref), (1, eta_north_ref)):
+                    u, u_west = get("U", r, p, t), get("U", r, p, t, -1)
+                    both.append(u + u_west)
+                    spread = (u - u_west) + (get("V", r, p, t) - get("V", r - 1, p, t))
+                    ref[t, at(p), :] = get("e", r, p, t) - get("tw", r, p, t) * spread
+                q_ref[t, at(p), :] = get("V", 0, p, t) + get("V", -1, p, t)
+                t_ref[t, at(p), :] = both[0] + both[1]
+        return finish(first, last, (total_u, total_v), kept["U0"], kept["V0"])
 
     carry = (zero, zero)
     done = 0
     for ring in range(REACH):
         until = SUBSTEPS - COLS * (REACH - 1 - ring)
-        carry = lax.fori_loop(0, until - done, substep(ring, blocks - ring), carry, unroll=until - done)
+        if ring < PAIRS:
+            carry = lax.fori_loop(0, until - done, substep(ring, blocks - ring), carry, unroll=until - done)
+        else:
+            for _ in range((until - done) // 2):
+                carry = pair_of_steps(ring, blocks - ring, carry)
         done = until
     out_eta[...] = eta_ref[0, at(REACH), :]
     water = [w_ref[t, at(REACH), :] for t in range(2)]
@@ -440,7 +535,7 @@
     near_a = swap(y, "lon", 0, 1, True)
     state = (2, (2 * REACH + 3) * COLS, LANES)
     new_u, new_v, surface = call(
-        substeps_kernel, [flat, flat, (COLS, LANES)], [state] * 16, y, near_a, near_z, x, star_u, star_v
+        substeps_kernel, [flat, flat, (COLS, LANES)], [state] * 16 + [(27, *state)], y, near_a, near_z, x, star_u, star_v
     )
     return new_u.reshape(velocity_u.shape), new_v.reshape(velocity_v.shape), surface
 

time: 63.1 us -> 63 us (level)
  no operation moved by 1% of the time
where the time goes in v10:
time: 63 us; the launch traced here: 62.6 us
  starting transfers between devices  42.3 us (67%)
  waiting for transfers between devices  12.8 us (20%)
  Pallas kernels  6.81 us (11%)
  between operations  0.75 us (1%)
    ppermute x8, starting transfers between devices, swap(): return lax.ppermute(x, axis, pairs)  42.3 us
    ppermute x8, waiting for transfers between devices, swap(): return lax.ppermute(x, axis, pairs)  12.8 us
    pallas_call x5, Pallas kernels, call(): pl.pallas_call(kernel, out_shape=[jax.ShapeDtypeStruct(s, jnp.float32) fo...  6.81 us
  transfers between devices with their start and end apart: 8, of which 5 were waited for; matrix products, arithmetic and copies ran while one was open for 0% of the time, Pallas kernels for 0%

profile of v10, /device:TPU:56, one launch (start us, length us, event | category | flops | bytes accessed | tf_op | source)
XLA Modules:
  0.0 62.6 jit_solution(14492803890037770886)
XLA Ops:
  0.6 1.2 %shard_map.103 = (f32[104,128]{1,0:T(8,128)S(1)}, f32[104,128]{1,0:T(8,128)S(1)}, f32[384,128]{1,0:T(8,128)S(1)}, f32[384,128]{1,0:T(8,128)S(1)}, f32[384,128]{1,0:T(8,128)S(1)}, /*index=5*/f32[32,128]{1,0:T(8,128)S(1)}) custom-call(f32[384,128]{1,0:T(8,128)} %bitcast.5, f32[384,128]{1,0:T(8,128)} %bitcast.6, f32[384,128]{1,0:T(8,128)} %bitcast.7, ...), custom_call_target="tpu_custom_call" | custom-call | tf_op jit(solution)/shard_map/pallas_call | solution.py:484
  1.9 3.8 %collective-permute-start = (f32[104,128]{1,0:T(8,128)S(1)}, f32[104,128]{1,0:T(8,128)S(1)}, u32[]{:S(2)}, u32[]{:S(2)}) collective-permute-start(f32[104,128]{1,0:T(8,128)S(1)} %get-tuple-element.24), channel_id=1, source_target_pairs={{8,16},{16,8},{24,32},{32,24},{40,48},{48,40},{56,64},{64,56},{72,... | collective-permute-start | bytes 159752 | tf_op jit(solution)/shard_map/ppermute | solution.py:500
  5.7 19.1 %collective-permute-start.1 = (f32[104,128]{1,0:T(8,128)S(1)}, f32[104,128]{1,0:T(8,128)S(1)}, u32[]{:S(2)}, u32[]{:S(2)}) collective-permute-start(f32[104,128]{1,0:T(8,128)S(1)} %get-tuple-element.25), channel_id=1, source_target_pairs={{0,8},{8,0},{16,24},{24,16},{32,40},{40,32},{48,56},{56,48},{64,72... | collective-permute-start | bytes 159752 | tf_op jit(solution)/shard_map/ppermute | solution.py:500
  24.8 0.2 shard_map.104
  25.0 0.0 collective-permute-done.col_z
  25.0 1.9 %collective-permute-done.1.col_a = f32[104,128]{1,0:T(8,128)S(1)} collective-permute-done((f32[104,128]{1,0:T(8,128)S(1)}, f32[104,128]{1,0:T(8,128)S(1)}, u32[]{:S(2)}, u32[]{:S(2)}) %collective-permute-start.1) | collective-permute-done | bytes 53280 | tf_op jit(solution)/shard_map/ppermute | solution.py:500
  26.9 0.1 shard_map.105
  27.0 1.9 %collective-permute-start.2 = (f32[352,128]{1,0:T(8,128)S(1)}, f32[352,128]{1,0:T(8,128)S(1)}, u32[]{:S(2)}, u32[]{:S(2)}) collective-permute-start(f32[352,128]{1,0:T(8,128)S(1)} %get-tuple-element.28), channel_id=1, source_target_pairs={{1,2},{2,1},{3,4},{4,3},{5,6},{6,5},{9,10},{10,9},{11,12},{12,11},... | collective-permute-start | bytes 540680 | tf_op jit(solution)/shard_map/ppermute | solution.py:500
  28.9 1.9 %collective-permute-start.3 = (f32[352,128]{1,0:T(8,128)S(1)}, f32[352,128]{1,0:T(8,128)S(1)}, u32[]{:S(2)}, u32[]{:S(2)}) collective-permute-start(f32[352,128]{1,0:T(8,128)S(1)} %get-tuple-element.29), channel_id=1, source_target_pairs={{0,1},{1,0},{2,3},{3,2},{4,5},{5,4},{6,7},{7,6},{8,9},{9,8},{10,11... | collective-permute-start | bytes 540680 | tf_op jit(solution)/shard_map/ppermute | solution.py:500
  30.9 3.0 %collective-permute-done.2.z_in = f32[352,128]{1,0:T(8,128)S(1)} collective-permute-done((f32[352,128]{1,0:T(8,128)S(1)}, f32[352,128]{1,0:T(8,128)S(1)}, u32[]{:S(2)}, u32[]{:S(2)}) %collective-permute-start.2) | collective-permute-done | bytes 180256 | tf_op jit(solution)/shard_map/ppermute | solution.py:500
  33.8 0.0 collective-permute-done.3.a_in
  33.8 0.9 %shard_map.106 = (f32[64,128]{1,0:T(8,128)S(1)}, f32[72,128]{1,0:T(8,128)S(1)}, f32[384,128]{1,0:T(8,128)S(1)}, f32[384,128]{1,0:T(8,128)S(1)}) custom-call(f32[384,128]{1,0:T(8,128)S(1)} %get-tuple-element.20.u_ref, f32[384,128]{1,0:T(8,128)S(1)} %get-tuple-element.21.v_ref, f32[384,128]{1,0:T(8,128)S(1)} %get-tuple-element.22.p_ref, ...), custom_call_target="tpu_custom_call" | custom-call | tf_op jit(solution)/shard_map/pallas_call | solution.py:484
  34.7 1.9 %collective-permute-start.4 = (f32[64,128]{1,0:T(8,128)S(1)}, f32[64,128]{1,0:T(8,128)S(1)}, u32[]{:S(2)}, u32[]{:S(2)}) collective-permute-start(f32[64,128]{1,0:T(8,128)S(1)} %get-tuple-element.30), channel_id=1, source_target_pairs={{8,32},{32,8},{24,48},{48,24},{40,64},{64,40},{56,80},{80,56},{72,... | collective-permute-start | bytes 98312 | tf_op jit(solution)/shard_map/ppermute | solution.py:500
  36.6 7.9 %collective-permute-start.5 = (f32[64,128]{1,0:T(8,128)S(1)}, f32[64,128]{1,0:T(8,128)S(1)}, u32[]{:S(2)}, u32[]{:S(2)}) collective-permute-start(f32[64,128]{1,0:T(8,128)S(1)} %get-tuple-element.30), channel_id=1, source_target_pairs={{0,24},{24,0},{16,40},{40,16},{32,56},{56,32},{48,72},{72,48},{64,... | collective-permute-start | bytes 98312 | tf_op jit(solution)/shard_map/ppermute | solution.py:500
  44.6 0.0 collective-permute-done.4
  44.6 3.3 %collective-permute-done.5 = f32[64,128]{1,0:T(8,128)S(1)} collective-permute-done((f32[64,128]{1,0:T(8,128)S(1)}, f32[64,128]{1,0:T(8,128)S(1)}, u32[]{:S(2)}, u32[]{:S(2)}) %collective-permute-start.5) | collective-permute-done | bytes 32800 | tf_op jit(solution)/shard_map/ppermute | solution.py:500
  47.9 3.8 %collective-permute-start.7 = (f32[200,128]{1,0:T(8,128)S(1)}, f32[200,128]{1,0:T(8,128)S(1)}, u32[]{:S(2)}, u32[]{:S(2)}) collective-permute-start(f32[200,128]{1,0:T(8,128)S(1)} %constant_dynamic-update-slice_fusion.y_ref), channel_id=1, source_target_pairs={{8,16},{16,8},{24,32},{32,24},{40,48},{48,40},{56,64},{64,56},{72,... | collective-permute-start | bytes 307208 | tf_op jit(solution)/shard_map/ppermute | solution.py:500
  51.7 1.9 %collective-permute-start.6 = (f32[200,128]{1,0:T(8,128)S(1)}, f32[200,128]{1,0:T(8,128)S(1)}, u32[]{:S(2)}, u32[]{:S(2)}) collective-permute-start(f32[200,128]{1,0:T(8,128)S(1)} %constant_dynamic-update-slice_fusion.y_ref), channel_id=1, source_target_pairs={{0,8},{8,0},{16,24},{24,16},{32,40},{40,32},{48,56},{56,48},{64,72... | collective-permute-start | bytes 307208 | tf_op jit(solution)/shard_map/ppermute | solution.py:500
  53.6 0.8 %collective-permute-done.7.z_in = f32[200,128]{1,0:T(8,128)S(1)} collective-permute-done((f32[200,128]{1,0:T(8,128)S(1)}, f32[200,128]{1,0:T(8,128)S(1)}, u32[]{:S(2)}, u32[]{:S(2)}) %collective-permute-start.7) | collective-permute-done | bytes 102432 | tf_op jit(solution)/shard_map/ppermute | solution.py:500
  54.4 3.8 %collective-permute-done.6.a_in = f32[200,128]{1,0:T(8,128)S(1)} collective-permute-done((f32[200,128]{1,0:T(8,128)S(1)}, f32[200,128]{1,0:T(8,128)S(1)}, u32[]{:S(2)}, u32[]{:S(2)}) %collective-permute-start.6) | collective-permute-done | bytes 102432 | tf_op jit(solution)/shard_map/ppermute | solution.py:500
  58.2 4.4 %shard_map.107 = (f32[384,128]{1,0:T(8,128)}, f32[384,128]{1,0:T(8,128)}, f32[8,128]{1,0:T(8,128)}) custom-call(f32[200,128]{1,0:T(8,128)S(1)} %constant_dynamic-update-slice_fusion.y_ref, f32[200,128]{1,0:T(8,128)S(1)} %collective-permute-done.6.a_in, f32[200,128]{1,0:T(8,128)S(1)} %collective-permute-done.7.z_in, f32[72,128]{1,0:T(8,128)S(1)} %get-tuple-element.31.x_ref, ...), custom_call_target="tpu_custom_call" | custom-call | tf_op jit(solution)/shard_map/pallas_call | solution.py:484
  (3 shorter events, 0.0 us)
Async XLA Ops:
  1.9 23.1 %collective-permute-start = (f32[104,128]{1,0:T(8,128)S(1)}, f32[104,128]{1,0:T(8,128)S(1)}, u32[]{:S(2)}, u32[]{:S(2)}) collective-permute-start(f32[104,128]{1,0:T(8,128)S(1)} %get-tuple-element.24), channel_id=1, source_target_pairs={{8,16},{16,8},{24,32},{32,24},{40,48},{48,40},{56,64},{64,56},{72,... | collective-permute-start | bytes 159752 | tf_op jit(solution)/shard_map/ppermute | solution.py:500
  5.7 21.2 %collective-permute-start.1 = (f32[104,128]{1,0:T(8,128)S(1)}, f32[104,128]{1,0:T(8,128)S(1)}, u32[]{:S(2)}, u32[]{:S(2)}) collective-permute-start(f32[104,128]{1,0:T(8,128)S(1)} %get-tuple-element.25), channel_id=1, source_target_pairs={{0,8},{8,0},{16,24},{24,16},{32,40},{40,32},{48,56},{56,48},{64,72... | collective-permute-start | bytes 159752 | tf_op jit(solution)/shard_map/ppermute | solution.py:500
  27.0 6.8 %collective-permute-start.2 = (f32[352,128]{1,0:T(8,128)S(1)}, f32[352,128]{1,0:T(8,128)S(1)}, u32[]{:S(2)}, u32[]{:S(2)}) collective-permute-start(f32[352,128]{1,0:T(8,128)S(1)} %get-tuple-element.28), channel_id=1, source_target_pairs={{1,2},{2,1},{3,4},{4,3},{5,6},{6,5},{9,10},{10,9},{11,12},{12,11},... | collective-permute-start | bytes 540680 | tf_op jit(solution)/shard_map/ppermute | solution.py:500
  28.9 4.9 %collective-permute-start.3 = (f32[352,128]{1,0:T(8,128)S(1)}, f32[352,128]{1,0:T(8,128)S(1)}, u32[]{:S(2)}, u32[]{:S(2)}) collective-permute-start(f32[352,128]{1,0:T(8,128)S(1)} %get-tuple-element.29), channel_id=1, source_target_pairs={{0,1},{1,0},{2,3},{3,2},{4,5},{5,4},{6,7},{7,6},{8,9},{9,8},{10,11... | collective-permute-start | bytes 540680 | tf_op jit(solution)/shard_map/ppermute | solution.py:500
  34.7 9.9 %collective-permute-start.4 = (f32[64,128]{1,0:T(8,128)S(1)}, f32[64,128]{1,0:T(8,128)S(1)}, u32[]{:S(2)}, u32[]{:S(2)}) collective-permute-start(f32[64,128]{1,0:T(8,128)S(1)} %get-tuple-element.30), channel_id=1, source_target_pairs={{8,32},{32,8},{24,48},{48,24},{40,64},{64,40},{56,80},{80,56},{72,... | collective-permute-start | bytes 98312 | tf_op jit(solution)/shard_map/ppermute | solution.py:500
  36.6 11.2 %collective-permute-start.5 = (f32[64,128]{1,0:T(8,128)S(1)}, f32[64,128]{1,0:T(8,128)S(1)}, u32[]{:S(2)}, u32[]{:S(2)}) collective-permute-start(f32[64,128]{1,0:T(8,128)S(1)} %get-tuple-element.30), channel_id=1, source_target_pairs={{0,24},{24,0},{16,40},{40,16},{32,56},{56,32},{48,72},{72,48},{64,... | collective-permute-start | bytes 98312 | tf_op jit(solution)/shard_map/ppermute | solution.py:500
  47.9 6.5 %collective-permute-start.7 = (f32[200,128]{1,0:T(8,128)S(1)}, f32[200,128]{1,0:T(8,128)S(1)}, u32[]{:S(2)}, u32[]{:S(2)}) collective-permute-start(f32[200,128]{1,0:T(8,128)S(1)} %constant_dynamic-update-slice_fusion.y_ref), channel_id=1, source_target_pairs={{8,16},{16,8},{24,32},{32,24},{40,48},{48,40},{56,64},{64,56},{72,... | collective-permute-start | bytes 307208 | tf_op jit(solution)/shard_map/ppermute | solution.py:500
  51.7 6.6 %collective-permute-start.6 = (f32[200,128]{1,0:T(8,128)S(1)}, f32[200,128]{1,0:T(8,128)S(1)}, u32[]{:S(2)}, u32[]{:S(2)}) collective-permute-start(f32[200,128]{1,0:T(8,128)S(1)} %constant_dynamic-update-slice_fusion.y_ref), channel_id=1, source_target_pairs={{0,8},{8,0},{16,24},{24,16},{32,40},{40,32},{48,56},{56,48},{64,72... | collective-permute-start | bytes 307208 | tf_op jit(solution)/shard_map/ppermute | solution.py:500

commit v11 on v10

--- a/solution.py
+++ b/solution.py
@@ -14,7 +14,7 @@
 REACH = 4
 NEAR_ROWS = 9 * COLS
 FAR_ROWS = 8 * COLS
-PAIRS = 1
+PAIRS = 2
 TRIOS = (((2, 0, 21), (3, 43, 22), (0, 86, 21)), ((1, 0, 21), (4, 42, 21), (5, 84, 21)))
 STEP = 6.0
 VMEM_BYTES = 32 * 1024 * 1024

time: 63 us -> 63 us (level)
  no operation moved by 1% of the time
where the time goes in v11:
time: 63 us; the launch traced here: 62.6 us
  starting transfers between devices  42.3 us (67%)
  waiting for transfers between devices  12.8 us (20%)
  Pallas kernels  6.84 us (11%)
  between operations  0.75 us (1%)
    ppermute x8, starting transfers between devices, swap(): return lax.ppermute(x, axis, pairs)  42.3 us
    ppermute x8, waiting for transfers between devices, swap(): return lax.ppermute(x, axis, pairs)  12.8 us
    pallas_call x5, Pallas kernels, call(): pl.pallas_call(kernel, out_shape=[jax.ShapeDtypeStruct(s, jnp.float32) fo...  6.84 us
  transfers between devices with their start and end apart: 8, of which 5 were waited for; matrix products, arithmetic and copies ran while one was open for 0% of the time, Pallas kernels for 0%

profile of v11, /device:TPU:56, one launch (start us, length us, event | category | flops | bytes accessed | tf_op | source)
XLA Modules:
  0.0 62.6 jit_solution(18382734072782954564)
XLA Ops:
  0.6 1.2 %shard_map.103 = (f32[104,128]{1,0:T(8,128)S(1)}, f32[104,128]{1,0:T(8,128)S(1)}, f32[384,128]{1,0:T(8,128)S(1)}, f32[384,128]{1,0:T(8,128)S(1)}, f32[384,128]{1,0:T(8,128)S(1)}, /*index=5*/f32[32,128]{1,0:T(8,128)S(1)}) custom-call(f32[384,128]{1,0:T(8,128)} %bitcast.5, f32[384,128]{1,0:T(8,128)} %bitcast.6, f32[384,128]{1,0:T(8,128)} %bitcast.7, ...), custom_call_target="tpu_custom_call" | custom-call | tf_op jit(solution)/shard_map/pallas_call | solution.py:484
  1.9 3.8 %collective-permute-start = (f32[104,128]{1,0:T(8,128)S(1)}, f32[104,128]{1,0:T(8,128)S(1)}, u32[]{:S(2)}, u32[]{:S(2)}) collective-permute-start(f32[104,128]{1,0:T(8,128)S(1)} %get-tuple-element.24), channel_id=1, source_target_pairs={{8,16},{16,8},{24,32},{32,24},{40,48},{48,40},{56,64},{64,56},{72,... | collective-permute-start | bytes 159752 | tf_op jit(solution)/shard_map/ppermute | solution.py:500
  5.7 19.1 %collective-permute-start.1 = (f32[104,128]{1,0:T(8,128)S(1)}, f32[104,128]{1,0:T(8,128)S(1)}, u32[]{:S(2)}, u32[]{:S(2)}) collective-permute-start(f32[104,128]{1,0:T(8,128)S(1)} %get-tuple-element.25), channel_id=1, source_target_pairs={{0,8},{8,0},{16,24},{24,16},{32,40},{40,32},{48,56},{56,48},{64,72... | collective-permute-start | bytes 159752 | tf_op jit(solution)/shard_map/ppermute | solution.py:500
  24.8 0.2 shard_map.104
  25.0 0.0 collective-permute-done.col_z
  25.0 1.9 %collective-permute-done.1.col_a = f32[104,128]{1,0:T(8,128)S(1)} collective-permute-done((f32[104,128]{1,0:T(8,128)S(1)}, f32[104,128]{1,0:T(8,128)S(1)}, u32[]{:S(2)}, u32[]{:S(2)}) %collective-permute-start.1) | collective-permute-done | bytes 53280 | tf_op jit(solution)/shard_map/ppermute | solution.py:500
  26.9 0.1 shard_map.105
  27.0 1.9 %collective-permute-start.2 = (f32[352,128]{1,0:T(8,128)S(1)}, f32[352,128]{1,0:T(8,128)S(1)}, u32[]{:S(2)}, u32[]{:S(2)}) collective-permute-start(f32[352,128]{1,0:T(8,128)S(1)} %get-tuple-element.28), channel_id=1, source_target_pairs={{1,2},{2,1},{3,4},{4,3},{5,6},{6,5},{9,10},{10,9},{11,12},{12,11},... | collective-permute-start | bytes 540680 | tf_op jit(solution)/shard_map/ppermute | solution.py:500
  28.9 1.9 %collective-permute-start.3 = (f32[352,128]{1,0:T(8,128)S(1)}, f32[352,128]{1,0:T(8,128)S(1)}, u32[]{:S(2)}, u32[]{:S(2)}) collective-permute-start(f32[352,128]{1,0:T(8,128)S(1)} %get-tuple-element.29), channel_id=1, source_target_pairs={{0,1},{1,0},{2,3},{3,2},{4,5},{5,4},{6,7},{7,6},{8,9},{9,8},{10,11... | collective-permute-start | bytes 540680 | tf_op jit(solution)/shard_map/ppermute | solution.py:500
  30.9 3.0 %collective-permute-done.2.z_in = f32[352,128]{1,0:T(8,128)S(1)} collective-permute-done((f32[352,128]{1,0:T(8,128)S(1)}, f32[352,128]{1,0:T(8,128)S(1)}, u32[]{:S(2)}, u32[]{:S(2)}) %collective-permute-start.2) | collective-permute-done | bytes 180256 | tf_op jit(solution)/shard_map/ppermute | solution.py:500
  33.8 0.0 collective-permute-done.3.a_in
  33.8 0.9 %shard_map.106 = (f32[64,128]{1,0:T(8,128)S(1)}, f32[72,128]{1,0:T(8,128)S(1)}, f32[384,128]{1,0:T(8,128)S(1)}, f32[384,128]{1,0:T(8,128)S(1)}) custom-call(f32[384,128]{1,0:T(8,128)S(1)} %get-tuple-element.20.u_ref, f32[384,128]{1,0:T(8,128)S(1)} %get-tuple-element.21.v_ref, f32[384,128]{1,0:T(8,128)S(1)} %get-tuple-element.22.p_ref, ...), custom_call_target="tpu_custom_call" | custom-call | tf_op jit(solution)/shard_map/pallas_call | solution.py:484
  34.7 1.9 %collective-permute-start.4 = (f32[64,128]{1,0:T(8,128)S(1)}, f32[64,128]{1,0:T(8,128)S(1)}, u32[]{:S(2)}, u32[]{:S(2)}) collective-permute-start(f32[64,128]{1,0:T(8,128)S(1)} %get-tuple-element.30), channel_id=1, source_target_pairs={{8,32},{32,8},{24,48},{48,24},{40,64},{64,40},{56,80},{80,56},{72,... | collective-permute-start | bytes 98312 | tf_op jit(solution)/shard_map/ppermute | solution.py:500
  36.6 7.9 %collective-permute-start.5 = (f32[64,128]{1,0:T(8,128)S(1)}, f32[64,128]{1,0:T(8,128)S(1)}, u32[]{:S(2)}, u32[]{:S(2)}) collective-permute-start(f32[64,128]{1,0:T(8,128)S(1)} %get-tuple-element.30), channel_id=1, source_target_pairs={{0,24},{24,0},{16,40},{40,16},{32,56},{56,32},{48,72},{72,48},{64,... | collective-permute-start | bytes 98312 | tf_op jit(solution)/shard_map/ppermute | solution.py:500
  44.6 0.0 collective-permute-done.4
  44.6 3.3 %collective-permute-done.5 = f32[64,128]{1,0:T(8,128)S(1)} collective-permute-done((f32[64,128]{1,0:T(8,128)S(1)}, f32[64,128]{1,0:T(8,128)S(1)}, u32[]{:S(2)}, u32[]{:S(2)}) %collective-permute-start.5) | collective-permute-done | bytes 32800 | tf_op jit(solution)/shard_map/ppermute | solution.py:500
  47.9 3.8 %collective-permute-start.7 = (f32[200,128]{1,0:T(8,128)S(1)}, f32[200,128]{1,0:T(8,128)S(1)}, u32[]{:S(2)}, u32[]{:S(2)}) collective-permute-start(f32[200,128]{1,0:T(8,128)S(1)} %constant_dynamic-update-slice_fusion.y_ref), channel_id=1, source_target_pairs={{8,16},{16,8},{24,32},{32,24},{40,48},{48,40},{56,64},{64,56},{72,... | collective-permute-start | bytes 307208 | tf_op jit(solution)/shard_map/ppermute | solution.py:500
  51.7 1.9 %collective-permute-start.6 = (f32[200,128]{1,0:T(8,128)S(1)}, f32[200,128]{1,0:T(8,128)S(1)}, u32[]{:S(2)}, u32[]{:S(2)}) collective-permute-start(f32[200,128]{1,0:T(8,128)S(1)} %constant_dynamic-update-slice_fusion.y_ref), channel_id=1, source_target_pairs={{0,8},{8,0},{16,24},{24,16},{32,40},{40,32},{48,56},{56,48},{64,72... | collective-permute-start | bytes 307208 | tf_op jit(solution)/shard_map/ppermute | solution.py:500
  53.6 0.8 %collective-permute-done.7.z_in = f32[200,128]{1,0:T(8,128)S(1)} collective-permute-done((f32[200,128]{1,0:T(8,128)S(1)}, f32[200,128]{1,0:T(8,128)S(1)}, u32[]{:S(2)}, u32[]{:S(2)}) %collective-permute-start.7) | collective-permute-done | bytes 102432 | tf_op jit(solution)/shard_map/ppermute | solution.py:500
  54.4 3.8 %collective-permute-done.6.a_in = f32[200,128]{1,0:T(8,128)S(1)} collective-permute-done((f32[200,128]{1,0:T(8,128)S(1)}, f32[200,128]{1,0:T(8,128)S(1)}, u32[]{:S(2)}, u32[]{:S(2)}) %collective-permute-start.6) | collective-permute-done | bytes 102432 | tf_op jit(solution)/shard_map/ppermute | solution.py:500
  58.2 4.4 %shard_map.107 = (f32[384,128]{1,0:T(8,128)}, f32[384,128]{1,0:T(8,128)}, f32[8,128]{1,0:T(8,128)}) custom-call(f32[200,128]{1,0:T(8,128)S(1)} %constant_dynamic-update-slice_fusion.y_ref, f32[200,128]{1,0:T(8,128)S(1)} %collective-permute-done.6.a_in, f32[200,128]{1,0:T(8,128)S(1)} %collective-permute-done.7.z_in, f32[72,128]{1,0:T(8,128)S(1)} %get-tuple-element.31.x_ref, ...), custom_call_target="tpu_custom_call" | custom-call | tf_op jit(solution)/shard_map/pallas_call | solution.py:484
  (3 shorter events, 0.0 us)
Async XLA Ops:
  1.9 23.1 %collective-permute-start = (f32[104,128]{1,0:T(8,128)S(1)}, f32[104,128]{1,0:T(8,128)S(1)}, u32[]{:S(2)}, u32[]{:S(2)}) collective-permute-start(f32[104,128]{1,0:T(8,128)S(1)} %get-tuple-element.24), channel_id=1, source_target_pairs={{8,16},{16,8},{24,32},{32,24},{40,48},{48,40},{56,64},{64,56},{72,... | collective-permute-start | bytes 159752 | tf_op jit(solution)/shard_map/ppermute | solution.py:500
  5.7 21.2 %collective-permute-start.1 = (f32[104,128]{1,0:T(8,128)S(1)}, f32[104,128]{1,0:T(8,128)S(1)}, u32[]{:S(2)}, u32[]{:S(2)}) collective-permute-start(f32[104,128]{1,0:T(8,128)S(1)} %get-tuple-element.25), channel_id=1, source_target_pairs={{0,8},{8,0},{16,24},{24,16},{32,40},{40,32},{48,56},{56,48},{64,72... | collective-permute-start | bytes 159752 | tf_op jit(solution)/shard_map/ppermute | solution.py:500
  27.0 6.8 %collective-permute-start.2 = (f32[352,128]{1,0:T(8,128)S(1)}, f32[352,128]{1,0:T(8,128)S(1)}, u32[]{:S(2)}, u32[]{:S(2)}) collective-permute-start(f32[352,128]{1,0:T(8,128)S(1)} %get-tuple-element.28), channel_id=1, source_target_pairs={{1,2},{2,1},{3,4},{4,3},{5,6},{6,5},{9,10},{10,9},{11,12},{12,11},... | collective-permute-start | bytes 540680 | tf_op jit(solution)/shard_map/ppermute | solution.py:500
  28.9 4.9 %collective-permute-start.3 = (f32[352,128]{1,0:T(8,128)S(1)}, f32[352,128]{1,0:T(8,128)S(1)}, u32[]{:S(2)}, u32[]{:S(2)}) collective-permute-start(f32[352,128]{1,0:T(8,128)S(1)} %get-tuple-element.29), channel_id=1, source_target_pairs={{0,1},{1,0},{2,3},{3,2},{4,5},{5,4},{6,7},{7,6},{8,9},{9,8},{10,11... | collective-permute-start | bytes 540680 | tf_op jit(solution)/shard_map/ppermute | solution.py:500
  34.7 9.9 %collective-permute-start.4 = (f32[64,128]{1,0:T(8,128)S(1)}, f32[64,128]{1,0:T(8,128)S(1)}, u32[]{:S(2)}, u32[]{:S(2)}) collective-permute-start(f32[64,128]{1,0:T(8,128)S(1)} %get-tuple-element.30), channel_id=1, source_target_pairs={{8,32},{32,8},{24,48},{48,24},{40,64},{64,40},{56,80},{80,56},{72,... | collective-permute-start | bytes 98312 | tf_op jit(solution)/shard_map/ppermute | solution.py:500
  36.6 11.2 %collective-permute-start.5 = (f32[64,128]{1,0:T(8,128)S(1)}, f32[64,128]{1,0:T(8,128)S(1)}, u32[]{:S(2)}, u32[]{:S(2)}) collective-permute-start(f32[64,128]{1,0:T(8,128)S(1)} %get-tuple-element.30), channel_id=1, source_target_pairs={{0,24},{24,0},{16,40},{40,16},{32,56},{56,32},{48,72},{72,48},{64,... | collective-permute-start | bytes 98312 | tf_op jit(solution)/shard_map/ppermute | solution.py:500
  47.9 6.5 %collective-permute-start.7 = (f32[200,128]{1,0:T(8,128)S(1)}, f32[200,128]{1,0:T(8,128)S(1)}, u32[]{:S(2)}, u32[]{:S(2)}) collective-permute-start(f32[200,128]{1,0:T(8,128)S(1)} %constant_dynamic-update-slice_fusion.y_ref), channel_id=1, source_target_pairs={{8,16},{16,8},{24,32},{32,24},{40,48},{48,40},{56,64},{64,56},{72,... | collective-permute-start | bytes 307208 | tf_op jit(solution)/shard_map/ppermute | solution.py:500
  51.7 6.6 %collective-permute-start.6 = (f32[200,128]{1,0:T(8,128)S(1)}, f32[200,128]{1,0:T(8,128)S(1)}, u32[]{:S(2)}, u32[]{:S(2)}) collective-permute-start(f32[200,128]{1,0:T(8,128)S(1)} %constant_dynamic-update-slice_fusion.y_ref), channel_id=1, source_target_pairs={{0,8},{8,0},{16,24},{24,16},{32,40},{40,32},{48,56},{56,48},{64,72... | collective-permute-start | bytes 307208 | tf_op jit(solution)/shard_map/ppermute | solution.py:500
